TPU v7x, 32 devices: a whole 2x2x4 slice. The times are simulated.
32 devices in a mesh: groups: 2 (over y), tensor: 8 (over z, x), store: 2 (over core).
Axes of the slice: x: 2, y: 2, z: 4, core: 2. Of those that a mesh axis runs over, the one named last changes fastest.
Arguments:
- tokens: bfloat16 [2560, 3072], P(('groups', 'store'), 'tensor'), parts along dimension 0, may hold values from -6 to 6
- modulation: bfloat16 [4, 8, 3, 3072], P(('groups', 'store')), parts along dimension 0, may hold values from -3 to 3
- adapter_per_request: int32 [4, 8], P('groups'), parts along dimension 0, may hold values from 0 to 255
- tokens_per_request: int32 [4, 8], P(('groups', 'store')), parts along dimension 0, may hold values from 1 to 160, 640 in all within a row
- first_weight: bfloat16 [3072, 12288], P(None, 'tensor'), may hold values from -0.109375 to 0.109375
- first_bias: bfloat16 [12288], P('tensor'), may hold values from -3 to 3
- second_weight: bfloat16 [12288, 3072], P('tensor'), may hold values from -0.0546875 to 0.0546875
- second_bias: bfloat16 [3072], P('tensor'), may hold values from -3 to 3
- adapter_down_matrices: bfloat16 [256, 3072, 64], P('store', 'tensor'), may hold values from -0.109375 to 0.109375
- adapter_up_matrices: bfloat16 [256, 64, 12288], P('store', None, 'tensor'), may hold values from -0.75 to 0.75
Outputs:
- block_out: bfloat16 [2560, 3072], P(('groups', 'store'), 'tensor'), parts along dimension 0
There are 2 independent parts, one for each index of `groups`. A program takes and returns all parts, laid end to end along the dimension named above; an argument that names none is the same for every part. Nothing has to cross between parts.
Inputs may be any that keep to these rules, and one draw needn't show every extreme that they name: `adapter_per_request`: adapter ids of the store. `tokens_per_request`: each row sums to 640, the largest entry is exactly 160.
All inputs are finite; a program needn't handle non-finite values.
Results may differ from a plain program's by a relative error of at most 0.0043.
Values may be sent and summed in bfloat16 or wider, within the bound.
No kernel may reach another device: no remote copies, remote signals or barrier semaphores. Data moves between devices by JAX's collectives and lax.ppermute only.
A program may use at most 192 MiB of HBM per device.

v0:
```python
import jax
import jax.numpy as jnp
from jax import lax
from jax.sharding import PartitionSpec as P


def partner(block, axis, stride):
    count = lax.axis_size(axis)
    route = []
    for low in range(count):
        high = low | 1 << stride
        if high != low and high < count:
            route += [(low, high), (high, low)]
    return lax.ppermute(block, axis, route)


def request_onehot(lengths, row_count, req_count):
    bounds = jnp.cumsum(lengths)
    places = jnp.arange(row_count, dtype=jnp.int32)
    owner_req = jnp.sum((places[:, None] >= bounds[None, :]).astype(jnp.int32), axis=1)
    return (owner_req[:, None] == jnp.arange(req_count, dtype=jnp.int32)[None, :]).astype(
        jnp.float32
    )


def on_device(
    tokens,
    modulation,
    adapter_per_request,
    tokens_per_request,
    first_weight,
    first_bias,
    second_weight,
    second_bias,
    adapter_down_matrices,
    adapter_up_matrices,
):
    tensor_index = lax.axis_index("tensor")
    store_index = lax.axis_index("store")
    tok_rows, feat_width = tokens.shape
    req_count = tokens_per_request.shape[1]
    rank_column_width = adapter_down_matrices.shape[2]
    hidden_width = first_weight.shape[1]
    store_request_count = adapter_down_matrices.shape[0]
    gathered = lax.all_gather(tokens, "tensor", axis=1, tiled=True).astype(jnp.float32)
    adapter_indicator = request_onehot(tokens_per_request[0], tok_rows, req_count)
    factors = modulation[0].astype(jnp.float32)
    shift_rows = jnp.dot(adapter_indicator, factors[:, 0], precision=lax.Precision.HIGHEST)
    scale_rows = jnp.dot(adapter_indicator, factors[:, 1], precision=lax.Precision.HIGHEST)
    gate_own = lax.dynamic_slice_in_dim(factors[:, 2], tensor_index * feat_width, feat_width, 1)
    gate_rows = jnp.dot(adapter_indicator, gate_own, precision=lax.Precision.HIGHEST)
    center = jnp.mean(gathered, axis=1, keepdims=True)
    spread = jnp.mean((gathered - center) ** 2, axis=1, keepdims=True)
    normed = (gathered - center) * lax.rsqrt(spread + 1e-06)
    modded = ((1.0 + scale_rows) * normed + shift_rows).astype(jnp.bfloat16)

    def pick_owned(wanted):
        owned_mask = wanted // store_request_count == store_index
        request_index_list = jnp.clip(
            wanted - store_index * store_request_count, 0, store_request_count - 1
        )
        down_matrix_rows = jnp.take(adapter_down_matrices, request_index_list, axis=0)
        up_matrix_rows = jnp.take(adapter_up_matrices, request_index_list, axis=0)
        keep = owned_mask[:, None, None]
        return (
            owned_mask,
            jnp.where(keep, down_matrix_rows, jnp.zeros_like(down_matrix_rows)),
            jnp.where(keep, up_matrix_rows, jnp.zeros_like(up_matrix_rows)),
        )

    mine_ids = lax.dynamic_index_in_dim(adapter_per_request, store_index, 0, keepdims=False)
    other_ids = lax.dynamic_index_in_dim(adapter_per_request, 1 - store_index, 0, keepdims=False)
    mine_owned, mine_down, mine_up = pick_owned(mine_ids)
    other_owned, send_down, send_up = pick_owned(other_ids)
    recv_down, recv_up = partner((send_down, send_up), "store", 0)
    down_now = jnp.where(mine_owned[:, None, None], mine_down, recv_down)
    up_now = jnp.where(mine_owned[:, None, None], mine_up, recv_up)
    low_rank_every = jnp.einsum(
        "tn,knr->tkr",
        modded,
        lax.all_gather(down_now, "tensor", axis=1, tiled=True),
        preferred_element_type=jnp.float32,
    )
    low_rank_sum = jnp.sum(adapter_indicator[:, :, None] * low_rank_every, axis=1)
    adapter_low_rank = low_rank_sum.astype(jnp.bfloat16)
    broadcast_low_rank = (
        (adapter_indicator[:, :, None] * adapter_low_rank.astype(jnp.float32)[:, None, :])
        .reshape(tok_rows, req_count * rank_column_width)
        .astype(jnp.bfloat16)
    )
    preact = jnp.dot(modded, first_weight, preferred_element_type=jnp.float32) + first_bias.astype(
        jnp.float32
    )
    preact = preact + jnp.dot(
        broadcast_low_rank,
        up_now.reshape(req_count * rank_column_width, hidden_width),
        preferred_element_type=jnp.float32,
    )
    activated = jax.nn.gelu(preact, approximate=True).astype(jnp.bfloat16)
    own_share = lax.psum_scatter(
        lax.dot_general(
            second_weight, activated, (((0,), (1,)), ((), ())), preferred_element_type=jnp.float32
        ),
        "tensor",
        scatter_dimension=0,
        tiled=True,
    ).T
    block_out = tokens.astype(jnp.float32) + gate_rows * (
        own_share + second_bias.astype(jnp.float32)
    )
    return block_out.astype(jnp.bfloat16)


def solution(mesh):
    in_specs = (
        P(("groups", "store"), "tensor"),
        P(("groups", "store"), None, None, None),
        P("groups", None),
        P(("groups", "store"), None),
        P(None, "tensor"),
        P("tensor"),
        P("tensor", None),
        P("tensor"),
        P("store", "tensor", None),
        P("store", None, "tensor"),
    )
    out_specs = P(("groups", "store"), "tensor")
    return jax.shard_map(
        on_device, mesh=mesh, in_specs=in_specs, out_specs=out_specs, check_vma=False
    )
```

profile of v0, /device:TPU:0, one launch (start us, length us, event | category | flops | bytes accessed | tf_op | source)
XLA Modules:
  0.0 328.0 jit_solution(1868830770173502894)
XLA Ops:
  6.5 0.7 all-gather.3.cloned.1.call-update
  7.3 0.8 compare_and_fusion.1
  8.1 3.4 %gather_fusion.1 = bf16[8,384,64]{1,2,0:T(8,128)(2,1)S(1)} fusion(bf16[128,384,64]{1,2,0:T(8,128)(2,1)} %param.22, s32[1024]{0:T(1024)S(1)} %pad_clamp_fusion), kind=kCustom, calls=%fused_computation.2.clone | custom fusion | bytes 786464 | tf_op jit(solution)/shard_map/jit(_take)/gather | solution.py:62
  11.5 0.1 select_select_fusion.2
  11.7 0.5 collective-permute-start
  12.2 3.4 %gather_fusion = bf16[8,384,64]{1,2,0:T(8,128)(2,1)S(1)} fusion(bf16[128,384,64]{1,2,0:T(8,128)(2,1)} %param.22, s32[1024]{0:T(1024)S(1)} %pad_clamp_fusion.1), kind=kCustom, calls=%fused_computation.clone | custom fusion | bytes 786464 | tf_op jit(solution)/shard_map/jit(_take)/gather | solution.py:62
  15.6 0.9 fusion.24
  16.6 9.3 %gather_fusion.3 = bf16[8,64,1536]{2,1,0:T(8,128)(2,1)S(1)} fusion(bf16[128,64,1536]{2,1,0:T(8,128)(2,1)} %param.23, s32[1024]{0:T(1024)S(1)} %pad_clamp_fusion), kind=kCustom, calls=%fused_computation.3.clone | custom fusion | bytes 3145760 | tf_op jit(solution)/shard_map/jit(_take)/gather | solution.py:63
  26.0 0.2 select_select_fusion
  26.2 0.1 collective-permute-start.1
  26.3 8.9 %gather_fusion.2 = bf16[8,64,1536]{2,1,0:T(8,128)(2,1)S(1)} fusion(bf16[128,64,1536]{2,1,0:T(8,128)(2,1)} %param.23, s32[1024]{0:T(1024)S(1)} %pad_clamp_fusion.1), kind=kCustom, calls=%fused_computation.1.clone | custom fusion | bytes 3145760 | tf_op jit(solution)/shard_map/jit(_take)/gather | solution.py:63
  35.2 0.2 reduce-window.8
  35.5 4.3 %fusion.25 = f32[640,3072]{1,0:T(8,128)} fusion(bf16[8,3,3072]{2,0,1:T(8,128)(2,1)S(1)} %bitcast.49, s32[640]{0:T(1024)S(1)} %convert_reduce_fusion.1), kind=kOutput, calls=%fused_computation.43 | convolution fusion | flops 31462400 | bytes 7917568 | tf_op jit(solution)/shard_map/dot_general | solution.py:49
  39.9 44.3 %all-gather.3.cloned.1.call-done = bf16[640,3072]{1,0:T(8,128)(2,1)} async-done(((bf16[640,384]{1,0:T(8,128)(2,1)}), bf16[640,3072]{1,0:T(8,128)(2,1)}) %all-gather.3.cloned.1.call-update) | async-done | bytes 3932176 | tf_op jit(solution)/shard_map/all_gather | solution.py:45
  84.2 2.8 convert_reduce_fusion
  87.0 3.7 %fusion.2 = f32[640]{0:T(1024)S(1)} fusion(bf16[640,3072]{1,0:T(8,128)(2,1)} %all-gather.3.cloned.1.call-done, f32[640]{0:T(1024)S(1)} %broadcast_multiply_fusion), kind=kLoop, calls=%fused_computation.8 | loop fusion | flops 7863680 | bytes 3937280 | tf_op jit(solution)/shard_map/reduce_sum | solution.py:53
  90.8 6.3 %fusion.5 = bf16[640,3072]{1,0:T(8,128)(2,1)} fusion(bf16[640,3072]{1,0:T(8,128)(2,1)} %all-gather.3.cloned.1.call-done, f32[640,3072]{1,0:T(8,128)S(1)} %copy-done, f32[640]{0:T(1024)S(1)} %add_rsqrt_fusion, f32[640]{0:T(1024)S(1)} %broadcast_multiply_fusion, bf16[8,3,3072]{2,0,1:T(8,128)(2,1)S(1)} %bitcast.50, s32[640]{0:T(1024)S(1)} %convert_reduce_fusion.1), kind=kOutput, calls=%fused_computation.11 | convolution fusion | flops 45224960 | bytes 15790080 | tf_op jit(solution)/shard_map/dot_general | solution.py:48
  97.1 50.4 %all-gather.5.cloned.1.call-done = bf16[8,3072,64]{1,2,0:T(8,128)(2,1)} async-done(((bf16[8,384,64]{1,2,0:T(8,128)(2,1)}), bf16[8,3072,64]{1,2,0:T(8,128)(2,1)}) %all-gather.5.cloned.1.call-update) | async-done | bytes 3145744 | tf_op jit(solution)/shard_map/all_gather | solution.py:81
  147.5 5.9 %fusion.40 = f32[640,512]{0,1:S(1)} fusion(bf16[640,3072]{1,0:T(8,128)(2,1)} %fusion.5, bf16[3072,512]{0,1:T(8,128)(2,1)} %bitcast.53), kind=kOutput, calls=%fused_computation.79 | convolution fusion | flops 2013265920 | bytes 8388608
  153.5 10.4 %fusion.39 = f32[640,1536]{1,0:T(8,128)} fusion(bf16[640,3072]{1,0:T(8,128)(2,1)S(1)} %copy-done.1, bf16[3072,1536]{1,0:T(8,128)(2,1)} %param.18), kind=kOutput, calls=%fused_computation.78 | convolution fusion | flops 6039797760 | bytes 17301504 | tf_op jit(solution)/shard_map/dot_general | solution.py:91
  163.9 16.9 %convolution_bitcast_fusion = f32[3072,640]{0,1:T(8,128)} fusion(bf16[1536,3072]{1,0:T(8,128)(2,1)} %param.20, f32[640,1536]{1,0:T(8,128)} %fusion.39, f32[1536]{0:T(1024)S(1)} %convert_element_type.54, bf16[8,64,1536]{2,1,0:T(8,128)(2,1)} %collective-permute-done.1, bf16[8,64,1536]{2,1,0:T(8,128)(2,1)S(1)} %gather_fusion.2, ...), kind=kOutput, calls=%fused_computation.13 | convolution fusion | flops 7060258816 | bytes 24569872 | tf_op jit(solution)/shard_map/dot_general | solution.py:101
  180.8 0.6 copy-done.5
  181.4 137.7 %reduce-scatter.2.cloned.1.call-done = f32[384,640]{0,1:T(8,128)} async-done(((f32[3072,640]{0,1:T(8,128)}), f32[384,640]{0,1:T(8,128)}) %reduce-scatter.2.cloned.1.call-update) | async-done | bytes 983056 | tf_op jit(solution)/shard_map/reduce_scatter | solution.py:100
  319.1 2.4 fusion.19
  (31 shorter events, 0.4 us)
Async XLA Ops:
  6.5 77.7 %all-gather.3.cloned.1.call-start = ((), (), s32[]{:S(2)}) async-start(), calls=%async_computation.1 | async-start | bytes 4423680 | tf_op jit(solution)/shard_map/all_gather | solution.py:45
  7.3 140.3 %all-gather.5.cloned.1.call-start = ((), (), s32[]{:S(2)}) async-start(), calls=%async_computation.2 | async-start | bytes 3538944 | tf_op jit(solution)/shard_map/all_gather | solution.py:81
  11.7 3.9 %collective-permute-start = (bf16[8,384,64]{1,2,0:T(8,128)(2,1)S(1)}, bf16[8,384,64]{1,2,0:T(8,128)(2,1)S(1)}, u32[]{:S(2)}, u32[]{:S(2)}) collective-permute-start(bf16[8,384,64]{1,2,0:T(8,128)(2,1)S(1)} %select_select_fusion.2), channel_id=1, source_target_pairs={{0,1},{1,0},{2,3},{3,2},{4,5},{5,4},{6,7},{7,6},{8,9},{9,8},{10,11... | collective-permute-start | bytes 1179656 | tf_op jit(solution)/shard_map/ppermute | solution.py:14
  16.6 302.5 %reduce-scatter.2.cloned.1.call-start = ((), (), s32[]{:S(2)}) async-start(), calls=%async_computation.3 | async-start | bytes 8847360 | tf_op jit(solution)/shard_map/reduce_scatter | solution.py:100
  25.9 9.3 %copy-start.6 = (s32[1,8]{1,0:T(1,128)S(1)}, s32[1,8]{1,0:T(1,128)}, u32[]{:S(2)}) copy-start(s32[1,8]{1,0:T(1,128)} %param.17) | copy-start | bytes 100
  25.9 9.5 %copy-start.4 = (bf16[1536]{0:T(1024)(128)(2,1)S(1)}, bf16[1536]{0:T(1024)(128)(2,1)}, u32[]{:S(2)}) copy-start(bf16[1536]{0:T(1024)(128)(2,1)} %param.19) | copy-start | bytes 9220
  26.0 9.6 %copy-start.3 = (bf16[1,8,3,3072]{3,1,2,0:T(8,128)(2,1)S(1)}, bf16[1,8,3,3072]{3,1,2,0:T(8,128)(2,1)}, u32[]{:S(2)}) copy-start(bf16[1,8,3,3072]{3,1,2,0:T(8,128)(2,1)} %param.15) | copy-start | bytes 442372
  26.2 137.7 %collective-permute-start.1 = (bf16[8,64,1536]{2,1,0:T(8,128)(2,1)S(1)}, bf16[8,64,1536]{2,1,0:T(8,128)(2,1)}, u32[]{:S(2)}, u32[]{:S(2)}) collective-permute-start(bf16[8,64,1536]{2,1,0:T(8,128)(2,1)S(1)} %select_select_fusion), channel_id=1, source_target_pairs={{0,1},{1,0},{2,3},{3,2},{4,5},{5,4},{6,7},{7,6},{8,9},{9,8},{10,11... | collective-permute-start | bytes 4718600 | tf_op jit(solution)/shard_map/ppermute | solution.py:14
  84.2 6.6 %copy-start = (f32[640,3072]{1,0:T(8,128)S(1)}, f32[640,3072]{1,0:T(8,128)}, u32[]{:S(2)}) copy-start(f32[640,3072]{1,0:T(8,128)} %fusion.25) | copy-start | bytes 23592964
  147.5 6.0 %copy-start.1 = (bf16[640,3072]{1,0:T(8,128)(2,1)S(1)}, bf16[640,3072]{1,0:T(8,128)(2,1)}, u32[]{:S(2)}) copy-start(bf16[640,3072]{1,0:T(8,128)(2,1)} %fusion.5) | copy-start | bytes 11796484
  180.7 0.7 copy-start.5
  180.7 138.3 %copy-start.2 = (bf16[640,384]{1,0:T(8,128)(2,1)S(1)}, bf16[640,384]{1,0:T(8,128)(2,1)}, u32[]{:S(2)}) copy-start(bf16[640,384]{1,0:T(8,128)(2,1)} %param.14) | copy-start | bytes 1474564
Sparse Core Ops, SparseCore 0:
  9.4 74.7 all-gather.2
  86.2 61.2 all-gather.4
  180.9 138.1 reduce-scatter.1
where the time goes:
time: 328 us
  waiting for transfers between devices  233 us (71%)
  matrix products  46.1 us (14%)
  local copies, waits for them, and re-layouts  25.7 us (8%)
  between operations  13.3 us (4%)
  other arithmetic  9.05 us (3%)
    reduce_scatter x1, waiting for transfers between devices, on_device(): lax.psum_scatter(lax.dot_general(second_weight, activated, (((0,), (1,)),...  138 us
    all_gather x1, waiting for transfers between devices, on_device(): lax.all_gather(down_now, 'tensor', axis=1, tiled=True)  50.4 us
    all_gather x1, waiting for transfers between devices, on_device(): lax.all_gather(tokens, 'tensor', axis=1, tiled=True).astype(jnp.float32)  44.3 us
    gather x2, local copies, waits for them, and re-layouts, pick_owned(): up_matrix_rows = jnp.take(adapter_up_matrices, request_index_list, axis=0)  18.2 us
    dot_general x1, matrix products, on_device(): lax.dot_general(second_weight, activated, (((0,), (1,)), ((), ())), prefe...  16.9 us
    dot_general x1, matrix products, on_device(): jnp.dot(modded, first_weight, preferred_element_type=jnp.float32)  10.4 us
    gather x2, local copies, waits for them, and re-layouts, pick_owned(): jnp.take(adapter_down_matrices, request_index_list, axis=0)  6.83 us
  transfers between devices with their start and end apart: 5, of which 3 were waited for; matrix products, arithmetic and copies ran while one was open for 19% of the time, Pallas kernels for 0%

commit v1 on v0

--- a/solution.py
+++ b/solution.py
@@ -1,7 +1,464 @@
+import functools
+
 import jax
 import jax.numpy as jnp
 from jax import lax
+from jax.experimental import pallas as pl
+from jax.experimental.pallas import tpu as pltpu
 from jax.sharding import PartitionSpec as P
+
+BF = jnp.bfloat16
+F32 = jnp.float32
+VMEM_LIMIT = 56 * 1024 * 1024
+HIGH = lax.Precision.HIGHEST
+ANY = pl.BlockSpec(memory_space=pl.ANY)
+SMEM = pl.BlockSpec(memory_space=pltpu.SMEM)
+WHOLE = pl.BlockSpec(memory_space=pltpu.VMEM)
+
+
+def params(**more):
+    return pltpu.CompilerParams(vmem_limit_bytes=VMEM_LIMIT, **more)
+
+
+def cost(flops, nbytes, trans=0):
+    return pl.CostEstimate(
+        flops=int(flops), bytes_accessed=int(nbytes), transcendentals=int(trans)
+    )
+
+
+def ring_order(count):
+    cols = 2 if count < 32 else 4
+    rows = count // cols
+    walk = [r * cols for r in range(rows)]
+    for i, r in enumerate(reversed(range(rows))):
+        across = list(range(1, cols))
+        walk += [r * cols + c for c in (across if i % 2 == 0 else across[::-1])]
+    return walk
+
+
+def send_kernel(ids, down_ref, up_ref, down_out, up_out, sem):
+    count = down_out.shape[0]
+    copies = []
+    for r in range(count):
+        copies.append(pltpu.make_async_copy(down_ref.at[ids[r]], down_out.at[r], sem.at[2 * r]))
+        copies.append(pltpu.make_async_copy(up_ref.at[ids[r]], up_out.at[r], sem.at[2 * r + 1]))
+    for c in copies:
+        c.start()
+    for c in copies:
+        c.wait()
+
+
+def fetch_adapters(ids, owned, store_ref, recv_ref, dst, sem, wait):
+    count = recv_ref.shape[0]
+    rank = recv_ref.shape[1]
+    for r in range(count):
+        here = dst.at[pl.ds(r * rank, rank)]
+        if wait:
+            pltpu.make_async_copy(recv_ref.at[r], here, sem.at[r]).wait()
+            continue
+
+        @pl.when(owned[r] == 1)
+        def _():
+            pltpu.make_async_copy(store_ref.at[ids[r]], here, sem.at[r]).start()
+
+        @pl.when(owned[r] == 0)
+        def _():
+            pltpu.make_async_copy(recv_ref.at[r], here, sem.at[r]).start()
+
+
+def prep_kernel(
+    ids, owned, lengths, x_ref, mod_ref, down_ref, recv_ref,
+    low_out, stat_out, side_out, hot_out, down_now, sem,
+):
+    rows, feat = x_ref.shape
+    reqs = recv_ref.shape[0]
+    rank = recv_ref.shape[1]
+    fetch_adapters(ids, owned, down_ref, recv_ref, down_now, sem, False)
+    x = x_ref[...].astype(F32)
+    mean = jnp.mean(x, axis=1, keepdims=True)
+    cent = x - mean
+    m2 = jnp.sum(cent * cent, axis=1, keepdims=True)
+    row = lax.broadcasted_iota(jnp.int32, (rows, 128), 0)
+    lane = lax.broadcasted_iota(jnp.int32, (rows, 128), 1)
+    hot = jnp.zeros((rows, 128), F32)
+    begin = jnp.int32(0)
+    for r in range(reqs):
+        end = begin + lengths[r]
+        hot = jnp.where((lane == r) & (row >= begin) & (row < end), 1.0, hot)
+        begin = end
+    hot_out[...] = hot.astype(BF)
+    stat_out[...] = jnp.where(lane == 0, mean, jnp.where(lane == 1, m2, 0.0)).T[:8]
+    hot8 = hot[:, :reqs].astype(BF)
+    scale_rows = jnp.dot(hot8, mod_ref[1], preferred_element_type=F32)
+    lhs = (cent * (1.0 + scale_rows)).astype(BF)
+    hot_t = hot.T
+    fetch_adapters(ids, owned, down_ref, recv_ref, down_now, sem, True)
+    every = lax.dot_general(
+        down_now[...], lhs, (((1,), (1,)), ((), ())), preferred_element_type=F32
+    )
+    total = jnp.zeros((rank, rows), F32)
+    side = jnp.zeros((rank, 128), F32)
+    lane_s = lax.broadcasted_iota(jnp.int32, (rank, 128), 1)
+    for r in range(reqs):
+        total = total + every[r * rank : (r + 1) * rank] * hot_t[r : r + 1]
+        mat = down_now[pl.ds(r * rank, rank), :].astype(F32)
+        per_scale = jnp.sum(mat * (1.0 + mod_ref[1, pl.ds(r, 1), :].astype(F32)), axis=1, keepdims=True)
+        per_shift = jnp.sum(mat * mod_ref[0, pl.ds(r, 1), :].astype(F32), axis=1, keepdims=True)
+        side = jnp.where(lane_s == r, per_scale, side)
+        side = jnp.where(lane_s == reqs + r, per_shift, side)
+    low_out[...] = total.astype(BF)
+    side_out[...] = side
+
+
+def merge(count, low_a, stat_a, side_a, low_b, stat_b, side_b, hot_ref):
+    hot_t = hot_ref[...].astype(F32).T
+    sa, sb = stat_a[...], stat_b[...]
+    gap = sa[0:1] - sb[0:1]
+    mean = 0.5 * (sa[0:1] + sb[0:1])
+    m2 = sa[1:2] + sb[1:2] + gap * gap * (count * 0.5)
+    fa, fb = side_a[...], side_b[...]
+    back = jnp.dot(fa - fb, hot_t, precision=HIGH, preferred_element_type=F32)
+    low = low_a[...].astype(F32) + low_b[...].astype(F32) + (0.5 * gap) * back
+    return low, mean, m2, fa + fb, hot_t
+
+
+def merge_kernel(count, *refs):
+    low_out, stat_out, side_out = refs[-3:]
+    low, mean, m2, side, _ = merge(count, *refs[:-3])
+    low_out[...] = low.astype(BF)
+    stat_out[...] = jnp.concatenate([mean, m2, jnp.zeros((6, mean.shape[1]), F32)], axis=0)
+    side_out[...] = side
+
+
+def last_merge_kernel(count, reqs, *refs):
+    wide_out, col_out = refs[-2:]
+    low, mean, m2, side, hot_t = merge(count, *refs[:-2])
+    rank, rows = low.shape
+    rstd = lax.rsqrt(m2 / (2 * count) + 1e-06)
+    sums = jnp.dot(pltpu.roll(side, 128 - reqs, 1), hot_t, precision=HIGH, preferred_element_type=F32)
+    low = (low * rstd + sums).astype(BF).astype(F32)
+    low = jnp.concatenate([low] * (128 // rank), axis=0).T.astype(BF)[:, :rank]
+    src = lax.broadcasted_iota(jnp.int32, (rank, reqs * rank), 0)
+    dst = lax.broadcasted_iota(jnp.int32, (rank, reqs * rank), 1)
+    spread = jnp.where(dst % rank == src, 1.0, 0.0).astype(BF)
+    hot8 = refs[6][...][:, :reqs]
+    who = lax.broadcasted_iota(jnp.int32, (reqs, reqs * rank), 0)
+    col = lax.broadcasted_iota(jnp.int32, (reqs, reqs * rank), 1)
+    mask = jnp.dot(
+        hot8, jnp.where(col // rank == who, 1.0, 0.0).astype(BF), preferred_element_type=F32
+    )
+    wide_out[...] = (jnp.dot(low, spread, preferred_element_type=F32) * mask).astype(BF)
+    both = jnp.concatenate([mean, rstd, jnp.zeros((126, rows), F32)], axis=0)
+    col_out[...] = both.T
+
+
+def normed(x, hot8, mod_ref, cols):
+    scale_rows = jnp.dot(hot8, mod_ref[1], preferred_element_type=F32)
+    shift_rows = jnp.dot(hot8, mod_ref[0], preferred_element_type=F32)
+    flat = (x.astype(F32) - cols[:, 0:1]) * cols[:, 1:2]
+    return ((1.0 + scale_rows) * flat + shift_rows).astype(BF)
+
+
+def first_kernel(blocks, reqs, fresh, idx, *refs):
+    xs = refs[:blocks]
+    hot_ref, col_ref, mod_ref, w_ref = refs[blocks : blocks + 4]
+    acc_in = None if fresh else refs[blocks + 4]
+    acc_out = refs[-1]
+    step = pl.program_id(0)
+    hot8 = hot_ref[...][:, :reqs]
+    cols = col_ref[...]
+    for k in range(blocks):
+
+        @pl.when(step == k)
+        def _(k=k):
+            lhs = normed(xs[k][...], hot8, mod_ref, cols)
+            part = jnp.dot(lhs, w_ref[...], preferred_element_type=F32)
+            if k == 0 and fresh:
+                acc_out[...] = part
+            elif k == 0:
+                acc_out[...] = acc_in[...] + part
+            else:
+                acc_out[...] += part
+
+
+def first_call(idx, xs, hot, cols, mod, weight, acc):
+    blocks = len(xs)
+    rows, feat = xs[0].shape
+    hidden = weight.shape[1]
+    reqs = mod.shape[1]
+    fresh = acc is None
+    full = pl.BlockSpec((rows, hidden), lambda i, s: (0, 0))
+    in_specs = [pl.BlockSpec((rows, feat), lambda i, s: (0, 0))] * blocks + [
+        pl.BlockSpec((rows, 128), lambda i, s: (0, 0)),
+        pl.BlockSpec((rows, 128), lambda i, s: (0, 0)),
+        pl.BlockSpec((3, reqs, feat), lambda i, s: (0, 0, s[i])),
+        pl.BlockSpec((feat, hidden), lambda i, s: (s[i], 0)),
+    ]
+    args = list(xs) + [hot, cols, mod, weight]
+    if not fresh:
+        in_specs.append(full)
+        args.append(acc)
+    return pl.pallas_call(
+        functools.partial(first_kernel, blocks, reqs, fresh),
+        grid_spec=pltpu.PrefetchScalarGridSpec(
+            num_scalar_prefetch=1,
+            grid=(blocks,),
+            in_specs=in_specs,
+            out_specs=full,
+        ),
+        out_shape=jax.ShapeDtypeStruct((rows, hidden), F32),
+        compiler_params=params(),
+        cost_estimate=cost(2 * rows * feat * hidden * blocks, (blocks + 4) * feat * hidden * 2),
+        name="first_blocks",
+    )(idx, *args)
+
+
+def finish_kernel(
+    reqs, idx, ids, owned, x_ref, hot_ref, col_ref, mod_ref, w_ref, acc_ref, wide_ref,
+    bias_ref, up_ref, recv_ref, w2_ref, act_out, part_out, up_now, sem,
+):
+    step = pl.program_id(0)
+
+    @pl.when(step == 0)
+    def _():
+        fetch_adapters(ids, owned, up_ref, recv_ref, up_now, sem, False)
+
+    lhs = normed(x_ref[...], hot_ref[...][:, :reqs], mod_ref, col_ref[...])
+    pre = acc_ref[...] + jnp.dot(lhs, w_ref[...], preferred_element_type=F32)
+    pre = pre + bias_ref[...].astype(F32)
+
+    @pl.when(step == 0)
+    def _():
+        fetch_adapters(ids, owned, up_ref, recv_ref, up_now, sem, True)
+
+    pre = pre + jnp.dot(wide_ref[...], up_now[...], preferred_element_type=F32)
+    act = jax.nn.gelu(pre, approximate=True).astype(BF)
+    act_out[...] = act
+    part_out[...] = jnp.dot(act, w2_ref[...], preferred_element_type=F32).astype(BF)
+
+
+def finish_call(idx, ids, owned, x, hot, cols, mod, weight, acc, wide, bias, up, recv, weight2, tiles):
+    rows, feat = x.shape
+    tile = rows // tiles
+    hidden = weight.shape[1]
+    reqs, rank = recv.shape[:2]
+    tiled = lambda width: pl.BlockSpec((tile, width), lambda i, *s: (i, 0))
+    return pl.pallas_call(
+        functools.partial(finish_kernel, reqs),
+        grid_spec=pltpu.PrefetchScalarGridSpec(
+            num_scalar_prefetch=3,
+            grid=(tiles,),
+            in_specs=[
+                tiled(feat),
+                tiled(128),
+                tiled(128),
+                pl.BlockSpec((3, reqs, feat), lambda i, *s: (0, 0, s[0][0])),
+                pl.BlockSpec((feat, hidden), lambda i, *s: (s[0][0], 0)),
+                tiled(hidden),
+                tiled(reqs * rank),
+                pl.BlockSpec((1, hidden), lambda i, *s: (0, 0)),
+                ANY,
+                ANY,
+                pl.BlockSpec((hidden, feat), lambda i, *s: (0, s[0][0])),
+            ],
+            out_specs=[tiled(hidden), tiled(feat)],
+            scratch_shapes=[
+                pltpu.VMEM((reqs * rank, hidden), BF),
+                pltpu.SemaphoreType.DMA((reqs,)),
+            ],
+        ),
+        out_shape=[
+            jax.ShapeDtypeStruct((rows, hidden), BF),
+            jax.ShapeDtypeStruct((rows, feat), BF),
+        ],
+        compiler_params=params(),
+        cost_estimate=cost(
+            2 * rows * hidden * (2 * feat + reqs * rank), 14 * rows * hidden, rows * hidden
+        ),
+        name="finish_first",
+    )(idx, ids, owned, x, hot, cols, mod, weight, acc, wide, bias, up, recv, weight2)
+
+
+def second_kernel(idx, act_ref, w_ref, out_ref):
+    out_ref[0] = jnp.dot(act_ref[...], w_ref[...], preferred_element_type=F32)
+
+
+def second_call(idx, act, weight2, feat):
+    blocks = idx.shape[0]
+    rows, hidden = act.shape
+    return pl.pallas_call(
+        second_kernel,
+        grid_spec=pltpu.PrefetchScalarGridSpec(
+            num_scalar_prefetch=1,
+            grid=(blocks,),
+            in_specs=[
+                pl.BlockSpec((rows, hidden), lambda i, s: (0, 0)),
+                pl.BlockSpec((hidden, feat), lambda i, s: (0, s[i])),
+            ],
+            out_specs=pl.BlockSpec((1, rows, feat), lambda i, s: (i, 0, 0)),
+        ),
+        out_shape=jax.ShapeDtypeStruct((blocks, rows, feat), F32),
+        compiler_params=params(),
+        cost_estimate=cost(2 * rows * hidden * feat * blocks, blocks * rows * feat * 8),
+        name="second_blocks",
+    )(idx, act, weight2)
+
+
+def ring_device(
+    count, tokens, modulation, adapter_per_request, tokens_per_request, first_weight,
+    first_bias, second_weight, second_bias, adapter_down_matrices, adapter_up_matrices,
+):
+    me = lax.axis_index("tensor")
+    store = lax.axis_index("store")
+    rows, feat = tokens.shape
+    hidden = first_weight.shape[1]
+    stored, rank = adapter_up_matrices.shape[:2]
+    reqs = tokens_per_request.shape[1]
+    order = ring_order(count)
+    forth = [(order[i], order[(i + 1) % count]) for i in range(count)]
+    back = [(b, a) for a, b in forth]
+    table = [[0] * count for _ in range(count)]
+    for at, dev in enumerate(order):
+        table[dev] = [order[(at + k) % count] for k in range(count)]
+    mine = lax.dynamic_index_in_dim(jnp.array(table, jnp.int32), me, 0, keepdims=False)
+    half = count // 2
+
+    def at(*steps):
+        return jnp.stack([mine[k % count] for k in steps])
+
+    def go(x, route):
+        return lax.ppermute(x, "tensor", route)
+
+    down = jnp.swapaxes(adapter_down_matrices, 1, 2)
+    mod = jnp.swapaxes(modulation[0], 0, 1)
+    lengths = tokens_per_request[0]
+
+    my_ids = lax.dynamic_index_in_dim(adapter_per_request, store, 0, keepdims=False)
+    their_ids = lax.dynamic_index_in_dim(adapter_per_request, 1 - store, 0, keepdims=False)
+    owned = (my_ids // stored == store).astype(jnp.int32)
+    my_ids = jnp.clip(my_ids - store * stored, 0, stored - 1)
+    their_ids = jnp.clip(their_ids - store * stored, 0, stored - 1)
+    send_down, send_up = pl.pallas_call(
+        send_kernel,
+        in_specs=[SMEM, ANY, ANY],
+        out_specs=[ANY, ANY],
+        out_shape=[
+            jax.ShapeDtypeStruct((reqs, rank, feat), BF),
+            jax.ShapeDtypeStruct((reqs, rank, hidden), BF),
+        ],
+        scratch_shapes=[pltpu.SemaphoreType.DMA((2 * reqs,))],
+        cost_estimate=cost(0, 4 * reqs * rank * (feat + hidden)),
+        name="adapters_to_send",
+    )(their_ids, down, adapter_up_matrices)
+    swap = [(s, s ^ 1) for s in range(lax.axis_size("store"))]
+    recv_down = lax.ppermute(send_down, "store", swap)
+    recv_up = lax.ppermute(send_up, "store", swap)
+
+    my_mod = lax.dynamic_slice_in_dim(mod, me * feat, feat, 2)
+    low, stat, side, hot = pl.pallas_call(
+        prep_kernel,
+        in_specs=[SMEM, SMEM, SMEM, WHOLE, WHOLE, ANY, ANY],
+        out_specs=[WHOLE] * 4,
+        out_shape=[
+            jax.ShapeDtypeStruct((rank, rows), BF),
+            jax.ShapeDtypeStruct((8, rows), F32),
+            jax.ShapeDtypeStruct((rank, 128), F32),
+            jax.ShapeDtypeStruct((rows, 128), BF),
+        ],
+        scratch_shapes=[
+            pltpu.VMEM((reqs * rank, feat), BF),
+            pltpu.SemaphoreType.DMA((reqs,)),
+        ],
+        compiler_params=params(),
+        cost_estimate=cost(2 * rows * feat * reqs * rank, 4 * rows * feat),
+        name="own_features",
+    )(my_ids, owned, lengths, tokens, my_mod, down, recv_down)
+    span = 1
+    while span < count:
+        route = [(t, t ^ span) for t in range(count)]
+        theirs = [go(v, route) for v in (low, stat, side)]
+        last = 2 * span == count
+        args = (low, stat, side, *theirs, hot)
+        if last:
+            kernel = functools.partial(last_merge_kernel, span * feat, reqs)
+            shapes = [
+                jax.ShapeDtypeStruct((rows, reqs * rank), BF),
+                jax.ShapeDtypeStruct((rows, 128), F32),
+            ]
+        else:
+            kernel = functools.partial(merge_kernel, span * feat)
+            shapes = [jax.ShapeDtypeStruct(v.shape, v.dtype) for v in (low, stat, side)]
+        out = pl.pallas_call(
+            kernel,
+            in_specs=[WHOLE] * 7,
+            out_specs=[WHOLE] * len(shapes),
+            out_shape=shapes,
+            compiler_params=params(),
+            cost_estimate=cost(2 * 6 * rank * 128 * rows, 8 * rank * rows),
+            name="merge_sums",
+        )(*args)
+        if last:
+            wide, cols = out
+        else:
+            low, stat, side = out
+        span *= 2
+
+    cut = rows // 2
+    a = b = tokens
+    seen = [(0, tokens)]
+    for k in range(1, half):
+        a, b = go(a, forth), go(b, back)
+        seen += [(-k, a), (k, b)]
+    far = jnp.concatenate([go(a[:cut], forth), go(b[cut:], back)])
+
+    bias = first_bias.reshape(1, hidden)
+    acc = None
+    early = 2 * half - 3
+    groups = [seen[:early], seen[early:]] if half > 2 else [seen]
+    for group in groups:
+        acc = first_call(
+            at(*[k for k, _ in group]), [x for _, x in group], hot, cols, mod, first_weight, acc
+        )
+    act, far_part = finish_call(
+        at(half), my_ids, owned, far, hot, cols, mod, first_weight, acc, wide, bias,
+        adapter_up_matrices, recv_up, second_weight, 4,
+    )
+
+    steps = [s for k in range(half - 1, 0, -1) for s in (k, -k)] + [0]
+    parts = {}
+    for group in (steps[:2], steps[2:]):
+        got = second_call(at(*group), act, second_weight, feat)
+        for i, s in enumerate(group):
+            parts[s] = got[i]
+    gate = jnp.dot(
+        hot[:, :reqs], lax.dynamic_slice_in_dim(mod[2], me * feat, feat, 1),
+        preferred_element_type=F32,
+    )
+    outs = []
+    chains = 2
+    size = rows // chains
+    for c in range(chains):
+        lo = c * size
+        mid = size // 2
+        right = go(far_part[lo : lo + mid], forth)
+        left = go(far_part[lo + mid : lo + size], back)
+        for k in range(half - 1, 0, -1):
+            r = parts[k][lo : lo + size]
+            l = parts[-k][lo : lo + size]
+            if k == half - 1:
+                r = jnp.concatenate([r[:mid] + right.astype(F32), r[mid:]])
+                l = jnp.concatenate([l[:mid], l[mid:] + left.astype(F32)])
+            else:
+                r = r + right.astype(F32)
+                l = l + left.astype(F32)
+            right = go(r.astype(BF), forth)
+            left = go(l.astype(BF), back)
+        mixed = parts[0][lo : lo + size] + right.astype(F32) + left.astype(F32)
+        outs.append(
+            tokens[lo : lo + size].astype(F32)
+            + gate[lo : lo + size] * (mixed + second_bias.astype(F32))
+        )
+    return jnp.concatenate(outs).astype(BF)
 
 
 def partner(block, axis, stride):
@@ -23,7 +480,7 @@
     )
 
 
-def on_device(
+def plain_device(
     tokens,
     modulation,
     adapter_per_request,
@@ -111,6 +568,12 @@
     return block_out.astype(jnp.bfloat16)
 
 
+def on_device(count, tokens, *rest):
+    if tokens.shape[1] % 128 == 0 and count % 4 == 0 and count & (count - 1) == 0:
+        return ring_device(count, tokens, *rest)
+    return plain_device(tokens, *rest)
+
+
 def solution(mesh):
     in_specs = (
         P(("groups", "store"), "tensor"),
@@ -126,5 +589,5 @@
     )
     out_specs = P(("groups", "store"), "tensor")
     return jax.shard_map(
-        on_device, mesh=mesh, in_specs=in_specs, out_specs=out_specs, check_vma=False
-    )
+        functools.partial(on_device, mesh.shape["tensor"]), mesh=mesh, in_specs=in_specs, out_specs=out_specs, check_vma=False
+    )

time: 328 us -> 238 us (0.73)
  waiting for transfers between devices: 233 us -> 50.7 us
  Pallas kernels: 0 us -> 121 us
  matrix products: 46.1 us -> 0.26 us
  starting transfers between devices: 0.72 us -> 36.4 us
  between operations: 13.3 us -> 0.27 us
  local copies, waits for them, and re-layouts: 25.7 us -> 17.5 us
    reduce_scatter x1 -> x0, waiting for transfers between devices: 138 us -> none  [on_device(): lax.psum_scatter(lax.dot_general(second_weight, activated, (((0,), (1,)),...]
    pallas_call x0 -> x10, Pallas kernels: none -> 121 us  [the longest x1 61.6 us: ring_device(): pl.pallas_call(send_kernel, in_specs=[SMEM, ANY, ANY], out_specs=[ANY, AN...]
    all_gather x2 -> x0, waiting for transfers between devices: 94.8 us -> none  [the longest x1 50.4 us: on_device(): lax.all_gather(down_now, 'tensor', axis=1, tiled=True)]
    ppermute x2 -> x35, waiting for transfers between devices: 0.01 us -> 50.7 us  [the longest x33 50.7 us: go(): return lax.ppermute(x, 'tensor', route)]
    dot_general x5 -> x1, matrix products: 40.2 us -> 0.26 us  [ring_device(): jnp.dot(hot[:, :reqs], lax.dynamic_slice_in_dim(mod[2], me * feat, feat,...]
    ppermute x2 -> x35, starting transfers between devices: 0.64 us -> 36.4 us  [the longest x33 35.8 us: go(): return lax.ppermute(x, 'tensor', route)]
    gather x4 -> x0, local copies, waits for them, and re-layouts: 25 us -> none  [the longest x2 18.2 us: pick_owned(): up_matrix_rows = jnp.take(adapter_up_matrices, request_index_list, axis=0)]
    another operation x0 -> x2, local copies, waits for them, and re-layouts: none -> 7.65 us  [at(): return jnp.stack([mine[k % count] for k in steps])]
  transfers between devices with their start and end apart: 5 -> 35, of which waited for: 3 -> 15; matrix products, arithmetic and copies ran while one was open for 19% -> 9% of each run, Pallas kernels for 0% -> 46%
where the time goes in v1:
time: 238 us; the launch traced here: 237 us
  Pallas kernels  121 us (51%)
  waiting for transfers between devices  50.7 us (21%)
  starting transfers between devices  36.4 us (15%)
  local copies, waits for them, and re-layouts  17.5 us (7%)
  other arithmetic  10.4 us (4%)
    pallas_call x1, Pallas kernels, ring_device(): pl.pallas_call(send_kernel, in_specs=[SMEM, ANY, ANY], out_specs=[ANY, AN...  61.6 us
    ppermute x33, waiting for transfers between devices, go(): return lax.ppermute(x, 'tensor', route)  50.7 us
    ppermute x33, starting transfers between devices, go(): return lax.ppermute(x, 'tensor', route)  35.8 us
    pallas_call x2, Pallas kernels, first_call(): pl.pallas_call(functools.partial(first_kernel, blocks, reqs, fresh), grid...  20.9 us
    pallas_call x2, Pallas kernels, second_call(): pl.pallas_call(second_kernel, grid_spec=pltpu.PrefetchScalarGridSpec(num_...  16.5 us
    pallas_call x1, Pallas kernels, finish_call(): pl.pallas_call(functools.partial(finish_kernel, reqs), grid_spec=pltpu.Pr...  11.1 us
    pallas_call x3, Pallas kernels, ring_device(): pl.pallas_call(kernel, in_specs=[WHOLE] * 7, out_specs=[WHOLE] * len(shap...  7.65 us
    another operation x2, local copies, waits for them, and re-layouts, at(): return jnp.stack([mine[k % count] for k in steps])  7.65 us
  transfers between devices with their start and end apart: 35, of which 15 were waited for; matrix products, arithmetic and copies ran while one was open for 9% of the time, Pallas kernels for 46%

profile of v1, /device:TPU:0, one launch (start us, length us, event | category | flops | bytes accessed | tf_op | source)
XLA Modules:
  0.0 236.7 jit_solution(17082911552321182450)
XLA Ops:
  0.0 3.0 %collective-permute-start.1 = (bf16[640,384]{1,0:T(8,128)(2,1)}, bf16[640,384]{1,0:T(8,128)(2,1)S(1)}, u32[]{:S(2)}, u32[]{:S(2)}) collective-permute-start(bf16[640,384]{1,0:T(8,128)(2,1)} %refs_0_.1), channel_id=1, source_target_pairs={{0,4},{4,8},{8,12},{12,14},{14,10},{10,6},{6,2},{2,0},{1,5},{5,9},... | collective-permute-start | bytes 1474568 | tf_op jit(solution)/shard_map/ppermute | solution.py:330
  3.0 11.3 %collective-permute-done.1.refs_1_ = bf16[640,384]{1,0:T(8,128)(2,1)S(1)} collective-permute-done((bf16[640,384]{1,0:T(8,128)(2,1)}, bf16[640,384]{1,0:T(8,128)(2,1)S(1)}, u32[]{:S(2)}, u32[]{:S(2)}) %collective-permute-start.1) | collective-permute-done | bytes 491552 | tf_op jit(solution)/shard_map/ppermute | solution.py:330
  17.6 61.6 %adapters_to_send.1 = (bf16[8,64,384]{2,1,0:T(8,128)(2,1)}, bf16[8,64,1536]{2,1,0:T(8,128)(2,1)}) custom-call(s32[8]{0:T(128)} %fusion.44.ids, bf16[128,64,384]{2,1,0:T(8,128)(2,1)} %bitcast.136, bf16[128,64,1536]{2,1,0:T(8,128)(2,1)} %up_ref.3), custom_call_target="tpu_custom_call" | custom-call | bytes 3932160 | tf_op jit(solution)/shard_map/adapters_to_send/pallas_call | solution.py:341
  83.0 3.3 %own_features.1 = (bf16[64,640]{1,0:T(8,128)(2,1)}, f32[8,640]{1,0:T(8,128)}, f32[64,128]{1,0:T(8,128)}, bf16[640,128]{1,0:T(8,128)(2,1)}) custom-call(s32[8]{0:T(128)} %subtract_clamp_fusion.ids, s32[8]{0:T(128)} %compare_convert_fusion.owned, s32[8]{0:T(128)} %bitcast.142, bf16[640,384]{1,0:T(8,128)(2,1)} %refs_0_.1, ...), custom_call_target="tpu_custom_call" | custom-call | flops 251658240 | bytes 983040 | tf_op jit(solution)/shard_map/own_features/pallas_call | solution.py:358
  88.4 3.7 %collective-permute-done.10.refs_4_ = f32[8,640]{1,0:T(8,128)S(1)} collective-permute-done((f32[8,640]{1,0:T(8,128)}, f32[8,640]{1,0:T(8,128)S(1)}, u32[]{:S(2)}, u32[]{:S(2)}) %collective-permute-start.10) | collective-permute-done | bytes 20512 | tf_op jit(solution)/shard_map/ppermute | solution.py:330
  96.7 2.2 merge_sums.3
  101.6 6.8 %collective-permute-done.13.refs_4_ = f32[8,640]{1,0:T(8,128)S(1)} collective-permute-done((f32[8,640]{1,0:T(8,128)}, f32[8,640]{1,0:T(8,128)S(1)}, u32[]{:S(2)}, u32[]{:S(2)}) %collective-permute-start.13) | collective-permute-done | bytes 20512 | tf_op jit(solution)/shard_map/ppermute | solution.py:330
  109.2 3.3 %collective-permute-done.14.refs_5_ = f32[64,128]{1,0:T(8,128)S(1)} collective-permute-done((f32[64,128]{1,0:T(8,128)}, f32[64,128]{1,0:T(8,128)S(1)}, u32[]{:S(2)}, u32[]{:S(2)}) %collective-permute-start.14) | collective-permute-done | bytes 32800 | tf_op jit(solution)/shard_map/ppermute | solution.py:330
  113.8 2.2 merge_sums.4
  116.0 2.6 %collective-permute-start.16 = (f32[8,640]{1,0:T(8,128)}, f32[8,640]{1,0:T(8,128)S(1)}, u32[]{:S(2)}, u32[]{:S(2)}) collective-permute-start(f32[8,640]{1,0:T(8,128)} %get-tuple-element.30.refs_1_), channel_id=1, source_target_pairs={{0,8},{2,10},{4,12},{6,14},{8,0},{10,2},{12,4},{14,6},{1,9},{3,11}... | collective-permute-start | bytes 61448 | tf_op jit(solution)/shard_map/ppermute | solution.py:330
  125.4 3.8 %stack.14.idx = s32[5]{0:T(128)} concatenate(s32[1]{0:T(128)} %bitcast.13, s32[1]{0:T(128)} %bitcast.12, s32[1]{0:T(128)} %bitcast.11, s32[1]{0:T(128)} %bitcast.10, s32[1]{0:T(128)} %bitcast.9), dimensions={0} | concatenate | bytes 40 | tf_op jit(solution)/shard_map/stack | solution.py:327
  129.2 3.8 %stack.12.idx = s32[5]{0:T(128)} concatenate(s32[1]{0:T(128)} %bitcast.9, s32[1]{0:T(128)} %bitcast.10, s32[1]{0:T(128)} %bitcast.11, s32[1]{0:T(128)} %bitcast.12, s32[1]{0:T(128)} %bitcast.13), dimensions={0} | concatenate | bytes 40 | tf_op jit(solution)/shard_map/stack | solution.py:327
  134.9 3.2 %merge_sums.5 = (bf16[640,512]{1,0:T(8,128)(2,1)}, f32[640,128]{1,0:T(8,128)}) custom-call(bf16[64,640]{1,0:T(8,128)(2,1)} %get-tuple-element.29.refs_0_, f32[8,640]{1,0:T(8,128)} %get-tuple-element.30.refs_1_, f32[64,128]{1,0:T(8,128)} %get-tuple-element.31.refs_2_, bf16[64,640]{1,0:T(8,128)(2,1)} %copy-done.11, f32[8,640]{1,0:T(8,128)} %copy-done.16, ...), custom_call_target="tpu_custom_call" | custom-call | flops 62914560 | bytes 327680 | tf_op jit(solution)/shard_map/merge_sums/pallas_call | solution.py:391
  140.5 12.4 %first_blocks.2.refs_6_ = f32[640,1536]{1,0:T(8,128)} custom-call(s32[5]{0:T(128)} %stack.14.idx, bf16[640,384]{1,0:T(8,128)(2,1)} %refs_0_.1, bf16[640,384]{1,0:T(8,128)(2,1)} %copy-done.7, bf16[640,384]{1,0:T(8,128)(2,1)} %copy-done.8, bf16[640,384]{1,0:T(8,128)(2,1)} %collective-permute-done.2.refs_3_, bf16[640,384]{1,0:T(8,128)(2,1)} %collective-permute-done.6.refs_4_, ...), custom_call_target="tpu_custom_call" | custom-call | flops 3774873600 | bytes 10616832 | tf_op jit(solution)/shard_map/first_blocks/pallas_call | solution.py:201
  152.9 8.5 %first_blocks.3.acc_ref = f32[640,1536]{1,0:T(8,128)} custom-call(s32[2]{0:T(128)} %pad_add_fusion.idx, bf16[640,384]{1,0:T(8,128)(2,1)} %copy-done.5, bf16[640,384]{1,0:T(8,128)(2,1)} %copy-done.6, bf16[640,128]{1,0:T(8,128)(2,1)} %get-tuple-element.22.refs_6_.refs_5_.refs_2_.hot_ref, f32[640,128]{1,0:T(8,128)} %get-tuple-element.32.refs_6_.refs_3_.col_ref, ...), custom_call_target="tpu_custom_call" | custom-call | flops 1509949440 | bytes 7077888 | tf_op jit(solution)/shard_map/first_blocks/pallas_call | solution.py:201
  163.5 11.1 %finish_first.1 = (bf16[640,1536]{1,0:T(8,128)(2,1)}, bf16[640,384]{1,0:T(8,128)(2,1)}) custom-call(s32[1]{0:T(128)} %bitcast.14.idx, s32[8]{0:T(128)} %subtract_clamp_fusion.ids, s32[8]{0:T(128)} %compare_convert_fusion.owned, bf16[640,384]{1,0:T(8,128)(2,1)} %pad_maximum_fusion.x_ref, bf16[640,128]{1,0:T(8,128)(2,1)} %get-tuple-element.22.refs_6_.refs_5_.refs_2_.hot_ref, ...), custom_call_target="tpu_custom_call" | custom-call | flops 2516582400 | bytes 13762560 | tf_op jit(solution)/shard_map/finish_first/pallas_call | solution.py:246
  179.8 6.0 %second_blocks.3 = f32[2,640,384]{2,1,0:T(8,128)} custom-call(s32[2]{0:T(128)} %pad_add_fusion.1.idx, bf16[640,1536]{1,0:T(8,128)(2,1)} %get-tuple-element.35.act_ref, bf16[1536,3072]{1,0:T(8,128)(2,1)} %w_ref.5), custom_call_target="tpu_custom_call" | custom-call | flops 1509949440 | bytes 3932160 | tf_op jit(solution)/shard_map/second_blocks/pallas_call | solution.py:289
  187.5 10.6 %second_blocks.2 = f32[5,640,384]{2,1,0:T(8,128)} custom-call(s32[5]{0:T(128)} %stack.12.idx, bf16[640,1536]{1,0:T(8,128)(2,1)} %get-tuple-element.35.act_ref, bf16[1536,3072]{1,0:T(8,128)(2,1)} %w_ref.5), custom_call_target="tpu_custom_call" | custom-call | flops 3774873600 | bytes 9830400 | tf_op jit(solution)/shard_map/second_blocks/pallas_call | solution.py:289
  202.7 2.5 %collective-permute-done.20 = bf16[320,384]{1,0:T(8,128)(2,1)S(1)} collective-permute-done((bf16[320,384]{1,0:T(8,128)(2,1)S(1)}, bf16[320,384]{1,0:T(8,128)(2,1)S(1)}, u32[]{:S(2)}, u32[]{:S(2)}) %collective-permute-start.20) | collective-permute-done | bytes 245792 | tf_op jit(solution)/shard_map/ppermute | solution.py:330
  205.9 3.2 %collective-permute-done.28 = bf16[320,384]{1,0:T(8,128)(2,1)S(1)} collective-permute-done((bf16[320,384]{1,0:T(8,128)(2,1)S(1)}, bf16[320,384]{1,0:T(8,128)(2,1)S(1)}, u32[]{:S(2)}, u32[]{:S(2)}) %collective-permute-start.28) | collective-permute-done | bytes 245792 | tf_op jit(solution)/shard_map/ppermute | solution.py:330
  209.3 5.1 %collective-permute-done.21 = bf16[320,384]{1,0:T(8,128)(2,1)S(1)} collective-permute-done((bf16[320,384]{1,0:T(8,128)(2,1)S(1)}, bf16[320,384]{1,0:T(8,128)(2,1)S(1)}, u32[]{:S(2)}, u32[]{:S(2)}) %collective-permute-start.21) | collective-permute-done | bytes 245792 | tf_op jit(solution)/shard_map/ppermute | solution.py:330
  219.6 4.0 %collective-permute-done.25 = bf16[320,384]{1,0:T(8,128)(2,1)S(1)} collective-permute-done((bf16[320,384]{1,0:T(8,128)(2,1)S(1)}, bf16[320,384]{1,0:T(8,128)(2,1)S(1)}, u32[]{:S(2)}, u32[]{:S(2)}) %collective-permute-start.25) | collective-permute-done | bytes 245792 | tf_op jit(solution)/shard_map/ppermute | solution.py:330
  223.6 2.8 %collective-permute-done.33 = bf16[320,384]{1,0:T(8,128)(2,1)S(1)} collective-permute-done((bf16[320,384]{1,0:T(8,128)(2,1)S(1)}, bf16[320,384]{1,0:T(8,128)(2,1)S(1)}, u32[]{:S(2)}, u32[]{:S(2)}) %collective-permute-start.33) | collective-permute-done | bytes 245792 | tf_op jit(solution)/shard_map/ppermute | solution.py:330
  230.6 2.3 collective-permute-done.26
  (126 shorter events, 56.9 us)
Async XLA Ops:
  0.0 14.4 %collective-permute-start.1 = (bf16[640,384]{1,0:T(8,128)(2,1)}, bf16[640,384]{1,0:T(8,128)(2,1)S(1)}, u32[]{:S(2)}, u32[]{:S(2)}) collective-permute-start(bf16[640,384]{1,0:T(8,128)(2,1)} %refs_0_.1), channel_id=1, source_target_pairs={{0,4},{4,8},{8,12},{12,14},{14,10},{10,6},{6,2},{2,0},{1,5},{5,9},... | collective-permute-start | bytes 1474568 | tf_op jit(solution)/shard_map/ppermute | solution.py:330
  3.0 13.2 %collective-permute-start.5 = (bf16[640,384]{1,0:T(8,128)(2,1)}, bf16[640,384]{1,0:T(8,128)(2,1)S(1)}, u32[]{:S(2)}, u32[]{:S(2)}) collective-permute-start(bf16[640,384]{1,0:T(8,128)(2,1)} %refs_0_.1), channel_id=1, source_target_pairs={{4,0},{8,4},{12,8},{14,12},{10,14},{6,10},{2,6},{0,2},{5,1},{9,5},... | collective-permute-start | bytes 1474568 | tf_op jit(solution)/shard_map/ppermute | solution.py:330
  14.4 78.9 %collective-permute-start.2 = (bf16[640,384]{1,0:T(8,128)(2,1)S(1)}, bf16[640,384]{1,0:T(8,128)(2,1)}, u32[]{:S(2)}, u32[]{:S(2)}) collective-permute-start(bf16[640,384]{1,0:T(8,128)(2,1)S(1)} %collective-permute-done.1.refs_1_), channel_id=1, source_target_pairs={{0,4},{4,8},{8,12},{12,14},{14,10},{10,6},{6,2},{2,0},{1,5},{5,9},... | collective-permute-start | bytes 1474568 | tf_op jit(solution)/shard_map/ppermute | solution.py:330
  16.2 78.6 %collective-permute-start.6 = (bf16[640,384]{1,0:T(8,128)(2,1)S(1)}, bf16[640,384]{1,0:T(8,128)(2,1)}, u32[]{:S(2)}, u32[]{:S(2)}) collective-permute-start(bf16[640,384]{1,0:T(8,128)(2,1)S(1)} %collective-permute-done.5.refs_2_), channel_id=1, source_target_pairs={{4,0},{8,4},{12,8},{14,12},{10,14},{6,10},{2,6},{0,2},{5,1},{9,5},... | collective-permute-start | bytes 1474568 | tf_op jit(solution)/shard_map/ppermute | solution.py:330
  79.3 82.9 %collective-permute-start.18 = (bf16[8,64,1536]{2,1,0:T(8,128)(2,1)}, bf16[8,64,1536]{2,1,0:T(8,128)(2,1)S(1)}, u32[]{:S(2)}, u32[]{:S(2)}) collective-permute-start(bf16[8,64,1536]{2,1,0:T(8,128)(2,1)} %get-tuple-element.34), channel_id=1, source_target_pairs={{0,1},{1,0},{2,3},{3,2},{4,5},{5,4},{6,7},{7,6},{8,9},{9,8},{10,11... | collective-permute-start | bytes 4718600 | tf_op jit(solution)/shard_map/ppermute | solution.py:355
  86.3 10.4 %collective-permute-start.9 = (bf16[64,640]{1,0:T(8,128)(2,1)}, bf16[64,640]{1,0:T(8,128)(2,1)}, u32[]{:S(2)}, u32[]{:S(2)}) collective-permute-start(bf16[64,640]{1,0:T(8,128)(2,1)} %get-tuple-element.23.refs_0_), channel_id=1, source_target_pairs={{0,2},{2,0},{4,6},{6,4},{8,10},{10,8},{12,14},{14,12},{1,3},{3,1},... | collective-permute-start | bytes 245768 | tf_op jit(solution)/shard_map/ppermute | solution.py:330
  93.2 44.8 %collective-permute-start.3 = (bf16[640,384]{1,0:T(8,128)(2,1)}, bf16[640,384]{1,0:T(8,128)(2,1)S(1)}, u32[]{:S(2)}, u32[]{:S(2)}) collective-permute-start(bf16[640,384]{1,0:T(8,128)(2,1)} %collective-permute-done.2.refs_3_), channel_id=1, source_target_pairs={{0,4},{4,8},{8,12},{12,14},{14,10},{10,6},{6,2},{2,0},{1,5},{5,9},... | collective-permute-start | bytes 1474568 | tf_op jit(solution)/shard_map/ppermute | solution.py:330
  94.8 43.7 %collective-permute-start.7 = (bf16[640,384]{1,0:T(8,128)(2,1)}, bf16[640,384]{1,0:T(8,128)(2,1)S(1)}, u32[]{:S(2)}, u32[]{:S(2)}) collective-permute-start(bf16[640,384]{1,0:T(8,128)(2,1)} %collective-permute-done.6.refs_4_), channel_id=1, source_target_pairs={{4,0},{8,4},{12,8},{14,12},{10,14},{6,10},{2,6},{0,2},{5,1},{9,5},... | collective-permute-start | bytes 1474568 | tf_op jit(solution)/shard_map/ppermute | solution.py:330
  98.9 9.5 %collective-permute-start.13 = (f32[8,640]{1,0:T(8,128)}, f32[8,640]{1,0:T(8,128)S(1)}, u32[]{:S(2)}, u32[]{:S(2)}) collective-permute-start(f32[8,640]{1,0:T(8,128)} %get-tuple-element.27.refs_1_), channel_id=1, source_target_pairs={{0,4},{2,6},{4,0},{6,2},{8,12},{10,14},{12,8},{14,10},{1,5},{3,7},... | collective-permute-start | bytes 61448 | tf_op jit(solution)/shard_map/ppermute | solution.py:330
  100.9 11.7 %collective-permute-start.12 = (bf16[64,640]{1,0:T(8,128)(2,1)}, bf16[64,640]{1,0:T(8,128)(2,1)S(1)}, u32[]{:S(2)}, u32[]{:S(2)}) collective-permute-start(bf16[64,640]{1,0:T(8,128)(2,1)} %get-tuple-element.26.refs_0_), channel_id=1, source_target_pairs={{0,4},{2,6},{4,0},{6,2},{8,12},{10,14},{12,8},{14,10},{1,5},{3,7},... | collective-permute-start | bytes 245768 | tf_op jit(solution)/shard_map/ppermute | solution.py:330
  120.4 13.2 %collective-permute-start.15 = (bf16[64,640]{1,0:T(8,128)(2,1)}, bf16[64,640]{1,0:T(8,128)(2,1)S(1)}, u32[]{:S(2)}, u32[]{:S(2)}) collective-permute-start(bf16[64,640]{1,0:T(8,128)(2,1)} %get-tuple-element.29.refs_0_), channel_id=1, source_target_pairs={{0,8},{2,10},{4,12},{6,14},{8,0},{10,2},{12,4},{14,6},{1,9},{3,11}... | collective-permute-start | bytes 245768 | tf_op jit(solution)/shard_map/ppermute | solution.py:330
  122.1 11.5 %collective-permute-start.17 = (f32[64,128]{1,0:T(8,128)}, f32[64,128]{1,0:T(8,128)S(1)}, u32[]{:S(2)}, u32[]{:S(2)}) collective-permute-start(f32[64,128]{1,0:T(8,128)} %get-tuple-element.31.refs_2_), channel_id=1, source_target_pairs={{0,8},{2,10},{4,12},{6,14},{8,0},{10,2},{12,4},{14,6},{1,9},{3,11}... | collective-permute-start | bytes 98312 | tf_op jit(solution)/shard_map/ppermute | solution.py:330
  138.1 23.3 %collective-permute-start.4 = (bf16[320,384]{1,0:T(8,128)(2,1)S(1)}, bf16[320,384]{1,0:T(8,128)(2,1)S(1)}, u32[]{:S(2)}, u32[]{:S(2)}) collective-permute-start(bf16[320,384]{1,0:T(8,128)(2,1)S(1)} %slice.306), channel_id=1, source_target_pairs={{0,4},{4,8},{8,12},{12,14},{14,10},{10,6},{6,2},{2,0},{1,5},{5,9},... | collective-permute-start | bytes 737288 | tf_op jit(solution)/shard_map/ppermute | solution.py:330
  138.5 22.9 %collective-permute-start.8 = (bf16[320,384]{1,0:T(8,128)(2,1)S(1)}, bf16[320,384]{1,0:T(8,128)(2,1)S(1)}, u32[]{:S(2)}, u32[]{:S(2)}) collective-permute-start(bf16[320,384]{1,0:T(8,128)(2,1)S(1)} %slice.307), channel_id=1, source_target_pairs={{4,0},{8,4},{12,8},{14,12},{10,14},{6,10},{2,6},{0,2},{5,1},{9,5},... | collective-permute-start | bytes 737288 | tf_op jit(solution)/shard_map/ppermute | solution.py:330
  175.7 22.4 %collective-permute-start.19 = (bf16[160,384]{1,0:T(8,128)(2,1)S(1)}, bf16[160,384]{1,0:T(8,128)(2,1)S(1)}, u32[]{:S(2)}, u32[]{:S(2)}) collective-permute-start(bf16[160,384]{1,0:T(8,128)(2,1)S(1)} %get-tuple-element.54), channel_id=1, source_target_pairs={{0,4},{4,8},{8,12},{12,14},{14,10},{10,6},{6,2},{2,0},{1,5},{5,9},... | collective-permute-start | bytes 368648 | tf_op jit(solution)/shard_map/ppermute | solution.py:330
  176.1 22.0 %collective-permute-start.23 = (bf16[160,384]{1,0:T(8,128)(2,1)S(1)}, bf16[160,384]{1,0:T(8,128)(2,1)S(1)}, u32[]{:S(2)}, u32[]{:S(2)}) collective-permute-start(bf16[160,384]{1,0:T(8,128)(2,1)S(1)} %get-tuple-element.57), channel_id=1, source_target_pairs={{4,0},{8,4},{12,8},{14,12},{10,14},{6,10},{2,6},{0,2},{5,1},{9,5},... | collective-permute-start | bytes 368648 | tf_op jit(solution)/shard_map/ppermute | solution.py:330
  177.8 20.3 %collective-permute-start.27 = (bf16[160,384]{1,0:T(8,128)(2,1)S(1)}, bf16[160,384]{1,0:T(8,128)(2,1)S(1)}, u32[]{:S(2)}, u32[]{:S(2)}) collective-permute-start(bf16[160,384]{1,0:T(8,128)(2,1)S(1)} %get-tuple-element.56), channel_id=1, source_target_pairs={{0,4},{4,8},{8,12},{12,14},{14,10},{10,6},{6,2},{2,0},{1,5},{5,9},... | collective-permute-start | bytes 368648 | tf_op jit(solution)/shard_map/ppermute | solution.py:330
  178.1 20.0 %collective-permute-start.31 = (bf16[160,384]{1,0:T(8,128)(2,1)S(1)}, bf16[160,384]{1,0:T(8,128)(2,1)S(1)}, u32[]{:S(2)}, u32[]{:S(2)}) collective-permute-start(bf16[160,384]{1,0:T(8,128)(2,1)S(1)} %get-tuple-element.55), channel_id=1, source_target_pairs={{4,0},{8,4},{12,8},{14,12},{10,14},{6,10},{2,6},{0,2},{5,1},{9,5},... | collective-permute-start | bytes 368648 | tf_op jit(solution)/shard_map/ppermute | solution.py:330
  200.5 8.6 %collective-permute-start.28 = (bf16[320,384]{1,0:T(8,128)(2,1)S(1)}, bf16[320,384]{1,0:T(8,128)(2,1)S(1)}, u32[]{:S(2)}, u32[]{:S(2)}) collective-permute-start(bf16[320,384]{1,0:T(8,128)(2,1)S(1)} %pad_maximum_fusion.4), channel_id=1, source_target_pairs={{0,4},{4,8},{8,12},{12,14},{14,10},{10,6},{6,2},{2,0},{1,5},{5,9},... | collective-permute-start | bytes 737288 | tf_op jit(solution)/shard_map/ppermute | solution.py:330
  205.3 9.1 %collective-permute-start.21 = (bf16[320,384]{1,0:T(8,128)(2,1)S(1)}, bf16[320,384]{1,0:T(8,128)(2,1)S(1)}, u32[]{:S(2)}, u32[]{:S(2)}) collective-permute-start(bf16[320,384]{1,0:T(8,128)(2,1)S(1)} %fusion.19), channel_id=1, source_target_pairs={{0,4},{4,8},{8,12},{12,14},{14,10},{10,6},{6,2},{2,0},{1,5},{5,9},... | collective-permute-start | bytes 737288 | tf_op jit(solution)/shard_map/ppermute | solution.py:330
  214.6 8.9 %collective-permute-start.25 = (bf16[320,384]{1,0:T(8,128)(2,1)S(1)}, bf16[320,384]{1,0:T(8,128)(2,1)S(1)}, u32[]{:S(2)}, u32[]{:S(2)}) collective-permute-start(bf16[320,384]{1,0:T(8,128)(2,1)S(1)} %get-tuple-element.42), channel_id=1, source_target_pairs={{4,0},{8,4},{12,8},{14,12},{10,14},{6,10},{2,6},{0,2},{5,1},{9,5},... | collective-permute-start | bytes 737288 | tf_op jit(solution)/shard_map/ppermute | solution.py:330
  215.0 8.6 %collective-permute-start.29 = (bf16[320,384]{1,0:T(8,128)(2,1)S(1)}, bf16[320,384]{1,0:T(8,128)(2,1)S(1)}, u32[]{:S(2)}, u32[]{:S(2)}) collective-permute-start(bf16[320,384]{1,0:T(8,128)(2,1)S(1)} %get-tuple-element.41), channel_id=1, source_target_pairs={{0,4},{4,8},{8,12},{12,14},{14,10},{10,6},{6,2},{2,0},{1,5},{5,9},... | collective-permute-start | bytes 737288 | tf_op jit(solution)/shard_map/ppermute | solution.py:330
  216.7 9.7 %collective-permute-start.33 = (bf16[320,384]{1,0:T(8,128)(2,1)S(1)}, bf16[320,384]{1,0:T(8,128)(2,1)S(1)}, u32[]{:S(2)}, u32[]{:S(2)}) collective-permute-start(bf16[320,384]{1,0:T(8,128)(2,1)S(1)} %get-tuple-element.40), channel_id=1, source_target_pairs={{4,0},{8,4},{12,8},{14,12},{10,14},{6,10},{2,6},{0,2},{5,1},{9,5},... | collective-permute-start | bytes 737288 | tf_op jit(solution)/shard_map/ppermute | solution.py:330
  217.8 12.8 %collective-permute-start.22 = (bf16[320,384]{1,0:T(8,128)(2,1)S(1)}, bf16[320,384]{1,0:T(8,128)(2,1)S(1)}, u32[]{:S(2)}, u32[]{:S(2)}) collective-permute-start(bf16[320,384]{1,0:T(8,128)(2,1)S(1)} %get-tuple-element.39), channel_id=1, source_target_pairs={{0,4},{4,8},{8,12},{12,14},{14,10},{10,6},{6,2},{2,0},{1,5},{5,9},... | collective-permute-start | bytes 737288 | tf_op jit(solution)/shard_map/ppermute | solution.py:330
  (31 other events, 462.3 us)

commit v2 on v1

--- a/solution.py
+++ b/solution.py
@@ -181,7 +181,7 @@
                 acc_out[...] += part
 
 
-def first_call(idx, xs, hot, cols, mod, weight, acc):
+def first_call(idx, base, xs, hot, cols, mod, weight, acc):
     blocks = len(xs)
     rows, feat = xs[0].shape
     hidden = weight.shape[1]
@@ -191,8 +191,8 @@
     in_specs = [pl.BlockSpec((rows, feat), lambda i, s: (0, 0))] * blocks + [
         pl.BlockSpec((rows, 128), lambda i, s: (0, 0)),
         pl.BlockSpec((rows, 128), lambda i, s: (0, 0)),
-        pl.BlockSpec((3, reqs, feat), lambda i, s: (0, 0, s[i])),
-        pl.BlockSpec((feat, hidden), lambda i, s: (s[i], 0)),
+        pl.BlockSpec((3, reqs, feat), lambda i, s: (0, 0, s[base + i])),
+        pl.BlockSpec((feat, hidden), lambda i, s: (s[base + i], 0)),
     ]
     args = list(xs) + [hot, cols, mod, weight]
     if not fresh:
@@ -237,7 +237,7 @@
     part_out[...] = jnp.dot(act, w2_ref[...], preferred_element_type=F32).astype(BF)
 
 
-def finish_call(idx, ids, owned, x, hot, cols, mod, weight, acc, wide, bias, up, recv, weight2, tiles):
+def finish_call(idx, base, ids, owned, x, hot, cols, mod, weight, acc, wide, bias, up, recv, weight2, tiles):
     rows, feat = x.shape
     tile = rows // tiles
     hidden = weight.shape[1]
@@ -252,14 +252,14 @@
                 tiled(feat),
                 tiled(128),
                 tiled(128),
-                pl.BlockSpec((3, reqs, feat), lambda i, *s: (0, 0, s[0][0])),
-                pl.BlockSpec((feat, hidden), lambda i, *s: (s[0][0], 0)),
+                pl.BlockSpec((3, reqs, feat), lambda i, *s: (0, 0, s[0][base])),
+                pl.BlockSpec((feat, hidden), lambda i, *s: (s[0][base], 0)),
                 tiled(hidden),
                 tiled(reqs * rank),
                 pl.BlockSpec((1, hidden), lambda i, *s: (0, 0)),
                 ANY,
                 ANY,
-                pl.BlockSpec((hidden, feat), lambda i, *s: (0, s[0][0])),
+                pl.BlockSpec((hidden, feat), lambda i, *s: (0, s[0][base])),
             ],
             out_specs=[tiled(hidden), tiled(feat)],
             scratch_shapes=[
@@ -283,8 +283,7 @@
     out_ref[0] = jnp.dot(act_ref[...], w_ref[...], preferred_element_type=F32)
 
 
-def second_call(idx, act, weight2, feat):
-    blocks = idx.shape[0]
+def second_call(idx, base, blocks, act, weight2, feat):
     rows, hidden = act.shape
     return pl.pallas_call(
         second_kernel,
@@ -293,7 +292,7 @@
             grid=(blocks,),
             in_specs=[
                 pl.BlockSpec((rows, hidden), lambda i, s: (0, 0)),
-                pl.BlockSpec((hidden, feat), lambda i, s: (0, s[i])),
+                pl.BlockSpec((hidden, feat), lambda i, s: (0, s[base - i])),
             ],
             out_specs=pl.BlockSpec((1, rows, feat), lambda i, s: (i, 0, 0)),
         ),
@@ -318,14 +317,11 @@
     forth = [(order[i], order[(i + 1) % count]) for i in range(count)]
     back = [(b, a) for a, b in forth]
     table = [[0] * count for _ in range(count)]
+    half = count // 2
+    visits = [0] + [s for k in range(1, half) for s in (-k, k)] + [half]
     for at, dev in enumerate(order):
-        table[dev] = [order[(at + k) % count] for k in range(count)]
+        table[dev] = [order[(at + k) % count] for k in visits]
     mine = lax.dynamic_index_in_dim(jnp.array(table, jnp.int32), me, 0, keepdims=False)
-    half = count // 2
-
-    def at(*steps):
-        return jnp.stack([mine[k % count] for k in steps])
-
     def go(x, route):
         return lax.ppermute(x, "tensor", route)
 
@@ -341,12 +337,13 @@
     send_down, send_up = pl.pallas_call(
         send_kernel,
         in_specs=[SMEM, ANY, ANY],
-        out_specs=[ANY, ANY],
+        out_specs=[WHOLE, WHOLE],
         out_shape=[
             jax.ShapeDtypeStruct((reqs, rank, feat), BF),
             jax.ShapeDtypeStruct((reqs, rank, hidden), BF),
         ],
         scratch_shapes=[pltpu.SemaphoreType.DMA((2 * reqs,))],
+        compiler_params=params(),
         cost_estimate=cost(0, 4 * reqs * rank * (feat + hidden)),
         name="adapters_to_send",
     )(their_ids, down, adapter_up_matrices)
@@ -415,19 +412,23 @@
     acc = None
     early = 2 * half - 3
     groups = [seen[:early], seen[early:]] if half > 2 else [seen]
+    base = 0
     for group in groups:
         acc = first_call(
-            at(*[k for k, _ in group]), [x for _, x in group], hot, cols, mod, first_weight, acc
+            mine, base, [x for _, x in group], hot, cols, mod, first_weight, acc
         )
+        base += len(group)
     act, far_part = finish_call(
-        at(half), my_ids, owned, far, hot, cols, mod, first_weight, acc, wide, bias,
+        mine, base, my_ids, owned, far, hot, cols, mod, first_weight, acc, wide, bias,
         adapter_up_matrices, recv_up, second_weight, 4,
     )
 
     steps = [s for k in range(half - 1, 0, -1) for s in (k, -k)] + [0]
     parts = {}
+    base = count - 2
     for group in (steps[:2], steps[2:]):
-        got = second_call(at(*group), act, second_weight, feat)
+        got = second_call(mine, base, len(group), act, second_weight, feat)
+        base -= len(group)
         for i, s in enumerate(group):
             parts[s] = got[i]
     gate = jnp.dot(

time: 238 us -> 176 us (0.74)
  Pallas kernels: 121 us -> 62.9 us
  local copies, waits for them, and re-layouts: 17.5 us -> 8.53 us
  starting transfers between devices: 36.4 us -> 43.1 us
  other arithmetic: 10.4 us -> 5.21 us
  waiting for transfers between devices: 50.7 us -> 54.7 us
    pallas_call x1, Pallas kernels: 61.6 us -> 4 us  [ring_device(): pl.pallas_call(send_kernel, in_specs=[SMEM, ANY, ANY], out_specs=[WHOLE,...]
    another operation x2 -> x0, local copies, waits for them, and re-layouts: 7.65 us -> none  [at(): return jnp.stack([mine[k % count] for k in steps])]
    ppermute x33, starting transfers between devices: 35.8 us -> 42.5 us  [go(): return lax.ppermute(x, 'tensor', route)]
    another operation x5 -> x3, other arithmetic: 5.81 us -> 0.54 us  [the longest x2 3.7 us: at(): return jnp.stack([mine[k % count] for k in steps])]
    ppermute x33, waiting for transfers between devices: 50.7 us -> 54.7 us  [go(): return lax.ppermute(x, 'tensor', route)]
  transfers between devices with their start and end apart: 35 -> 35, of which waited for: 15 -> 22; matrix products, arithmetic and copies ran while one was open for 9% -> 5% of each run, Pallas kernels for 46% -> 21%
where the time goes in v2:
time: 176 us; the launch traced here: 175 us
  Pallas kernels  62.9 us (36%)
  waiting for transfers between devices  54.7 us (31%)
  starting transfers between devices  43.1 us (24%)
  local copies, waits for them, and re-layouts  8.53 us (5%)
  other arithmetic  5.21 us (3%)
    ppermute x33, waiting for transfers between devices, go(): return lax.ppermute(x, 'tensor', route)  54.7 us
    ppermute x33, starting transfers between devices, go(): return lax.ppermute(x, 'tensor', route)  42.5 us
    pallas_call x2, Pallas kernels, first_call(): pl.pallas_call(functools.partial(first_kernel, blocks, reqs, fresh), grid...  20.9 us
    pallas_call x2, Pallas kernels, second_call(): pl.pallas_call(second_kernel, grid_spec=pltpu.PrefetchScalarGridSpec(num_...  16.5 us
    pallas_call x1, Pallas kernels, finish_call(): pl.pallas_call(functools.partial(finish_kernel, reqs), grid_spec=pltpu.Pr...  10.5 us
    pallas_call x3, Pallas kernels, ring_device(): pl.pallas_call(kernel, in_specs=[WHOLE] * 7, out_specs=[WHOLE] * len(shap...  7.63 us
    unnamed x44, local copies, waits for them, and re-layouts  4.39 us
    pallas_call x1, Pallas kernels, ring_device(): pl.pallas_call(send_kernel, in_specs=[SMEM, ANY, ANY], out_specs=[WHOLE,...  4 us
  transfers between devices with their start and end apart: 35, of which 22 were waited for; matrix products, arithmetic and copies ran while one was open for 5% of the time, Pallas kernels for 21%

profile of v2, /device:TPU:0, one launch (start us, length us, event | category | flops | bytes accessed | tf_op | source)
XLA Modules:
  0.0 174.9 jit_solution(18104970570005452261)
XLA Ops:
  0.0 3.0 %collective-permute-start.1 = (bf16[640,384]{1,0:T(8,128)(2,1)}, bf16[640,384]{1,0:T(8,128)(2,1)S(1)}, u32[]{:S(2)}, u32[]{:S(2)}) collective-permute-start(bf16[640,384]{1,0:T(8,128)(2,1)} %refs_0_.1), channel_id=1, source_target_pairs={{0,4},{4,8},{8,12},{12,14},{14,10},{10,6},{6,2},{2,0},{1,5},{5,9},... | collective-permute-start | bytes 1474568 | tf_op jit(solution)/shard_map/ppermute | solution.py:326
  3.0 11.3 %collective-permute-done.1.refs_1_ = bf16[640,384]{1,0:T(8,128)(2,1)S(1)} collective-permute-done((bf16[640,384]{1,0:T(8,128)(2,1)}, bf16[640,384]{1,0:T(8,128)(2,1)S(1)}, u32[]{:S(2)}, u32[]{:S(2)}) %collective-permute-start.1) | collective-permute-done | bytes 491552 | tf_op jit(solution)/shard_map/ppermute | solution.py:326
  17.7 4.0 %adapters_to_send.1 = (bf16[8,64,384]{2,1,0:T(8,128)(2,1)}, bf16[8,64,1536]{2,1,0:T(8,128)(2,1)}) custom-call(s32[8]{0:T(128)} %fusion.45.ids, bf16[128,64,384]{2,1,0:T(8,128)(2,1)} %bitcast.130, bf16[128,64,1536]{2,1,0:T(8,128)(2,1)} %up_ref.3), custom_call_target="tpu_custom_call" | custom-call | bytes 3932160 | tf_op jit(solution)/shard_map/adapters_to_send/pallas_call | solution.py:337
  22.9 4.0 %collective-permute-done.2.refs_3_ = bf16[640,384]{1,0:T(8,128)(2,1)} collective-permute-done((bf16[640,384]{1,0:T(8,128)(2,1)S(1)}, bf16[640,384]{1,0:T(8,128)(2,1)}, u32[]{:S(2)}, u32[]{:S(2)}) %collective-permute-start.2) | collective-permute-done | bytes 491552 | tf_op jit(solution)/shard_map/ppermute | solution.py:326
  30.8 3.3 %own_features.1 = (bf16[64,640]{1,0:T(8,128)(2,1)}, f32[8,640]{1,0:T(8,128)}, f32[64,128]{1,0:T(8,128)}, bf16[640,128]{1,0:T(8,128)(2,1)}) custom-call(s32[8]{0:T(128)} %subtract_clamp_fusion.ids, s32[8]{0:T(128)} %compare_convert_fusion.owned, s32[8]{0:T(128)} %bitcast.136, bf16[640,384]{1,0:T(8,128)(2,1)} %refs_0_.1, ...), custom_call_target="tpu_custom_call" | custom-call | flops 251658240 | bytes 983040 | tf_op jit(solution)/shard_map/own_features/pallas_call | solution.py:355
  36.3 4.5 %collective-permute-done.10.refs_4_ = f32[8,640]{1,0:T(8,128)S(1)} collective-permute-done((f32[8,640]{1,0:T(8,128)}, f32[8,640]{1,0:T(8,128)S(1)}, u32[]{:S(2)}, u32[]{:S(2)}) %collective-permute-start.10) | collective-permute-done | bytes 20512 | tf_op jit(solution)/shard_map/ppermute | solution.py:326
  42.5 2.4 %collective-permute-done.11.refs_5_ = f32[64,128]{1,0:T(8,128)S(1)} collective-permute-done((f32[64,128]{1,0:T(8,128)}, f32[64,128]{1,0:T(8,128)S(1)}, u32[]{:S(2)}, u32[]{:S(2)}) %collective-permute-start.11) | collective-permute-done | bytes 32800 | tf_op jit(solution)/shard_map/ppermute | solution.py:326
  45.5 2.2 %merge_sums.3 = (bf16[64,640]{1,0:T(8,128)(2,1)}, f32[8,640]{1,0:T(8,128)}, f32[64,128]{1,0:T(8,128)}) custom-call(bf16[64,640]{1,0:T(8,128)(2,1)} %get-tuple-element.23.refs_0_, f32[8,640]{1,0:T(8,128)} %get-tuple-element.24.refs_1_, f32[64,128]{1,0:T(8,128)} %get-tuple-element.25.refs_2_, bf16[64,640]{1,0:T(8,128)(2,1)} %copy-done.10, ...), custom_call_target="tpu_custom_call" | custom-call | flops 62914560 | bytes 327680 | tf_op jit(solution)/shard_map/merge_sums/pallas_call | solution.py:388
  49.8 2.8 %collective-permute-done.13.refs_4_ = f32[8,640]{1,0:T(8,128)S(1)} collective-permute-done((f32[8,640]{1,0:T(8,128)}, f32[8,640]{1,0:T(8,128)S(1)}, u32[]{:S(2)}, u32[]{:S(2)}) %collective-permute-start.13) | collective-permute-done | bytes 20512 | tf_op jit(solution)/shard_map/ppermute | solution.py:326
  53.8 3.0 %collective-permute-done.14.refs_5_ = f32[64,128]{1,0:T(8,128)S(1)} collective-permute-done((f32[64,128]{1,0:T(8,128)}, f32[64,128]{1,0:T(8,128)S(1)}, u32[]{:S(2)}, u32[]{:S(2)}) %collective-permute-start.14) | collective-permute-done | bytes 32800 | tf_op jit(solution)/shard_map/ppermute | solution.py:326
  60.2 4.4 %collective-permute-start.16 = (f32[8,640]{1,0:T(8,128)}, f32[8,640]{1,0:T(8,128)S(1)}, u32[]{:S(2)}, u32[]{:S(2)}) collective-permute-start(f32[8,640]{1,0:T(8,128)} %get-tuple-element.30.refs_1_), channel_id=1, source_target_pairs={{0,8},{2,10},{4,12},{6,14},{8,0},{10,2},{12,4},{14,6},{1,9},{3,11}... | collective-permute-start | bytes 61448 | tf_op jit(solution)/shard_map/ppermute | solution.py:326
  66.6 3.0 %collective-permute-start.17 = (f32[64,128]{1,0:T(8,128)}, f32[64,128]{1,0:T(8,128)S(1)}, u32[]{:S(2)}, u32[]{:S(2)}) collective-permute-start(f32[64,128]{1,0:T(8,128)} %get-tuple-element.31.refs_2_), channel_id=1, source_target_pairs={{0,8},{2,10},{4,12},{6,14},{8,0},{10,2},{12,4},{14,6},{1,9},{3,11}... | collective-permute-start | bytes 98312 | tf_op jit(solution)/shard_map/ppermute | solution.py:326
  73.4 3.2 %merge_sums.5 = (bf16[640,512]{1,0:T(8,128)(2,1)}, f32[640,128]{1,0:T(8,128)}) custom-call(bf16[64,640]{1,0:T(8,128)(2,1)} %get-tuple-element.29.refs_0_, f32[8,640]{1,0:T(8,128)} %get-tuple-element.30.refs_1_, f32[64,128]{1,0:T(8,128)} %get-tuple-element.31.refs_2_, bf16[64,640]{1,0:T(8,128)(2,1)} %copy-done.12, f32[8,640]{1,0:T(8,128)} %copy-done.16, ...), custom_call_target="tpu_custom_call" | custom-call | flops 62914560 | bytes 327680 | tf_op jit(solution)/shard_map/merge_sums/pallas_call | solution.py:388
  79.0 12.4 %first_blocks.2.refs_6_ = f32[640,1536]{1,0:T(8,128)} custom-call(s32[8]{0:T(128)} %fusion.44.idx, bf16[640,384]{1,0:T(8,128)(2,1)} %refs_0_.1, bf16[640,384]{1,0:T(8,128)(2,1)} %copy-done.7, bf16[640,384]{1,0:T(8,128)(2,1)} %copy-done.8, bf16[640,384]{1,0:T(8,128)(2,1)} %collective-permute-done.2.refs_3_, bf16[640,384]{1,0:T(8,128)(2,1)} %collective-permute-done.6.refs_4_, ...), custom_call_target="tpu_custom_call" | custom-call | flops 3774873600 | bytes 10616832 | tf_op jit(solution)/shard_map/first_blocks/pallas_call | solution.py:201
  91.4 8.5 %first_blocks.3.acc_ref = f32[640,1536]{1,0:T(8,128)} custom-call(s32[8]{0:T(128)} %fusion.44.idx, bf16[640,384]{1,0:T(8,128)(2,1)} %copy-done.5, bf16[640,384]{1,0:T(8,128)(2,1)} %copy-done.6, bf16[640,128]{1,0:T(8,128)(2,1)} %get-tuple-element.22.refs_6_.refs_5_.refs_2_.hot_ref, f32[640,128]{1,0:T(8,128)} %get-tuple-element.32.refs_6_.refs_3_.col_ref, ...), custom_call_target="tpu_custom_call" | custom-call | flops 1509949440 | bytes 7077888 | tf_op jit(solution)/shard_map/first_blocks/pallas_call | solution.py:201
  102.0 10.5 %finish_first.1 = (bf16[640,1536]{1,0:T(8,128)(2,1)}, bf16[640,384]{1,0:T(8,128)(2,1)}) custom-call(s32[8]{0:T(128)} %fusion.44.idx, s32[8]{0:T(128)} %subtract_clamp_fusion.ids, s32[8]{0:T(128)} %compare_convert_fusion.owned, bf16[640,384]{1,0:T(8,128)(2,1)} %pad_maximum_fusion.x_ref, bf16[640,128]{1,0:T(8,128)(2,1)} %get-tuple-element.22.refs_6_.refs_5_.refs_2_.hot_ref, ...), custom_call_target="tpu_custom_call" | custom-call | flops 2516582400 | bytes 13762560 | tf_op jit(solution)/shard_map/finish_first/pallas_call | solution.py:246
  112.5 6.0 %second_blocks.3 = f32[2,640,384]{2,1,0:T(8,128)} custom-call(s32[8]{0:T(128)} %fusion.44.idx, bf16[640,1536]{1,0:T(8,128)(2,1)} %get-tuple-element.35.act_ref, bf16[1536,3072]{1,0:T(8,128)(2,1)} %w_ref.5), custom_call_target="tpu_custom_call" | custom-call | flops 1509949440 | bytes 3932160 | tf_op jit(solution)/shard_map/second_blocks/pallas_call | solution.py:288
  118.4 10.6 %second_blocks.2 = f32[5,640,384]{2,1,0:T(8,128)} custom-call(s32[8]{0:T(128)} %fusion.44.idx, bf16[640,1536]{1,0:T(8,128)(2,1)} %get-tuple-element.35.act_ref, bf16[1536,3072]{1,0:T(8,128)(2,1)} %w_ref.5), custom_call_target="tpu_custom_call" | custom-call | flops 3774873600 | bytes 9830400 | tf_op jit(solution)/shard_map/second_blocks/pallas_call | solution.py:288
  142.7 3.6 %collective-permute-done.20 = bf16[320,384]{1,0:T(8,128)(2,1)S(1)} collective-permute-done((bf16[320,384]{1,0:T(8,128)(2,1)S(1)}, bf16[320,384]{1,0:T(8,128)(2,1)S(1)}, u32[]{:S(2)}, u32[]{:S(2)}) %collective-permute-start.20) | collective-permute-done | bytes 245792 | tf_op jit(solution)/shard_map/ppermute | solution.py:326
  148.7 2.9 %collective-permute-done.28 = bf16[320,384]{1,0:T(8,128)(2,1)S(1)} collective-permute-done((bf16[320,384]{1,0:T(8,128)(2,1)S(1)}, bf16[320,384]{1,0:T(8,128)(2,1)S(1)}, u32[]{:S(2)}, u32[]{:S(2)}) %collective-permute-start.28) | collective-permute-done | bytes 245792 | tf_op jit(solution)/shard_map/ppermute | solution.py:326
  152.5 2.6 %collective-permute-done.21 = bf16[320,384]{1,0:T(8,128)(2,1)S(1)} collective-permute-done((bf16[320,384]{1,0:T(8,128)(2,1)S(1)}, bf16[320,384]{1,0:T(8,128)(2,1)S(1)}, u32[]{:S(2)}, u32[]{:S(2)}) %collective-permute-start.21) | collective-permute-done | bytes 245792 | tf_op jit(solution)/shard_map/ppermute | solution.py:326
  158.5 2.3 %collective-permute-start.22 = (bf16[320,384]{1,0:T(8,128)(2,1)S(1)}, bf16[320,384]{1,0:T(8,128)(2,1)S(1)}, u32[]{:S(2)}, u32[]{:S(2)}) collective-permute-start(bf16[320,384]{1,0:T(8,128)(2,1)S(1)} %get-tuple-element.39), channel_id=1, source_target_pairs={{0,4},{4,8},{8,12},{12,14},{14,10},{10,6},{6,2},{2,0},{1,5},{5,9},... | collective-permute-start | bytes 737288 | tf_op jit(solution)/shard_map/ppermute | solution.py:326
  161.9 2.6 %collective-permute-done.33 = bf16[320,384]{1,0:T(8,128)(2,1)S(1)} collective-permute-done((bf16[320,384]{1,0:T(8,128)(2,1)S(1)}, bf16[320,384]{1,0:T(8,128)(2,1)S(1)}, u32[]{:S(2)}, u32[]{:S(2)}) %collective-permute-start.33) | collective-permute-done | bytes 245792 | tf_op jit(solution)/shard_map/ppermute | solution.py:326
  168.7 2.4 %collective-permute-done.26 = bf16[320,384]{1,0:T(8,128)(2,1)S(1)} collective-permute-done((bf16[320,384]{1,0:T(8,128)(2,1)S(1)}, bf16[320,384]{1,0:T(8,128)(2,1)S(1)}, u32[]{:S(2)}, u32[]{:S(2)}) %collective-permute-start.26) | collective-permute-done | bytes 245792 | tf_op jit(solution)/shard_map/ppermute | solution.py:326
  (125 shorter events, 59.0 us)
Async XLA Ops:
  0.0 14.4 %collective-permute-start.1 = (bf16[640,384]{1,0:T(8,128)(2,1)}, bf16[640,384]{1,0:T(8,128)(2,1)S(1)}, u32[]{:S(2)}, u32[]{:S(2)}) collective-permute-start(bf16[640,384]{1,0:T(8,128)(2,1)} %refs_0_.1), channel_id=1, source_target_pairs={{0,4},{4,8},{8,12},{12,14},{14,10},{10,6},{6,2},{2,0},{1,5},{5,9},... | collective-permute-start | bytes 1474568 | tf_op jit(solution)/shard_map/ppermute | solution.py:326
  3.0 13.2 %collective-permute-start.5 = (bf16[640,384]{1,0:T(8,128)(2,1)}, bf16[640,384]{1,0:T(8,128)(2,1)S(1)}, u32[]{:S(2)}, u32[]{:S(2)}) collective-permute-start(bf16[640,384]{1,0:T(8,128)(2,1)} %refs_0_.1), channel_id=1, source_target_pairs={{4,0},{8,4},{12,8},{14,12},{10,14},{6,10},{2,6},{0,2},{5,1},{9,5},... | collective-permute-start | bytes 1474568 | tf_op jit(solution)/shard_map/ppermute | solution.py:326
  14.4 12.5 %collective-permute-start.2 = (bf16[640,384]{1,0:T(8,128)(2,1)S(1)}, bf16[640,384]{1,0:T(8,128)(2,1)}, u32[]{:S(2)}, u32[]{:S(2)}) collective-permute-start(bf16[640,384]{1,0:T(8,128)(2,1)S(1)} %collective-permute-done.1.refs_1_), channel_id=1, source_target_pairs={{0,4},{4,8},{8,12},{12,14},{14,10},{10,6},{6,2},{2,0},{1,5},{5,9},... | collective-permute-start | bytes 1474568 | tf_op jit(solution)/shard_map/ppermute | solution.py:326
  16.2 12.2 %collective-permute-start.6 = (bf16[640,384]{1,0:T(8,128)(2,1)S(1)}, bf16[640,384]{1,0:T(8,128)(2,1)}, u32[]{:S(2)}, u32[]{:S(2)}) collective-permute-start(bf16[640,384]{1,0:T(8,128)(2,1)S(1)} %collective-permute-done.5.refs_2_), channel_id=1, source_target_pairs={{4,0},{8,4},{12,8},{14,12},{10,14},{6,10},{2,6},{0,2},{5,1},{9,5},... | collective-permute-start | bytes 1474568 | tf_op jit(solution)/shard_map/ppermute | solution.py:326
  21.7 79.0 %collective-permute-start.18 = (bf16[8,64,1536]{2,1,0:T(8,128)(2,1)}, bf16[8,64,1536]{2,1,0:T(8,128)(2,1)S(1)}, u32[]{:S(2)}, u32[]{:S(2)}) collective-permute-start(bf16[8,64,1536]{2,1,0:T(8,128)(2,1)} %get-tuple-element.34), channel_id=1, source_target_pairs={{0,1},{1,0},{2,3},{3,2},{4,5},{5,4},{6,7},{7,6},{8,9},{9,8},{10,11... | collective-permute-start | bytes 4718600 | tf_op jit(solution)/shard_map/ppermute | solution.py:352
  21.8 9.1 %collective-permute-start = (bf16[8,64,384]{2,1,0:T(8,128)(2,1)}, bf16[8,64,384]{2,1,0:T(8,128)(2,1)}, u32[]{:S(2)}, u32[]{:S(2)}) collective-permute-start(bf16[8,64,384]{2,1,0:T(8,128)(2,1)} %get-tuple-element.21), channel_id=1, source_target_pairs={{0,1},{1,0},{2,3},{3,2},{4,5},{5,4},{6,7},{7,6},{8,9},{9,8},{10,11... | collective-permute-start | bytes 1179656 | tf_op jit(solution)/shard_map/ppermute | solution.py:351
  26.9 49.7 %collective-permute-start.3 = (bf16[640,384]{1,0:T(8,128)(2,1)}, bf16[640,384]{1,0:T(8,128)(2,1)S(1)}, u32[]{:S(2)}, u32[]{:S(2)}) collective-permute-start(bf16[640,384]{1,0:T(8,128)(2,1)} %collective-permute-done.2.refs_3_), channel_id=1, source_target_pairs={{0,4},{4,8},{8,12},{12,14},{14,10},{10,6},{6,2},{2,0},{1,5},{5,9},... | collective-permute-start | bytes 1474568 | tf_op jit(solution)/shard_map/ppermute | solution.py:326
  28.4 48.7 %collective-permute-start.7 = (bf16[640,384]{1,0:T(8,128)(2,1)}, bf16[640,384]{1,0:T(8,128)(2,1)S(1)}, u32[]{:S(2)}, u32[]{:S(2)}) collective-permute-start(bf16[640,384]{1,0:T(8,128)(2,1)} %collective-permute-done.6.refs_4_), channel_id=1, source_target_pairs={{4,0},{8,4},{12,8},{14,12},{10,14},{6,10},{2,6},{0,2},{5,1},{9,5},... | collective-permute-start | bytes 1474568 | tf_op jit(solution)/shard_map/ppermute | solution.py:326
  34.2 10.7 %collective-permute-start.9 = (bf16[64,640]{1,0:T(8,128)(2,1)}, bf16[64,640]{1,0:T(8,128)(2,1)S(1)}, u32[]{:S(2)}, u32[]{:S(2)}) collective-permute-start(bf16[64,640]{1,0:T(8,128)(2,1)} %get-tuple-element.23.refs_0_), channel_id=1, source_target_pairs={{0,2},{2,0},{4,6},{6,4},{8,10},{10,8},{12,14},{14,12},{1,3},{3,1},... | collective-permute-start | bytes 245768 | tf_op jit(solution)/shard_map/ppermute | solution.py:326
  47.8 9.0 %collective-permute-start.12 = (bf16[64,640]{1,0:T(8,128)(2,1)}, bf16[64,640]{1,0:T(8,128)(2,1)S(1)}, u32[]{:S(2)}, u32[]{:S(2)}) collective-permute-start(bf16[64,640]{1,0:T(8,128)(2,1)} %get-tuple-element.26.refs_0_), channel_id=1, source_target_pairs={{0,4},{2,6},{4,0},{6,2},{8,12},{10,14},{12,8},{14,10},{1,5},{3,7},... | collective-permute-start | bytes 245768 | tf_op jit(solution)/shard_map/ppermute | solution.py:326
  64.6 7.6 %collective-permute-start.15 = (bf16[64,640]{1,0:T(8,128)(2,1)}, bf16[64,640]{1,0:T(8,128)(2,1)S(1)}, u32[]{:S(2)}, u32[]{:S(2)}) collective-permute-start(bf16[64,640]{1,0:T(8,128)(2,1)} %get-tuple-element.29.refs_0_), channel_id=1, source_target_pairs={{0,8},{2,10},{4,12},{6,14},{8,0},{10,2},{12,4},{14,6},{1,9},{3,11}... | collective-permute-start | bytes 245768 | tf_op jit(solution)/shard_map/ppermute | solution.py:326
  76.7 23.3 %collective-permute-start.4 = (bf16[320,384]{1,0:T(8,128)(2,1)S(1)}, bf16[320,384]{1,0:T(8,128)(2,1)S(1)}, u32[]{:S(2)}, u32[]{:S(2)}) collective-permute-start(bf16[320,384]{1,0:T(8,128)(2,1)S(1)} %slice.235), channel_id=1, source_target_pairs={{0,4},{4,8},{8,12},{12,14},{14,10},{10,6},{6,2},{2,0},{1,5},{5,9},... | collective-permute-start | bytes 737288 | tf_op jit(solution)/shard_map/ppermute | solution.py:326
  77.2 22.7 %collective-permute-start.8 = (bf16[320,384]{1,0:T(8,128)(2,1)S(1)}, bf16[320,384]{1,0:T(8,128)(2,1)S(1)}, u32[]{:S(2)}, u32[]{:S(2)}) collective-permute-start(bf16[320,384]{1,0:T(8,128)(2,1)S(1)} %slice.236), channel_id=1, source_target_pairs={{4,0},{8,4},{12,8},{14,12},{10,14},{6,10},{2,6},{0,2},{5,1},{9,5},... | collective-permute-start | bytes 737288 | tf_op jit(solution)/shard_map/ppermute | solution.py:326
  131.1 6.9 %collective-permute-start.27 = (bf16[160,384]{1,0:T(8,128)(2,1)S(1)}, bf16[160,384]{1,0:T(8,128)(2,1)S(1)}, u32[]{:S(2)}, u32[]{:S(2)}) collective-permute-start(bf16[160,384]{1,0:T(8,128)(2,1)S(1)} %get-tuple-element.56), channel_id=1, source_target_pairs={{0,4},{4,8},{8,12},{12,14},{14,10},{10,6},{6,2},{2,0},{1,5},{5,9},... | collective-permute-start | bytes 368648 | tf_op jit(solution)/shard_map/ppermute | solution.py:326
  138.3 8.0 %collective-permute-start.20 = (bf16[320,384]{1,0:T(8,128)(2,1)S(1)}, bf16[320,384]{1,0:T(8,128)(2,1)S(1)}, u32[]{:S(2)}, u32[]{:S(2)}) collective-permute-start(bf16[320,384]{1,0:T(8,128)(2,1)S(1)} %pad_maximum_fusion.2), channel_id=1, source_target_pairs={{0,4},{4,8},{8,12},{12,14},{14,10},{10,6},{6,2},{2,0},{1,5},{5,9},... | collective-permute-start | bytes 737288 | tf_op jit(solution)/shard_map/ppermute | solution.py:326
  139.7 8.9 %collective-permute-start.24 = (bf16[320,384]{1,0:T(8,128)(2,1)S(1)}, bf16[320,384]{1,0:T(8,128)(2,1)S(1)}, u32[]{:S(2)}, u32[]{:S(2)}) collective-permute-start(bf16[320,384]{1,0:T(8,128)(2,1)S(1)} %pad_maximum_fusion.3), channel_id=1, source_target_pairs={{4,0},{8,4},{12,8},{14,12},{10,14},{6,10},{2,6},{0,2},{5,1},{9,5},... | collective-permute-start | bytes 737288 | tf_op jit(solution)/shard_map/ppermute | solution.py:326
  140.5 11.1 %collective-permute-start.28 = (bf16[320,384]{1,0:T(8,128)(2,1)S(1)}, bf16[320,384]{1,0:T(8,128)(2,1)S(1)}, u32[]{:S(2)}, u32[]{:S(2)}) collective-permute-start(bf16[320,384]{1,0:T(8,128)(2,1)S(1)} %pad_maximum_fusion.4), channel_id=1, source_target_pairs={{0,4},{4,8},{8,12},{12,14},{14,10},{10,6},{6,2},{2,0},{1,5},{5,9},... | collective-permute-start | bytes 737288 | tf_op jit(solution)/shard_map/ppermute | solution.py:326
  141.9 10.6 %collective-permute-start.32 = (bf16[320,384]{1,0:T(8,128)(2,1)S(1)}, bf16[320,384]{1,0:T(8,128)(2,1)S(1)}, u32[]{:S(2)}, u32[]{:S(2)}) collective-permute-start(bf16[320,384]{1,0:T(8,128)(2,1)S(1)} %pad_maximum_fusion.5), channel_id=1, source_target_pairs={{4,0},{8,4},{12,8},{14,12},{10,14},{6,10},{2,6},{0,2},{5,1},{9,5},... | collective-permute-start | bytes 737288 | tf_op jit(solution)/shard_map/ppermute | solution.py:326
  146.4 8.7 %collective-permute-start.21 = (bf16[320,384]{1,0:T(8,128)(2,1)S(1)}, bf16[320,384]{1,0:T(8,128)(2,1)S(1)}, u32[]{:S(2)}, u32[]{:S(2)}) collective-permute-start(bf16[320,384]{1,0:T(8,128)(2,1)S(1)} %fusion.19), channel_id=1, source_target_pairs={{0,4},{4,8},{8,12},{12,14},{14,10},{10,6},{6,2},{2,0},{1,5},{5,9},... | collective-permute-start | bytes 737288 | tf_op jit(solution)/shard_map/ppermute | solution.py:326
  155.3 6.5 %collective-permute-start.25 = (bf16[320,384]{1,0:T(8,128)(2,1)S(1)}, bf16[320,384]{1,0:T(8,128)(2,1)S(1)}, u32[]{:S(2)}, u32[]{:S(2)}) collective-permute-start(bf16[320,384]{1,0:T(8,128)(2,1)S(1)} %get-tuple-element.42), channel_id=1, source_target_pairs={{4,0},{8,4},{12,8},{14,12},{10,14},{6,10},{2,6},{0,2},{5,1},{9,5},... | collective-permute-start | bytes 737288 | tf_op jit(solution)/shard_map/ppermute | solution.py:326
  157.5 7.0 %collective-permute-start.33 = (bf16[320,384]{1,0:T(8,128)(2,1)S(1)}, bf16[320,384]{1,0:T(8,128)(2,1)S(1)}, u32[]{:S(2)}, u32[]{:S(2)}) collective-permute-start(bf16[320,384]{1,0:T(8,128)(2,1)S(1)} %get-tuple-element.40), channel_id=1, source_target_pairs={{4,0},{8,4},{12,8},{14,12},{10,14},{6,10},{2,6},{0,2},{5,1},{9,5},... | collective-permute-start | bytes 737288 | tf_op jit(solution)/shard_map/ppermute | solution.py:326
  158.5 10.2 %collective-permute-start.22 = (bf16[320,384]{1,0:T(8,128)(2,1)S(1)}, bf16[320,384]{1,0:T(8,128)(2,1)S(1)}, u32[]{:S(2)}, u32[]{:S(2)}) collective-permute-start(bf16[320,384]{1,0:T(8,128)(2,1)S(1)} %get-tuple-element.39), channel_id=1, source_target_pairs={{0,4},{4,8},{8,12},{12,14},{14,10},{10,6},{6,2},{2,0},{1,5},{5,9},... | collective-permute-start | bytes 737288 | tf_op jit(solution)/shard_map/ppermute | solution.py:326
  164.7 6.4 %collective-permute-start.26 = (bf16[320,384]{1,0:T(8,128)(2,1)S(1)}, bf16[320,384]{1,0:T(8,128)(2,1)S(1)}, u32[]{:S(2)}, u32[]{:S(2)}) collective-permute-start(bf16[320,384]{1,0:T(8,128)(2,1)S(1)} %get-tuple-element.43), channel_id=1, source_target_pairs={{4,0},{8,4},{12,8},{14,12},{10,14},{6,10},{2,6},{0,2},{5,1},{9,5},... | collective-permute-start | bytes 737288 | tf_op jit(solution)/shard_map/ppermute | solution.py:326
  167.0 6.7 %collective-permute-start.34 = (bf16[320,384]{1,0:T(8,128)(2,1)S(1)}, bf16[320,384]{1,0:T(8,128)(2,1)S(1)}, u32[]{:S(2)}, u32[]{:S(2)}) collective-permute-start(bf16[320,384]{1,0:T(8,128)(2,1)S(1)} %get-tuple-element.44), channel_id=1, source_target_pairs={{4,0},{8,4},{12,8},{14,12},{10,14},{6,10},{2,6},{0,2},{5,1},{9,5},... | collective-permute-start | bytes 737288 | tf_op jit(solution)/shard_map/ppermute | solution.py:326
  (33 other events, 305.9 us)

commit v3 on v0

--- a/solution.py
+++ b/solution.py
@@ -1,7 +1,560 @@
+import functools
+
 import jax
 import jax.numpy as jnp
 from jax import lax
+from jax.experimental import pallas as pl
+from jax.experimental.pallas import tpu as pltpu
 from jax.sharding import PartitionSpec as P
+
+BF = jnp.bfloat16
+F32 = jnp.float32
+VMEM_LIMIT = 24 * 1024 * 1024
+HIGH = lax.Precision.HIGHEST
+ANY = pl.BlockSpec(memory_space=pltpu.HBM)
+SMEM = pl.BlockSpec(memory_space=pltpu.SMEM)
+WHOLE = pl.BlockSpec(memory_space=pltpu.VMEM)
+
+
+def params(**more):
+    return pltpu.CompilerParams(vmem_limit_bytes=VMEM_LIMIT, **more)
+
+
+def cost(flops, nbytes, trans=0):
+    return pl.CostEstimate(
+        flops=int(flops), bytes_accessed=int(nbytes), transcendentals=int(trans)
+    )
+
+
+def ring_order(count):
+    cols = 2 if count < 32 else 4
+    rows = count // cols
+    walk = [r * cols for r in range(rows)]
+    for i, r in enumerate(reversed(range(rows))):
+        across = list(range(1, cols))
+        walk += [r * cols + c for c in (across if i % 2 == 0 else across[::-1])]
+    return walk
+
+
+def blocks_in(ref, width, at, axis):
+    place = pl.ds(pl.multiple_of(at * width, width), width)
+    return ref.at[place, :] if axis == 0 else ref.at[:, place]
+
+
+def send_kernel(count, ints, down_ref, up_ref, down_out, up_out, sem):
+    reqs = down_out.shape[0]
+    copies = []
+    for r in range(reqs):
+        at = ints[count + reqs + r]
+        copies.append(pltpu.make_async_copy(down_ref.at[at], down_out.at[r], sem.at[2 * r]))
+        copies.append(pltpu.make_async_copy(up_ref.at[at], up_out.at[r], sem.at[2 * r + 1]))
+    for c in copies:
+        c.start()
+    for c in copies:
+        c.wait()
+
+
+def fetch_adapters(count, ints, store_ref, recv_ref, dst, sem, wait):
+    reqs, rank = recv_ref.shape[:2]
+    for r in range(reqs):
+        here = dst.at[pl.ds(r * rank, rank)]
+        if wait:
+            pltpu.make_async_copy(recv_ref.at[r], here, sem.at[r]).wait()
+            continue
+        own = ints[count + 2 * reqs + r]
+
+        @pl.when(own == 1)
+        def _():
+            pltpu.make_async_copy(store_ref.at[ints[count + r]], here, sem.at[r]).start()
+
+        @pl.when(own == 0)
+        def _():
+            pltpu.make_async_copy(recv_ref.at[r], here, sem.at[r]).start()
+
+
+def own_kernel(ints, lengths, x_ref, mod_ref, u_out, hot_out, stat_out):
+    rows, feat = x_ref.shape
+    reqs = mod_ref.shape[1]
+    x = x_ref[...].astype(F32)
+    mean = jnp.mean(x, axis=1, keepdims=True)
+    cent = x - mean
+    m2 = jnp.sum(cent * cent, axis=1, keepdims=True)
+    row = lax.broadcasted_iota(jnp.int32, (rows, 128), 0)
+    lane = lax.broadcasted_iota(jnp.int32, (rows, 128), 1)
+    first = jnp.zeros((1, 128), jnp.int32)
+    after = jnp.zeros((1, 128), jnp.int32)
+    lane1 = lax.broadcasted_iota(jnp.int32, (1, 128), 1)
+    begin = jnp.int32(0)
+    for r in range(reqs):
+        end = begin + lengths[r]
+        first = jnp.where(lane1 == r, begin, first)
+        after = jnp.where(lane1 == r, end, after)
+        begin = end
+    hot = jnp.where((row >= first) & (row < after), 1.0, 0.0)
+    hot_out[...] = hot.astype(BF)
+    stat_out[...] = jnp.where(lane == 0, mean, jnp.where(lane == 1, m2, 0.0)).T[:8]
+    scale_rows = jnp.dot(hot[:, :reqs].astype(BF), mod_ref[1], preferred_element_type=F32)
+    u_out[...] = (cent * (1.0 + scale_rows)).astype(BF)
+
+
+def low_kernel(
+    count, ints, u_ref, hot_ref, stat_ref, mod_ref, down_ref, recv_ref, after_ref, low_out, pack_out, down_now, sem
+):
+    rows, feat = u_ref.shape
+    reqs, rank = recv_ref.shape[:2]
+    fetch_adapters(count, ints, down_ref, recv_ref, down_now, sem, False)
+    hot_t = hot_ref[...].astype(F32).T
+    fetch_adapters(count, ints, down_ref, recv_ref, down_now, sem, True)
+    every = lax.dot_general(
+        down_now[...], u_ref[...], (((1,), (1,)), ((), ())), preferred_element_type=F32
+    )
+    total = jnp.zeros((rank, rows), F32)
+    side = jnp.zeros((rank, 128), F32)
+    lane = lax.broadcasted_iota(jnp.int32, (rank, 128), 1)
+    for r in range(reqs):
+        total = total + every[r * rank : (r + 1) * rank] * hot_t[r : r + 1]
+        mat = down_now[pl.ds(r * rank, rank), :].astype(F32)
+        by_scale = jnp.sum(mat * (1.0 + mod_ref[1, pl.ds(r, 1), :].astype(F32)), axis=1, keepdims=True)
+        by_shift = jnp.sum(mat * mod_ref[0, pl.ds(r, 1), :].astype(F32), axis=1, keepdims=True)
+        side = jnp.where(lane == r, by_scale, side)
+        side = jnp.where(lane == reqs + r, by_shift, side)
+    low_out[...] = total.astype(BF)
+    stat = stat_ref[...]
+    here = lax.broadcasted_iota(jnp.int32, (count, rows), 0) == ints[0]
+    pack_out[pl.ds(0, count), :] = jnp.where(here, stat[0:1], 0.0)
+    turned = jnp.concatenate([side, jnp.zeros((128 - rank, 128), F32)], axis=0).T
+    flat = jnp.concatenate([turned[: 2 * reqs], jnp.zeros((2 * reqs, rows - 128), F32)], axis=1)
+    pack_out[pl.ds(count, 2 * reqs), :] = flat
+    pack_out[pl.ds(count + 2 * reqs, 8), :] = jnp.broadcast_to(stat[1:2], (8, rows))
+
+
+def merge(count, span, reqs, low_a, pack_a, low_b, pack_b, hot_ref):
+    hot_t = hot_ref[...].astype(F32).T[:reqs]
+    pa, pb = pack_a[...], pack_b[...]
+    rank = low_a.shape[0]
+    gap = (jnp.sum(pa[:count], axis=0, keepdims=True) - jnp.sum(pb[:count], axis=0, keepdims=True)) / span
+    diff = (pa - pb)[count : count + reqs, :rank]
+    back = lax.dot_general(
+        diff, hot_t, (((0,), (0,)), ((), ())), precision=HIGH, preferred_element_type=F32
+    )
+    low = low_a[...].astype(F32) + low_b[...].astype(F32) + (0.5 * gap) * back
+    return low, pa + pb, hot_t
+
+
+def merge_kernel(count, span, reqs, *refs):
+    low, pack, _ = merge(count, span, reqs, *refs[:5])
+    refs[5][...] = low.astype(BF)
+    refs[6][...] = pack
+
+
+def last_merge_kernel(count, span, reqs, feat, *refs):
+    wide_out, col_out = refs[5:]
+    low, pack, hot_t = merge(count, span, reqs, *refs[:5])
+    rank, rows = low.shape
+    means = pack[:count]
+    mean = jnp.sum(means, axis=0, keepdims=True) / count
+    dev = means - mean
+    m2 = pack[count + 2 * reqs : count + 2 * reqs + 1] + feat * jnp.sum(dev * dev, axis=0, keepdims=True)
+    rstd = lax.rsqrt(m2 / (count * feat) + 1e-06)
+    shifted = lax.dot_general(
+        pack[count + reqs : count + 2 * reqs, :rank], hot_t, (((0,), (0,)), ((), ())),
+        precision=HIGH, preferred_element_type=F32,
+    )
+    low = (low * rstd + shifted).astype(BF).astype(F32)
+    pad = 128 - rank - count - 1
+    turned = jnp.concatenate([low, dev * rstd, rstd, jnp.zeros((pad, rows), F32)], axis=0).T
+    col_out[...] = jnp.broadcast_to(turned[:, rank + count : rank + count + 1], (rows, 128))
+    turned = turned.astype(BF)
+    hot8 = refs[4][...][:, :reqs]
+
+    def spread(src_count, width, rule):
+        src = lax.broadcasted_iota(jnp.int32, (src_count, width), 0)
+        dst = lax.broadcasted_iota(jnp.int32, (src_count, width), 1)
+        return jnp.where(rule(src, dst), 1.0, 0.0).astype(BF)
+
+    def times(a, b):
+        return jnp.dot(a, b, preferred_element_type=F32)
+
+    width = reqs * rank
+    lora = times(turned, spread(128, width, lambda s, d: (d % rank == s) & (s < rank)))
+    lora = lora * times(hot8, spread(reqs, width, lambda s, d: d // rank == s))
+    pairs = count * reqs
+    coef = times(turned, spread(128, 128, lambda s, d: (s == rank + d // reqs) & (d < pairs)))
+    coef = coef * times(hot8, spread(reqs, 128, lambda s, d: (d % reqs == s) & (d < pairs)))
+    coef = coef + times(
+        hot8, spread(reqs, 128, lambda s, d: (d % reqs == s) & (d >= pairs) & (d < pairs + 2 * reqs))
+    )
+    wide_out[:, pl.ds(0, width)] = lora.astype(BF)
+    wide_out[:, pl.ds(width, 128)] = coef.astype(BF)
+
+
+def means_kernel(count, mod_ref, w_ref, bias_ref, after_ref, out_ref, total):
+    step = pl.program_id(0)
+    reqs = mod_ref.shape[1]
+    feat = mod_ref.shape[2]
+    lhs = jnp.concatenate([jnp.ones((reqs, feat), F32), mod_ref[1].astype(F32), mod_ref[0].astype(F32)], axis=0)
+    lhs = jnp.concatenate([lhs, jnp.zeros((8, feat), F32)], axis=0).astype(BF)
+    got = jnp.dot(lhs, w_ref[...], preferred_element_type=F32)
+    total[0, pl.ds(pl.multiple_of(step * reqs, reqs), reqs), :] = got[:reqs] + got[reqs : 2 * reqs]
+
+    @pl.when(step == 0)
+    def _():
+        total[1, pl.ds(0, reqs), :] = got[2 * reqs : 3 * reqs] + bias_ref[...].astype(F32)
+
+    @pl.when(step > 0)
+    def _():
+        total[1, pl.ds(0, reqs), :] += got[2 * reqs : 3 * reqs]
+
+    @pl.when(step == count - 1)
+    def _():
+        shift = total[1, pl.ds(0, reqs), :]
+        high = shift.astype(BF).astype(F32)
+        both = jnp.concatenate([high, shift - high], axis=0)
+        left = 128 - count * reqs - 2 * reqs
+        rows = [total[0, pl.ds(0, count * reqs), :], both]
+        if left:
+            rows.append(jnp.zeros((left, both.shape[1]), F32))
+        out_ref[...] = jnp.concatenate(rows, axis=0).astype(BF)
+
+
+N_TILE = 512
+
+
+def first_kernel(count, blocks, base, ints, *refs):
+    xs = refs[:blocks]
+    w_ref, acc_out, w_now, sem = refs[blocks:]
+    feat = xs[0].shape[1]
+    hidden = acc_out.shape[1]
+    tiles = hidden // N_TILE
+
+    def copy(k, n):
+        cols = pl.ds(n * N_TILE, N_TILE)
+        at = pl.multiple_of(ints[base + k] * feat, feat)
+        return pltpu.make_async_copy(
+            w_ref.at[pl.ds(at, feat), cols], w_now.at[n, pl.ds(k * feat, feat), :], sem.at[k, n]
+        )
+
+    for n in range(tiles):
+        for k in range(blocks):
+            copy(k, n).start()
+    lhs = jnp.concatenate([x[...] for x in xs], axis=1)
+    for n in range(tiles):
+        for k in range(blocks):
+            copy(k, n).wait()
+        acc_out[:, pl.ds(n * N_TILE, N_TILE)] = jnp.dot(lhs, w_now[n], preferred_element_type=F32)
+
+
+def lora_kernel(
+    count, blocks, base, ints, *refs
+):
+    xs = refs[:blocks]
+    (w_ref, acc_in, wide_ref, col_ref, tail_ref, up_ref, recv_ref, acc_out, w_now, up_now, sem, up_sem) = refs[blocks:]
+    feat = xs[0].shape[1]
+    hidden = acc_out.shape[1]
+    tiles = hidden // N_TILE
+    reqs, rank = recv_ref.shape[:2]
+
+    def copy(k, n):
+        cols = pl.ds(n * N_TILE, N_TILE)
+        at = pl.multiple_of(ints[base + k] * feat, feat)
+        return pltpu.make_async_copy(
+            w_ref.at[pl.ds(at, feat), cols], w_now.at[n, pl.ds(k * feat, feat), :], sem.at[k, n]
+        )
+
+    for n in range(tiles):
+        for k in range(blocks):
+            copy(k, n).start()
+    fetch_adapters(count, ints, up_ref, recv_ref, up_now, up_sem, False)
+    lhs = jnp.concatenate([x[...] for x in xs], axis=1)
+    scale = col_ref[:, 0:1]
+    for n in range(tiles):
+        cols = pl.ds(n * N_TILE, N_TILE)
+        for k in range(blocks):
+            copy(k, n).wait()
+        part = acc_in[:, cols] + jnp.dot(lhs, w_now[n], preferred_element_type=F32)
+        acc_out[:, cols] = part * scale
+    fetch_adapters(count, ints, up_ref, recv_ref, up_now, up_sem, True)
+    width = reqs * rank
+    wide = wide_ref[...]
+    for n in range(tiles):
+        cols = pl.ds(n * N_TILE, N_TILE)
+        both = jnp.concatenate([up_now[:, cols], tail_ref[:, cols]], axis=0)
+        acc_out[:, cols] += jnp.dot(wide, both, preferred_element_type=F32)
+
+
+def finish_kernel(ints, c_ref, d_ref, col_ref, w_ref, acc_ref, w2_ref, act_out, part_out):
+    upper = pl.program_id(0) < pl.num_programs(0) // 2
+    x = jnp.where(upper, c_ref[...].astype(F32), d_ref[...].astype(F32)).astype(BF)
+    pre = acc_ref[...] + jnp.dot(x, w_ref[...], preferred_element_type=F32) * col_ref[:, 0:1]
+    act = jax.nn.gelu(pre, approximate=True).astype(BF)
+    act_out[...] = act
+    part_out[...] = jnp.dot(act, w2_ref[...], preferred_element_type=F32).astype(BF)
+
+
+def second_kernel(blocks, base, ints, act_ref, w_ref, *refs):
+    outs = refs[:blocks]
+    w_now, sem = refs[blocks:]
+    feat = outs[0].shape[1]
+
+    def copy(k):
+        at = pl.multiple_of(ints[base - k] * feat, feat)
+        return pltpu.make_async_copy(
+            w_ref.at[:, pl.ds(at, feat)], w_now.at[:, pl.ds(k * feat, feat)], sem.at[k]
+        )
+
+    for k in range(blocks):
+        copy(k).start()
+    for k in range(blocks):
+        copy(k).wait()
+    got = jnp.dot(act_ref[...], w_now[...], preferred_element_type=F32)
+    for k in range(blocks):
+        outs[k][...] = got[:, k * feat : (k + 1) * feat]
+
+
+def ring_device(
+    count, tokens, modulation, adapter_per_request, tokens_per_request, first_weight,
+    first_bias, second_weight, second_bias, adapter_down_matrices, adapter_up_matrices,
+):
+    me = lax.axis_index("tensor")
+    store = lax.axis_index("store")
+    rows, feat = tokens.shape
+    hidden = first_weight.shape[1]
+    stored, rank = adapter_up_matrices.shape[:2]
+    reqs = tokens_per_request.shape[1]
+    order = ring_order(count)
+    forth = [(order[i], order[(i + 1) % count]) for i in range(count)]
+    back = [(b, a) for a, b in forth]
+    half = count // 2
+    visits = [0] + [s for k in range(1, half) for s in (-k, k)] + [half]
+    table = [[0] * count for _ in range(count)]
+    for at, dev in enumerate(order):
+        table[dev] = [order[(at + k) % count] for k in visits]
+    mine = lax.dynamic_index_in_dim(jnp.array(table, jnp.int32), me, 0, keepdims=False)
+
+    def go(x, route):
+        return lax.ppermute(x, "tensor", route)
+
+    def like(*shape, kind=BF):
+        return jax.ShapeDtypeStruct(shape, kind)
+
+    down = jnp.swapaxes(adapter_down_matrices, 1, 2)
+    mod = jnp.swapaxes(modulation[0], 0, 1)
+
+    my_ids = lax.dynamic_index_in_dim(adapter_per_request, store, 0, keepdims=False)
+    their_ids = lax.dynamic_index_in_dim(adapter_per_request, 1 - store, 0, keepdims=False)
+    ids = jnp.concatenate([my_ids, their_ids])
+    ints = jnp.concatenate(
+        [
+            mine,
+            jnp.clip(ids - store * stored, 0, stored - 1),
+            (my_ids // stored == store).astype(jnp.int32),
+        ]
+    )
+
+    own_mod = pl.BlockSpec((3, reqs, feat), lambda i, s, *_: (0, 0, s[0]))
+    flat = lambda *shape: pl.BlockSpec(shape, lambda i, *_: (0,) * len(shape))
+    u, hot, stat = pl.pallas_call(
+        own_kernel,
+        grid_spec=pltpu.PrefetchScalarGridSpec(
+            num_scalar_prefetch=2,
+            grid=(1,),
+            in_specs=[flat(rows, feat), own_mod],
+            out_specs=[flat(rows, feat), flat(rows, 128), flat(8, rows)],
+        ),
+        out_shape=[like(rows, feat), like(rows, 128), like(8, rows, kind=F32)],
+        compiler_params=params(),
+        cost_estimate=cost(20 * rows * feat, 6 * rows * feat),
+        name="own_features",
+    )(ints, tokens_per_request[0], tokens, mod)
+
+    send_down, send_up = pl.pallas_call(
+        functools.partial(send_kernel, count),
+        in_specs=[SMEM, ANY, ANY],
+        out_specs=[WHOLE, WHOLE],
+        out_shape=[like(reqs, rank, feat), like(reqs, rank, hidden)],
+        scratch_shapes=[pltpu.SemaphoreType.DMA((2 * reqs,))],
+        compiler_params=params(),
+        cost_estimate=cost(0, 4 * reqs * rank * (feat + hidden)),
+        name="adapters_to_send",
+    )(ints, down, adapter_up_matrices)
+    swap = [(s, s ^ 1) for s in range(lax.axis_size("store"))]
+    recv_down = lax.ppermute(send_down, "store", swap)
+    recv_up = lax.ppermute(send_up, "store", swap)
+
+    tail = pl.pallas_call(
+        functools.partial(means_kernel, count),
+        grid=(count,),
+        in_specs=[
+            pl.BlockSpec((3, reqs, feat), lambda i: (0, 0, i)),
+            pl.BlockSpec((feat, hidden), lambda i: (i, 0)),
+            pl.BlockSpec((1, hidden), lambda i: (0, 0)),
+            ANY,
+        ],
+        out_specs=pl.BlockSpec((128, hidden), lambda i: (0, 0)),
+        out_shape=like(128, hidden),
+        scratch_shapes=[pltpu.VMEM((2, count * reqs, hidden), F32)],
+        compiler_params=params(),
+        cost_estimate=cost(64 * count * feat * hidden, 2 * count * feat * hidden),
+        name="means_part",
+    )(mod, first_weight, first_bias.reshape(1, hidden), send_down)
+
+    low, pack = pl.pallas_call(
+        functools.partial(low_kernel, count),
+        grid_spec=pltpu.PrefetchScalarGridSpec(
+            num_scalar_prefetch=1,
+            grid=(1,),
+            in_specs=[flat(rows, feat), flat(rows, 128), flat(8, rows), own_mod, ANY, ANY, ANY],
+            out_specs=[flat(rank, rows), flat(count + 2 * reqs + 8, rows)],
+            scratch_shapes=[
+                pltpu.VMEM((reqs * rank, feat), BF),
+                pltpu.SemaphoreType.DMA((reqs,)),
+            ],
+        ),
+        out_shape=[like(rank, rows), like(count + 2 * reqs + 8, rows, kind=F32)],
+        compiler_params=params(),
+        cost_estimate=cost(2 * rows * feat * reqs * rank, 4 * rows * feat),
+        name="low_rank_parts",
+    )(ints, u, hot, stat, mod, down, recv_down, tail)
+    gates = [low]
+    span = 1
+    while span < count:
+        route = [(t, t ^ span) for t in range(count)]
+        args = (low, pack, go(low, route), go(pack, route), hot)
+        if 2 * span == count:
+            kernel = functools.partial(last_merge_kernel, count, span, reqs, feat)
+            shapes = [like(rows, reqs * rank + 128), like(rows, 128, kind=F32)]
+        else:
+            kernel = functools.partial(merge_kernel, count, span, reqs)
+            shapes = [like(*low.shape), like(*pack.shape, kind=F32)]
+        low, pack = pl.pallas_call(
+            kernel,
+            in_specs=[WHOLE] * 5,
+            out_specs=[WHOLE] * 2,
+            out_shape=shapes,
+            compiler_params=params(),
+            cost_estimate=cost(4e10, 8 * rank * rows),
+            name="merge_sums",
+        )(*args)
+        gates.append(low)
+        span *= 2
+    wide, cols = low, pack
+
+    cut = rows // 2
+    a = b = u
+    seen = [u]
+    for k in range(1, half):
+        a, b = go(a, forth), go(b, back)
+        seen += [a, b]
+        a, b, _ = lax.optimization_barrier((a, b, gates[k - 1]))
+    far_c, far_d = go(a[:cut], forth), go(b[cut:], back)
+
+    tiles = hidden // N_TILE
+    early, late = seen[:-2], seen[-2:]
+    w_scratch = lambda n: [
+        pltpu.VMEM((tiles, n * feat, N_TILE), BF),
+    ]
+    acc = pl.pallas_call(
+        functools.partial(first_kernel, count, len(early), 0),
+        in_specs=[SMEM] + [WHOLE] * len(early) + [ANY],
+        out_specs=WHOLE,
+        out_shape=like(rows, hidden, kind=F32),
+        scratch_shapes=w_scratch(len(early)) + [pltpu.SemaphoreType.DMA((len(early), tiles))],
+        compiler_params=params(),
+        cost_estimate=cost(2 * rows * feat * hidden * len(early), 2 * feat * hidden * len(early)),
+        name="first_blocks",
+    )(ints, *early, first_weight)
+    acc = pl.pallas_call(
+        functools.partial(lora_kernel, count, len(late), len(early)),
+        in_specs=[SMEM] + [WHOLE] * len(late) + [ANY] + [WHOLE] * 4 + [ANY, ANY],
+        out_specs=WHOLE,
+        out_shape=like(rows, hidden, kind=F32),
+        scratch_shapes=w_scratch(len(late))
+        + [
+            pltpu.VMEM((reqs * rank, hidden), BF),
+            pltpu.SemaphoreType.DMA((len(late), tiles)),
+            pltpu.SemaphoreType.DMA((reqs,)),
+        ],
+        compiler_params=params(),
+        cost_estimate=cost(
+            2 * rows * hidden * (feat * len(late) + reqs * rank), 2 * feat * hidden * len(late)
+        ),
+        name="low_rank_added",
+    )(ints, *late, first_weight, acc, wide, cols, tail, adapter_up_matrices, recv_up)
+    steps = 4
+    tile = rows // steps
+    last = count - 1
+    tiled = lambda width: pl.BlockSpec((tile, width), lambda i, *s: (i, 0))
+    act, far_part = pl.pallas_call(
+        finish_kernel,
+        grid_spec=pltpu.PrefetchScalarGridSpec(
+            num_scalar_prefetch=1,
+            grid=(steps,),
+            in_specs=[
+                pl.BlockSpec((tile, feat), lambda i, s: (jnp.minimum(i, steps // 2 - 1), 0)),
+                pl.BlockSpec((tile, feat), lambda i, s: (jnp.maximum(i - steps // 2, 0), 0)),
+                tiled(128),
+                pl.BlockSpec((feat, hidden), lambda i, s: (s[last], 0)),
+                tiled(hidden),
+                pl.BlockSpec((hidden, feat), lambda i, s: (0, s[last])),
+            ],
+            out_specs=[tiled(hidden), tiled(feat)],
+        ),
+        out_shape=[like(rows, hidden), like(rows, feat)],
+        compiler_params=params(),
+        cost_estimate=cost(4 * rows * hidden * feat, 14 * rows * hidden, rows * hidden),
+        name="finish_first",
+    )(ints, far_c, far_d, cols, first_weight, acc, second_weight)
+
+    def second(blocks, base, name):
+        return pl.pallas_call(
+            functools.partial(second_kernel, blocks, base),
+            in_specs=[SMEM, WHOLE, ANY],
+            out_specs=[WHOLE] * blocks,
+            out_shape=[like(rows, feat, kind=F32)] * blocks,
+            scratch_shapes=[
+                pltpu.VMEM((hidden, blocks * feat), BF),
+                pltpu.SemaphoreType.DMA((blocks,)),
+            ],
+            compiler_params=params(),
+            cost_estimate=cost(2 * rows * hidden * feat * blocks, blocks * rows * feat * 8),
+            name=name,
+        )(ints, act, second_weight)
+
+    parts = {}
+    base = count - 2
+    for k in range(half - 1, 0, -1):
+        blocks = 3 if k == 1 else 2
+        got = second(blocks, base, "second_blocks")
+        base -= blocks
+        parts[k], parts[-k] = got[0], got[1]
+    parts[0] = got[2]
+    gate = jnp.dot(
+        hot[:, :reqs], lax.dynamic_slice_in_dim(mod[2], me * feat, feat, 1),
+        preferred_element_type=F32,
+    )
+    rights, lefts = [], []
+    chains = 2
+    size = rows // chains
+    for c in range(chains):
+        lo = c * size
+        mid = size // 2
+        right = go(far_part[lo : lo + mid], forth)
+        left = go(far_part[lo + mid : lo + size], back)
+        for k in range(half - 1, 0, -1):
+            r = parts[k][lo : lo + size]
+            l = parts[-k][lo : lo + size]
+            if k == half - 1:
+                r = jnp.concatenate([r[:mid] + right.astype(F32), r[mid:]])
+                l = jnp.concatenate([l[:mid], l[mid:] + left.astype(F32)])
+            else:
+                r = r + right.astype(F32)
+                l = l + left.astype(F32)
+            right = go(r.astype(BF), forth)
+            left = go(l.astype(BF), back)
+        rights.append(right)
+        lefts.append(left)
+    mixed = parts[0] + jnp.concatenate(rights).astype(F32) + jnp.concatenate(lefts).astype(F32)
+    return (tokens.astype(F32) + gate * (mixed + second_bias.astype(F32))).astype(BF)
 
 
 def partner(block, axis, stride):
@@ -23,7 +576,7 @@
     )
 
 
-def on_device(
+def plain_device(
     tokens,
     modulation,
     adapter_per_request,
@@ -111,6 +664,12 @@
     return block_out.astype(jnp.bfloat16)
 
 
+def on_device(count, tokens, *rest):
+    if tokens.shape[1] % 128 == 0 and count % 4 == 0 and count & (count - 1) == 0:
+        return ring_device(count, tokens, *rest)
+    return plain_device(tokens, *rest)
+
+
 def solution(mesh):
     in_specs = (
         P(("groups", "store"), "tensor"),
@@ -126,5 +685,5 @@
     )
     out_specs = P(("groups", "store"), "tensor")
     return jax.shard_map(
-        on_device, mesh=mesh, in_specs=in_specs, out_specs=out_specs, check_vma=False
-    )
+        functools.partial(on_device, mesh.shape["tensor"]), mesh=mesh, in_specs=in_specs, out_specs=out_specs, check_vma=False
+    )

time: 328 us -> 139 us (0.42)
  waiting for transfers between devices: 233 us -> 49.2 us
  matrix products: 46.1 us -> 0.95 us
  Pallas kernels: 0 us -> 39.5 us
  starting transfers between devices: 0.72 us -> 39.4 us
  local copies, waits for them, and re-layouts: 25.7 us -> 6.15 us
  between operations: 13.3 us -> 0.47 us
  other arithmetic: 9.05 us -> 2.73 us
    reduce_scatter x1 -> x0, waiting for transfers between devices: 138 us -> none  [on_device(): lax.psum_scatter(lax.dot_general(second_weight, activated, (((0,), (1,)),...]
    all_gather x2 -> x0, waiting for transfers between devices: 94.8 us -> none  [the longest x1 50.4 us: on_device(): lax.all_gather(down_now, 'tensor', axis=1, tiled=True)]
    ppermute x2 -> x32, waiting for transfers between devices: 0.01 us -> 49.2 us  [the longest x30 49.2 us: go(): return lax.ppermute(x, 'tensor', route)]
    pallas_call x0 -> x13, Pallas kernels: none -> 39.5 us  [the longest x3 9.05 us: second(): pl.pallas_call(functools.partial(second_kernel, blocks, base), in_specs=[...]
    dot_general x5 -> x1, matrix products: 40.2 us -> 0.95 us  [ring_device(): jnp.dot(hot[:, :reqs], lax.dynamic_slice_in_dim(mod[2], me * feat, feat,...]
    ppermute x2 -> x32, starting transfers between devices: 0.64 us -> 39.4 us  [the longest x30 38.9 us: go(): return lax.ppermute(x, 'tensor', route)]
    gather x4 -> x0, local copies, waits for them, and re-layouts: 25 us -> none  [the longest x2 18.2 us: pick_owned(): up_matrix_rows = jnp.take(adapter_up_matrices, request_index_list, axis=0)]
    reduce_sum x4 -> x0, other arithmetic: 6.76 us -> none  [the longest x1 3.74 us: on_device(): spread = jnp.mean((gathered - center) ** 2, axis=1, keepdims=True)]
  transfers between devices with their start and end apart: 5 -> 32, of which waited for: 3 -> 19; matrix products, arithmetic and copies ran while one was open for 19% -> 2% of each run, Pallas kernels for 0% -> 19%
where the time goes in v3:
time: 139 us; the launch traced here: 138 us
  waiting for transfers between devices  49.2 us (35%)
  Pallas kernels  39.5 us (28%)
  starting transfers between devices  39.4 us (28%)
  local copies, waits for them, and re-layouts  6.15 us (4%)
  other arithmetic  2.73 us (2%)
    ppermute x30, waiting for transfers between devices, go(): return lax.ppermute(x, 'tensor', route)  49.2 us
    ppermute x30, starting transfers between devices, go(): return lax.ppermute(x, 'tensor', route)  38.9 us
    pallas_call x3, Pallas kernels, second(): pl.pallas_call(functools.partial(second_kernel, blocks, base), in_specs=[...  9.05 us
    pallas_call x1, Pallas kernels, ring_device(): pl.pallas_call(functools.partial(first_kernel, count, len(early), 0), in_...  6.83 us
    pallas_call x1, Pallas kernels, ring_device(): pl.pallas_call(functools.partial(lora_kernel, count, len(late), len(early...  5.74 us
    pallas_call x1, Pallas kernels, ring_device(): pl.pallas_call(finish_kernel, grid_spec=pltpu.PrefetchScalarGridSpec(num_...  4.2 us
    pallas_call x1, Pallas kernels, ring_device(): pl.pallas_call(functools.partial(send_kernel, count), in_specs=[SMEM, ANY...  4.07 us
    unnamed x40, local copies, waits for them, and re-layouts  3.99 us
  transfers between devices with their start and end apart: 32, of which 19 were waited for; matrix products, arithmetic and copies ran while one was open for 2% of the time, Pallas kernels for 19%

profile of v3, /device:TPU:0, one launch (start us, length us, event | category | flops | bytes accessed | tf_op | source)
XLA Modules:
  0.0 138.4 jit_solution(16998070981208235787)
XLA Ops:
  2.2 2.9 %copy-done = bf16[128,384,64]{1,2,0:T(8,128)(2,1)S(1)} copy-done((bf16[128,384,64]{1,2,0:T(8,128)(2,1)S(1)}, bf16[128,384,64]{1,2,0:T(8,128)(2,1)}, u32[]{:S(2)}) %copy-start) | copy-done | bytes 6291480
  5.2 4.1 %adapters_to_send.1 = (bf16[8,64,384]{2,1,0:T(8,128)(2,1)S(1)}, bf16[8,64,1536]{2,1,0:T(8,128)(2,1)}) custom-call(s32[32]{0:T(128)S(1)} %pad_add_fusion.ints, bf16[128,64,384]{2,1,0:T(8,128)(2,1)S(1)} %bitcast.21, bf16[128,64,1536]{2,1,0:T(8,128)(2,1)} %refs_7_.1), custom_call_target="tpu_custom_call" | custom-call | bytes 3932160 | tf_op jit(solution)/shard_map/adapters_to_send/pallas_call | solution.py:370
  10.9 2.8 %means_part.1.after_ref.refs_6_ = bf16[128,1536]{1,0:T(8,128)(2,1)S(1)} custom-call(bf16[3,8,3072]{2,1,0:T(8,128)(2,1)S(1)} %bitcast.24, bf16[3072,1536]{1,0:T(8,128)(2,1)S(1)} %bitcast.16, bf16[1,1536]{1,0:T(2,128)(2,1)S(1)} %reshape.5.bias_ref, bf16[8,64,384]{2,1,0:T(8,128)(2,1)S(1)} %get-tuple-element.36.after_ref), custom_call_target="tpu_custom_call" | custom-call | flops 301989888 | bytes 9437184 | tf_op jit(solution)/shard_map/means_part/pallas_call | solution.py:384
  15.7 2.6 %collective-permute-start.5 = (bf16[64,640]{1,0:T(8,128)(2,1)S(1)}, bf16[64,640]{1,0:T(8,128)(2,1)S(1)}, u32[]{:S(2)}, u32[]{:S(2)}) collective-permute-start(bf16[64,640]{1,0:T(8,128)(2,1)S(1)} %get-tuple-element.37.refs_0_), channel_id=1, source_target_pairs={{0,2},{2,0},{4,6},{6,4},{8,10},{10,8},{12,14},{14,12},{1,3},{3,1},... | collective-permute-start | bytes 245768 | tf_op jit(solution)/shard_map/ppermute | solution.py:335
  26.3 7.5 %collective-permute-done.refs_1_ = bf16[640,384]{1,0:T(8,128)(2,1)} collective-permute-done((bf16[640,384]{1,0:T(8,128)(2,1)S(1)}, bf16[640,384]{1,0:T(8,128)(2,1)}, u32[]{:S(2)}, u32[]{:S(2)}) %collective-permute-start) | collective-permute-done | bytes 491552 | tf_op jit(solution)/shard_map/ppermute | solution.py:335
  38.3 2.1 %collective-permute-start.13 = (bf16[64,640]{1,0:T(8,128)(2,1)}, bf16[64,640]{1,0:T(8,128)(2,1)}, u32[]{:S(2)}, u32[]{:S(2)}) collective-permute-start(bf16[64,640]{1,0:T(8,128)(2,1)} %get-tuple-element.45.refs_0_), channel_id=1, source_target_pairs={{0,8},{2,10},{4,12},{6,14},{8,0},{10,2},{12,4},{14,6},{1,9},{3,11}... | collective-permute-start | bytes 245768 | tf_op jit(solution)/shard_map/ppermute | solution.py:335
  41.9 5.1 %collective-permute-done.3.refs_3_ = bf16[640,384]{1,0:T(8,128)(2,1)} collective-permute-done((bf16[640,384]{1,0:T(8,128)(2,1)}, bf16[640,384]{1,0:T(8,128)(2,1)}, u32[]{:S(2)}, u32[]{:S(2)}) %collective-permute-start.3) | collective-permute-done | bytes 491552 | tf_op jit(solution)/shard_map/ppermute | solution.py:335
  48.0 7.4 %collective-permute-start.7 = (bf16[640,384]{1,0:T(8,128)(2,1)}, bf16[640,384]{1,0:T(8,128)(2,1)S(1)}, u32[]{:S(2)}, u32[]{:S(2)}) collective-permute-start(bf16[640,384]{1,0:T(8,128)(2,1)} %collective-permute-done.3.refs_3_), channel_id=1, source_target_pairs={{0,4},{4,8},{8,12},{12,14},{14,10},{10,6},{6,2},{2,0},{1,5},{5,9},... | collective-permute-start | bytes 1474568 | tf_op jit(solution)/shard_map/ppermute | solution.py:335
  59.2 2.2 %merge_sums.5 = (bf16[640,640]{1,0:T(8,128)(2,1)S(1)}, f32[640,128]{1,0:T(8,128)S(1)}) custom-call(bf16[64,640]{1,0:T(8,128)(2,1)} %get-tuple-element.45.refs_0_, f32[32,640]{1,0:T(8,128)} %get-tuple-element.48.refs_1_, bf16[64,640]{1,0:T(8,128)(2,1)} %collective-permute-done.13.refs_2_, f32[32,640]{1,0:T(8,128)} %collective-permute-done.14.refs_3_, ...), custom_call_target="tpu_custom_call" | custom-call | flops 40000000000 | bytes 327680 | tf_op jit(solution)/shard_map/merge_sums/pallas_call | solution.py:429
  62.1 2.3 %collective-permute-done.8.refs_1_ = bf16[640,384]{1,0:T(8,128)(2,1)S(1)} collective-permute-done((bf16[640,384]{1,0:T(8,128)(2,1)}, bf16[640,384]{1,0:T(8,128)(2,1)S(1)}, u32[]{:S(2)}, u32[]{:S(2)}) %collective-permute-start.8) | collective-permute-done | bytes 491552 | tf_op jit(solution)/shard_map/ppermute | solution.py:335
  64.5 2.8 %collective-permute-start.11 = (bf16[320,384]{1,0:T(8,128)(2,1)S(1)}, bf16[320,384]{1,0:T(8,128)(2,1)S(1)}, u32[]{:S(2)}, u32[]{:S(2)}) collective-permute-start(bf16[320,384]{1,0:T(8,128)(2,1)S(1)} %slice.90), channel_id=1, source_target_pairs={{0,4},{4,8},{8,12},{12,14},{14,10},{10,6},{6,2},{2,0},{1,5},{5,9},... | collective-permute-start | bytes 737288 | tf_op jit(solution)/shard_map/ppermute | solution.py:335
  67.4 6.8 %first_blocks.1.refs_3_ = f32[640,1536]{1,0:T(8,128)S(1)} custom-call(s32[32]{0:T(128)S(1)} %pad_add_fusion.ints, bf16[640,384]{1,0:T(8,128)(2,1)S(1)} %get-tuple-element.34.u_ref.refs_0_, bf16[640,384]{1,0:T(8,128)(2,1)} %collective-permute-done.refs_1_, bf16[640,384]{1,0:T(8,128)(2,1)} %collective-permute-done.1.refs_2_, ...), custom_call_target="tpu_custom_call" | custom-call | flops 3774873600 | bytes 5898240 | tf_op jit(solution)/shard_map/first_blocks/pallas_call | solution.py:456
  74.2 5.7 %low_rank_added.1.acc_ref = f32[640,1536]{1,0:T(8,128)S(1)} custom-call(s32[32]{0:T(128)S(1)} %pad_add_fusion.ints, bf16[640,384]{1,0:T(8,128)(2,1)S(1)} %collective-permute-done.7.refs_0_, bf16[640,384]{1,0:T(8,128)(2,1)S(1)} %collective-permute-done.8.refs_1_, bf16[3072,1536]{1,0:T(8,128)(2,1)S(1)} %bitcast.18, f32[640,1536]{1,0:T(8,128)S(1)} %first_blocks.1.refs_3_, ...), custom_call_target="tpu_custom_call" | custom-call | flops 2516582400 | bytes 2359296 | tf_op jit(solution)/shard_map/low_rank_added/pallas_call | solution.py:466
  80.1 4.2 %finish_first.1 = (bf16[640,1536]{1,0:T(8,128)(2,1)S(1)}, bf16[640,384]{1,0:T(8,128)(2,1)S(1)}) custom-call(s32[32]{0:T(128)S(1)} %pad_add_fusion.ints, bf16[320,384]{1,0:T(8,128)(2,1)S(1)} %collective-permute-done.11.c_ref, bf16[320,384]{1,0:T(8,128)(2,1)S(1)} %collective-permute-done.12.d_ref, f32[640,128]{1,0:T(8,128)S(1)} %get-tuple-element.49.refs_5_.col_ref, ...), custom_call_target="tpu_custom_call" | custom-call | flops 1509949440 | bytes 13762560 | tf_op jit(solution)/shard_map/finish_first/pallas_call | solution.py:487
  84.3 2.6 %second_blocks.5 = (f32[640,384]{1,0:T(8,128)S(1)}, f32[640,384]{1,0:T(8,128)S(1)}) custom-call(s32[32]{0:T(128)S(1)} %pad_add_fusion.ints, bf16[640,1536]{1,0:T(8,128)(2,1)S(1)} %get-tuple-element.52.act_ref, bf16[1536,3072]{1,0:T(8,128)(2,1)S(1)} %bitcast.20), custom_call_target="tpu_custom_call" | custom-call | flops 1509949440 | bytes 3932160 | tf_op jit(solution)/shard_map/second_blocks/pallas_call | solution.py:509
  91.2 3.9 %second_blocks.3 = (f32[640,384]{1,0:T(8,128)S(1)}, f32[640,384]{1,0:T(8,128)S(1)}, f32[640,384]{1,0:T(8,128)S(1)}) custom-call(s32[32]{0:T(128)S(1)} %pad_add_fusion.ints, bf16[640,1536]{1,0:T(8,128)(2,1)S(1)} %get-tuple-element.52.act_ref, bf16[1536,3072]{1,0:T(8,128)(2,1)S(1)} %bitcast.20), custom_call_target="tpu_custom_call" | custom-call | flops 2264924160 | bytes 5898240 | tf_op jit(solution)/shard_map/second_blocks/pallas_call | solution.py:509
  98.9 2.6 %second_blocks.4 = (f32[640,384]{1,0:T(8,128)S(1)}, f32[640,384]{1,0:T(8,128)S(1)}) custom-call(s32[32]{0:T(128)S(1)} %pad_add_fusion.ints, bf16[640,1536]{1,0:T(8,128)(2,1)S(1)} %get-tuple-element.52.act_ref, bf16[1536,3072]{1,0:T(8,128)(2,1)S(1)} %bitcast.20), custom_call_target="tpu_custom_call" | custom-call | flops 1509949440 | bytes 3932160 | tf_op jit(solution)/shard_map/second_blocks/pallas_call | solution.py:509
  104.3 4.6 %collective-permute-done.25 = bf16[320,384]{1,0:T(8,128)(2,1)S(1)} collective-permute-done((bf16[320,384]{1,0:T(8,128)(2,1)S(1)}, bf16[320,384]{1,0:T(8,128)(2,1)S(1)}, u32[]{:S(2)}, u32[]{:S(2)}) %collective-permute-start.25) | collective-permute-done | bytes 245792 | tf_op jit(solution)/shard_map/ppermute | solution.py:335
  110.3 4.1 %collective-permute-done.17 = bf16[320,384]{1,0:T(8,128)(2,1)S(1)} collective-permute-done((bf16[320,384]{1,0:T(8,128)(2,1)S(1)}, bf16[320,384]{1,0:T(8,128)(2,1)S(1)}, u32[]{:S(2)}, u32[]{:S(2)}) %collective-permute-start.17) | collective-permute-done | bytes 245792 | tf_op jit(solution)/shard_map/ppermute | solution.py:335
  114.5 2.4 %collective-permute-start.18 = (bf16[320,384]{1,0:T(8,128)(2,1)S(1)}, bf16[320,384]{1,0:T(8,128)(2,1)S(1)}, u32[]{:S(2)}, u32[]{:S(2)}) collective-permute-start(bf16[320,384]{1,0:T(8,128)(2,1)S(1)} %get-tuple-element.71), channel_id=1, source_target_pairs={{0,4},{4,8},{8,12},{12,14},{14,10},{10,6},{6,2},{2,0},{1,5},{5,9},... | collective-permute-start | bytes 737288 | tf_op jit(solution)/shard_map/ppermute | solution.py:335
  117.6 3.8 %collective-permute-done.30 = bf16[320,384]{1,0:T(8,128)(2,1)S(1)} collective-permute-done((bf16[320,384]{1,0:T(8,128)(2,1)S(1)}, bf16[320,384]{1,0:T(8,128)(2,1)S(1)}, u32[]{:S(2)}, u32[]{:S(2)}) %collective-permute-start.30) | collective-permute-done | bytes 245792 | tf_op jit(solution)/shard_map/ppermute | solution.py:335
  123.0 5.3 %collective-permute-done.22 = bf16[320,384]{1,0:T(8,128)(2,1)S(1)} collective-permute-done((bf16[320,384]{1,0:T(8,128)(2,1)S(1)}, bf16[320,384]{1,0:T(8,128)(2,1)S(1)}, u32[]{:S(2)}, u32[]{:S(2)}) %collective-permute-start.22) | collective-permute-done | bytes 245792 | tf_op jit(solution)/shard_map/ppermute | solution.py:335
  128.4 2.5 %collective-permute-start.19 = (bf16[320,384]{1,0:T(8,128)(2,1)S(1)}, bf16[320,384]{1,0:T(8,128)(2,1)S(1)}, u32[]{:S(2)}, u32[]{:S(2)}) collective-permute-start(bf16[320,384]{1,0:T(8,128)(2,1)S(1)} %get-tuple-element.69), channel_id=1, source_target_pairs={{0,4},{4,8},{8,12},{12,14},{14,10},{10,6},{6,2},{2,0},{1,5},{5,9},... | collective-permute-start | bytes 737288 | tf_op jit(solution)/shard_map/ppermute | solution.py:335
  134.7 2.6 %collective-permute-done.23 = bf16[320,384]{1,0:T(8,128)(2,1)S(1)} collective-permute-done((bf16[320,384]{1,0:T(8,128)(2,1)S(1)}, bf16[320,384]{1,0:T(8,128)(2,1)S(1)}, u32[]{:S(2)}, u32[]{:S(2)}) %collective-permute-start.23) | collective-permute-done | bytes 245792 | tf_op jit(solution)/shard_map/ppermute | solution.py:335
  (122 shorter events, 45.1 us)
Async XLA Ops:
  18.3 15.4 %collective-permute-start = (bf16[640,384]{1,0:T(8,128)(2,1)S(1)}, bf16[640,384]{1,0:T(8,128)(2,1)}, u32[]{:S(2)}, u32[]{:S(2)}) collective-permute-start(bf16[640,384]{1,0:T(8,128)(2,1)S(1)} %get-tuple-element.34.u_ref.refs_0_), channel_id=1, source_target_pairs={{0,4},{4,8},{8,12},{12,14},{14,10},{10,6},{6,2},{2,0},{1,5},{5,9},... | collective-permute-start | bytes 1474568 | tf_op jit(solution)/shard_map/ppermute | solution.py:335
  20.4 14.2 %collective-permute-start.1 = (bf16[640,384]{1,0:T(8,128)(2,1)S(1)}, bf16[640,384]{1,0:T(8,128)(2,1)}, u32[]{:S(2)}, u32[]{:S(2)}) collective-permute-start(bf16[640,384]{1,0:T(8,128)(2,1)S(1)} %get-tuple-element.34.u_ref.refs_0_), channel_id=1, source_target_pairs={{4,0},{8,4},{12,8},{14,12},{10,14},{6,10},{2,6},{0,2},{5,1},{9,5},... | collective-permute-start | bytes 1474568 | tf_op jit(solution)/shard_map/ppermute | solution.py:335
  24.2 12.4 %collective-permute-start.10 = (f32[32,640]{1,0:T(8,128)S(1)}, f32[32,640]{1,0:T(8,128)S(1)}, u32[]{:S(2)}, u32[]{:S(2)}) collective-permute-start(f32[32,640]{1,0:T(8,128)S(1)} %get-tuple-element.44.refs_1_), channel_id=1, source_target_pairs={{0,4},{2,6},{4,0},{6,2},{8,12},{10,14},{12,8},{14,10},{1,5},{3,7},... | collective-permute-start | bytes 245768 | tf_op jit(solution)/shard_map/ppermute | solution.py:335
  25.6 11.6 %collective-permute-start.9 = (bf16[64,640]{1,0:T(8,128)(2,1)S(1)}, bf16[64,640]{1,0:T(8,128)(2,1)S(1)}, u32[]{:S(2)}, u32[]{:S(2)}) collective-permute-start(bf16[64,640]{1,0:T(8,128)(2,1)S(1)} %get-tuple-element.41.refs_0_), channel_id=1, source_target_pairs={{0,4},{2,6},{4,0},{6,2},{8,12},{10,14},{12,8},{14,10},{1,5},{3,7},... | collective-permute-start | bytes 245768 | tf_op jit(solution)/shard_map/ppermute | solution.py:335
  34.6 12.3 %collective-permute-start.3 = (bf16[640,384]{1,0:T(8,128)(2,1)}, bf16[640,384]{1,0:T(8,128)(2,1)}, u32[]{:S(2)}, u32[]{:S(2)}) collective-permute-start(bf16[640,384]{1,0:T(8,128)(2,1)} %collective-permute-done.refs_1_), channel_id=1, source_target_pairs={{0,4},{4,8},{8,12},{12,14},{14,10},{10,6},{6,2},{2,0},{1,5},{5,9},... | collective-permute-start | bytes 1474568 | tf_op jit(solution)/shard_map/ppermute | solution.py:335
  34.8 13.2 %collective-permute-start.4 = (bf16[640,384]{1,0:T(8,128)(2,1)}, bf16[640,384]{1,0:T(8,128)(2,1)}, u32[]{:S(2)}, u32[]{:S(2)}) collective-permute-start(bf16[640,384]{1,0:T(8,128)(2,1)} %collective-permute-done.1.refs_2_), channel_id=1, source_target_pairs={{4,0},{8,4},{12,8},{14,12},{10,14},{6,10},{2,6},{0,2},{5,1},{9,5},... | collective-permute-start | bytes 1474568 | tf_op jit(solution)/shard_map/ppermute | solution.py:335
  38.3 18.3 %collective-permute-start.13 = (bf16[64,640]{1,0:T(8,128)(2,1)}, bf16[64,640]{1,0:T(8,128)(2,1)}, u32[]{:S(2)}, u32[]{:S(2)}) collective-permute-start(bf16[64,640]{1,0:T(8,128)(2,1)} %get-tuple-element.45.refs_0_), channel_id=1, source_target_pairs={{0,8},{2,10},{4,12},{6,14},{8,0},{10,2},{12,4},{14,6},{1,9},{3,11}... | collective-permute-start | bytes 245768 | tf_op jit(solution)/shard_map/ppermute | solution.py:335
  40.4 17.9 %collective-permute-start.14 = (f32[32,640]{1,0:T(8,128)}, f32[32,640]{1,0:T(8,128)}, u32[]{:S(2)}, u32[]{:S(2)}) collective-permute-start(f32[32,640]{1,0:T(8,128)} %get-tuple-element.48.refs_1_), channel_id=1, source_target_pairs={{0,8},{2,10},{4,12},{6,14},{8,0},{10,2},{12,4},{14,6},{1,9},{3,11}... | collective-permute-start | bytes 245768 | tf_op jit(solution)/shard_map/ppermute | solution.py:335
  41.2 33.0 %collective-permute-start.15 = (bf16[8,64,1536]{2,1,0:T(8,128)(2,1)}, bf16[8,64,1536]{2,1,0:T(8,128)(2,1)S(1)}, u32[]{:S(2)}, u32[]{:S(2)}) collective-permute-start(bf16[8,64,1536]{2,1,0:T(8,128)(2,1)} %get-tuple-element.51), channel_id=1, source_target_pairs={{0,1},{1,0},{2,3},{3,2},{4,5},{5,4},{6,7},{7,6},{8,9},{9,8},{10,11... | collective-permute-start | bytes 4718600 | tf_op jit(solution)/shard_map/ppermute | solution.py:382
  48.0 14.2 %collective-permute-start.7 = (bf16[640,384]{1,0:T(8,128)(2,1)}, bf16[640,384]{1,0:T(8,128)(2,1)S(1)}, u32[]{:S(2)}, u32[]{:S(2)}) collective-permute-start(bf16[640,384]{1,0:T(8,128)(2,1)} %collective-permute-done.3.refs_3_), channel_id=1, source_target_pairs={{0,4},{4,8},{8,12},{12,14},{14,10},{10,6},{6,2},{2,0},{1,5},{5,9},... | collective-permute-start | bytes 1474568 | tf_op jit(solution)/shard_map/ppermute | solution.py:335
  55.4 9.0 %collective-permute-start.8 = (bf16[640,384]{1,0:T(8,128)(2,1)}, bf16[640,384]{1,0:T(8,128)(2,1)S(1)}, u32[]{:S(2)}, u32[]{:S(2)}) collective-permute-start(bf16[640,384]{1,0:T(8,128)(2,1)} %collective-permute-done.4.refs_4_), channel_id=1, source_target_pairs={{4,0},{8,4},{12,8},{14,12},{10,14},{6,10},{2,6},{0,2},{5,1},{9,5},... | collective-permute-start | bytes 1474568 | tf_op jit(solution)/shard_map/ppermute | solution.py:335
  64.5 15.5 %collective-permute-start.11 = (bf16[320,384]{1,0:T(8,128)(2,1)S(1)}, bf16[320,384]{1,0:T(8,128)(2,1)S(1)}, u32[]{:S(2)}, u32[]{:S(2)}) collective-permute-start(bf16[320,384]{1,0:T(8,128)(2,1)S(1)} %slice.90), channel_id=1, source_target_pairs={{0,4},{4,8},{8,12},{12,14},{14,10},{10,6},{6,2},{2,0},{1,5},{5,9},... | collective-permute-start | bytes 737288 | tf_op jit(solution)/shard_map/ppermute | solution.py:335
  67.3 12.7 %collective-permute-start.12 = (bf16[320,384]{1,0:T(8,128)(2,1)S(1)}, bf16[320,384]{1,0:T(8,128)(2,1)S(1)}, u32[]{:S(2)}, u32[]{:S(2)}) collective-permute-start(bf16[320,384]{1,0:T(8,128)(2,1)S(1)} %slice.91), channel_id=1, source_target_pairs={{4,0},{8,4},{12,8},{14,12},{10,14},{6,10},{2,6},{0,2},{5,1},{9,5},... | collective-permute-start | bytes 737288 | tf_op jit(solution)/shard_map/ppermute | solution.py:335
  86.9 8.2 %collective-permute-start.16 = (bf16[160,384]{1,0:T(8,128)(2,1)S(1)}, bf16[160,384]{1,0:T(8,128)(2,1)S(1)}, u32[]{:S(2)}, u32[]{:S(2)}) collective-permute-start(bf16[160,384]{1,0:T(8,128)(2,1)S(1)} %get-tuple-element.80), channel_id=1, source_target_pairs={{0,4},{4,8},{8,12},{12,14},{14,10},{10,6},{6,2},{2,0},{1,5},{5,9},... | collective-permute-start | bytes 368648 | tf_op jit(solution)/shard_map/ppermute | solution.py:335
  97.4 7.0 %collective-permute-start.29 = (bf16[320,384]{1,0:T(8,128)(2,1)S(1)}, bf16[320,384]{1,0:T(8,128)(2,1)S(1)}, u32[]{:S(2)}, u32[]{:S(2)}) collective-permute-start(bf16[320,384]{1,0:T(8,128)(2,1)S(1)} %pad_maximum_fusion.3), channel_id=1, source_target_pairs={{4,0},{8,4},{12,8},{14,12},{10,14},{6,10},{2,6},{0,2},{5,1},{9,5},... | collective-permute-start | bytes 737288 | tf_op jit(solution)/shard_map/ppermute | solution.py:335
  98.8 10.1 %collective-permute-start.25 = (bf16[320,384]{1,0:T(8,128)(2,1)S(1)}, bf16[320,384]{1,0:T(8,128)(2,1)S(1)}, u32[]{:S(2)}, u32[]{:S(2)}) collective-permute-start(bf16[320,384]{1,0:T(8,128)(2,1)S(1)} %pad_maximum_fusion.2), channel_id=1, source_target_pairs={{4,0},{8,4},{12,8},{14,12},{10,14},{6,10},{2,6},{0,2},{5,1},{9,5},... | collective-permute-start | bytes 737288 | tf_op jit(solution)/shard_map/ppermute | solution.py:335
  101.5 8.7 %collective-permute-start.21 = (bf16[320,384]{1,0:T(8,128)(2,1)S(1)}, bf16[320,384]{1,0:T(8,128)(2,1)S(1)}, u32[]{:S(2)}, u32[]{:S(2)}) collective-permute-start(bf16[320,384]{1,0:T(8,128)(2,1)S(1)} %pad_maximum_fusion.1), channel_id=1, source_target_pairs={{0,4},{4,8},{8,12},{12,14},{14,10},{10,6},{6,2},{2,0},{1,5},{5,9},... | collective-permute-start | bytes 737288 | tf_op jit(solution)/shard_map/ppermute | solution.py:335
  103.6 10.7 %collective-permute-start.17 = (bf16[320,384]{1,0:T(8,128)(2,1)S(1)}, bf16[320,384]{1,0:T(8,128)(2,1)S(1)}, u32[]{:S(2)}, u32[]{:S(2)}) collective-permute-start(bf16[320,384]{1,0:T(8,128)(2,1)S(1)} %pad_maximum_fusion), channel_id=1, source_target_pairs={{0,4},{4,8},{8,12},{12,14},{14,10},{10,6},{6,2},{2,0},{1,5},{5,9},... | collective-permute-start | bytes 737288 | tf_op jit(solution)/shard_map/ppermute | solution.py:335
  109.1 8.6 %collective-permute-start.26 = (bf16[320,384]{1,0:T(8,128)(2,1)S(1)}, bf16[320,384]{1,0:T(8,128)(2,1)S(1)}, u32[]{:S(2)}, u32[]{:S(2)}) collective-permute-start(bf16[320,384]{1,0:T(8,128)(2,1)S(1)} %get-tuple-element.65), channel_id=1, source_target_pairs={{4,0},{8,4},{12,8},{14,12},{10,14},{6,10},{2,6},{0,2},{5,1},{9,5},... | collective-permute-start | bytes 737288 | tf_op jit(solution)/shard_map/ppermute | solution.py:335
  110.2 11.3 %collective-permute-start.30 = (bf16[320,384]{1,0:T(8,128)(2,1)S(1)}, bf16[320,384]{1,0:T(8,128)(2,1)S(1)}, u32[]{:S(2)}, u32[]{:S(2)}) collective-permute-start(bf16[320,384]{1,0:T(8,128)(2,1)S(1)} %get-tuple-element.66), channel_id=1, source_target_pairs={{4,0},{8,4},{12,8},{14,12},{10,14},{6,10},{2,6},{0,2},{5,1},{9,5},... | collective-permute-start | bytes 737288 | tf_op jit(solution)/shard_map/ppermute | solution.py:335
  114.5 8.6 %collective-permute-start.18 = (bf16[320,384]{1,0:T(8,128)(2,1)S(1)}, bf16[320,384]{1,0:T(8,128)(2,1)S(1)}, u32[]{:S(2)}, u32[]{:S(2)}) collective-permute-start(bf16[320,384]{1,0:T(8,128)(2,1)S(1)} %get-tuple-element.71), channel_id=1, source_target_pairs={{0,4},{4,8},{8,12},{12,14},{14,10},{10,6},{6,2},{2,0},{1,5},{5,9},... | collective-permute-start | bytes 737288 | tf_op jit(solution)/shard_map/ppermute | solution.py:335
  116.8 11.5 %collective-permute-start.22 = (bf16[320,384]{1,0:T(8,128)(2,1)S(1)}, bf16[320,384]{1,0:T(8,128)(2,1)S(1)}, u32[]{:S(2)}, u32[]{:S(2)}) collective-permute-start(bf16[320,384]{1,0:T(8,128)(2,1)S(1)} %get-tuple-element.72), channel_id=1, source_target_pairs={{0,4},{4,8},{8,12},{12,14},{14,10},{10,6},{6,2},{2,0},{1,5},{5,9},... | collective-permute-start | bytes 737288 | tf_op jit(solution)/shard_map/ppermute | solution.py:335
  121.5 11.2 %collective-permute-start.27 = (bf16[320,384]{1,0:T(8,128)(2,1)S(1)}, bf16[320,384]{1,0:T(8,128)(2,1)S(1)}, u32[]{:S(2)}, u32[]{:S(2)}) collective-permute-start(bf16[320,384]{1,0:T(8,128)(2,1)S(1)} %get-tuple-element.63), channel_id=1, source_target_pairs={{4,0},{8,4},{12,8},{14,12},{10,14},{6,10},{2,6},{0,2},{5,1},{9,5},... | collective-permute-start | bytes 737288 | tf_op jit(solution)/shard_map/ppermute | solution.py:335
  122.2 10.5 %collective-permute-start.31 = (bf16[320,384]{1,0:T(8,128)(2,1)S(1)}, bf16[320,384]{1,0:T(8,128)(2,1)S(1)}, u32[]{:S(2)}, u32[]{:S(2)}) collective-permute-start(bf16[320,384]{1,0:T(8,128)(2,1)S(1)} %get-tuple-element.64), channel_id=1, source_target_pairs={{4,0},{8,4},{12,8},{14,12},{10,14},{6,10},{2,6},{0,2},{5,1},{9,5},... | collective-permute-start | bytes 737288 | tf_op jit(solution)/shard_map/ppermute | solution.py:335
  (28 other events, 279.5 us)

commit v4 on v3

--- a/solution.py
+++ b/solution.py
@@ -9,18 +9,19 @@
 
 BF = jnp.bfloat16
 F32 = jnp.float32
-VMEM_LIMIT = 24 * 1024 * 1024
+SEND_MIB = 60
 HIGH = lax.Precision.HIGHEST
 ANY = pl.BlockSpec(memory_space=pltpu.HBM)
 SMEM = pl.BlockSpec(memory_space=pltpu.SMEM)
 WHOLE = pl.BlockSpec(memory_space=pltpu.VMEM)
 
 
-def params(**more):
-    return pltpu.CompilerParams(vmem_limit_bytes=VMEM_LIMIT, **more)
-
-
-def cost(flops, nbytes, trans=0):
+def params(mib=24):
+    return pltpu.CompilerParams(vmem_limit_bytes=mib * 1024 * 1024)
+
+
+def cost(flops, nbytes, trans=0, scale=1.0):
+    flops, nbytes, trans = flops * scale, nbytes * scale, trans * scale
     return pl.CostEstimate(
         flops=int(flops), bytes_accessed=int(nbytes), transcendentals=int(trans)
     )
@@ -41,13 +42,21 @@
     return ref.at[place, :] if axis == 0 else ref.at[:, place]
 
 
-def send_kernel(count, ints, down_ref, up_ref, down_out, up_out, sem):
+def place(ids, whose, r, stored):
+    return jnp.clip(ids[whose, r] - lax.axis_index("store") * stored, 0, stored - 1)
+
+
+def send_kernel(ids, down_ref, up_ref, down_out, mine_out, up_out, sem):
     reqs = down_out.shape[0]
+    stored = down_ref.shape[0]
+    me = lax.axis_index("store")
     copies = []
     for r in range(reqs):
-        at = ints[count + reqs + r]
-        copies.append(pltpu.make_async_copy(down_ref.at[at], down_out.at[r], sem.at[2 * r]))
-        copies.append(pltpu.make_async_copy(up_ref.at[at], up_out.at[r], sem.at[2 * r + 1]))
+        at = place(ids, 1 - me, r, stored)
+        own = place(ids, me, r, stored)
+        copies.append(pltpu.make_async_copy(down_ref.at[at], down_out.at[r], sem.at[0, r]))
+        copies.append(pltpu.make_async_copy(down_ref.at[own], mine_out.at[r], sem.at[1, r]))
+        copies.append(pltpu.make_async_copy(up_ref.at[at], up_out.at[r], sem.at[2, r]))
     for c in copies:
         c.start()
     for c in copies:
@@ -72,9 +81,10 @@
             pltpu.make_async_copy(recv_ref.at[r], here, sem.at[r]).start()
 
 
-def own_kernel(ints, lengths, x_ref, mod_ref, u_out, hot_out, stat_out):
+def own_kernel(lengths, x_ref, mod_ref, u_out, hot_out, stat_out):
     rows, feat = x_ref.shape
     reqs = mod_ref.shape[1]
+    own = pl.ds(pl.multiple_of(lax.axis_index("tensor") * feat, feat), feat)
     x = x_ref[...].astype(F32)
     mean = jnp.mean(x, axis=1, keepdims=True)
     cent = x - mean
@@ -86,25 +96,37 @@
     lane1 = lax.broadcasted_iota(jnp.int32, (1, 128), 1)
     begin = jnp.int32(0)
     for r in range(reqs):
-        end = begin + lengths[r]
+        end = begin + lengths[0, r]
         first = jnp.where(lane1 == r, begin, first)
         after = jnp.where(lane1 == r, end, after)
         begin = end
     hot = jnp.where((row >= first) & (row < after), 1.0, 0.0)
     hot_out[...] = hot.astype(BF)
     stat_out[...] = jnp.where(lane == 0, mean, jnp.where(lane == 1, m2, 0.0)).T[:8]
-    scale_rows = jnp.dot(hot[:, :reqs].astype(BF), mod_ref[1], preferred_element_type=F32)
+    scale_rows = jnp.dot(hot[:, :reqs].astype(BF), mod_ref[1, :, own], preferred_element_type=F32)
     u_out[...] = (cent * (1.0 + scale_rows)).astype(BF)
 
 
 def low_kernel(
-    count, ints, u_ref, hot_ref, stat_ref, mod_ref, down_ref, recv_ref, after_ref, low_out, pack_out, down_now, sem
+    count, stored, ids, u_ref, hot_ref, stat_ref, mod_ref, mine_ref, recv_ref, low_out, pack_out, down_now
 ):
     rows, feat = u_ref.shape
     reqs, rank = recv_ref.shape[:2]
-    fetch_adapters(count, ints, down_ref, recv_ref, down_now, sem, False)
+    me = lax.axis_index("tensor")
+    store = lax.axis_index("store")
+    own = pl.ds(pl.multiple_of(me * feat, feat), feat)
+    for r in range(reqs):
+        here = pl.ds(r * rank, rank)
+
+        @pl.when(ids[store, r] // stored == store)
+        def _():
+            down_now[here, :] = mine_ref[r]
+
+        @pl.when(ids[store, r] // stored != store)
+        def _():
+            down_now[here, :] = recv_ref[r]
+
     hot_t = hot_ref[...].astype(F32).T
-    fetch_adapters(count, ints, down_ref, recv_ref, down_now, sem, True)
     every = lax.dot_general(
         down_now[...], u_ref[...], (((1,), (1,)), ((), ())), preferred_element_type=F32
     )
@@ -114,13 +136,13 @@
     for r in range(reqs):
         total = total + every[r * rank : (r + 1) * rank] * hot_t[r : r + 1]
         mat = down_now[pl.ds(r * rank, rank), :].astype(F32)
-        by_scale = jnp.sum(mat * (1.0 + mod_ref[1, pl.ds(r, 1), :].astype(F32)), axis=1, keepdims=True)
-        by_shift = jnp.sum(mat * mod_ref[0, pl.ds(r, 1), :].astype(F32), axis=1, keepdims=True)
+        by_scale = jnp.sum(mat * (1.0 + mod_ref[1, pl.ds(r, 1), own].astype(F32)), axis=1, keepdims=True)
+        by_shift = jnp.sum(mat * mod_ref[0, pl.ds(r, 1), own].astype(F32), axis=1, keepdims=True)
         side = jnp.where(lane == r, by_scale, side)
         side = jnp.where(lane == reqs + r, by_shift, side)
     low_out[...] = total.astype(BF)
     stat = stat_ref[...]
-    here = lax.broadcasted_iota(jnp.int32, (count, rows), 0) == ints[0]
+    here = lax.broadcasted_iota(jnp.int32, (count, rows), 0) == me
     pack_out[pl.ds(0, count), :] = jnp.where(here, stat[0:1], 0.0)
     turned = jnp.concatenate([side, jnp.zeros((128 - rank, 128), F32)], axis=0).T
     flat = jnp.concatenate([turned[: 2 * reqs], jnp.zeros((2 * reqs, rows - 128), F32)], axis=1)
@@ -351,36 +373,40 @@
         ]
     )
 
-    own_mod = pl.BlockSpec((3, reqs, feat), lambda i, s, *_: (0, 0, s[0]))
-    flat = lambda *shape: pl.BlockSpec(shape, lambda i, *_: (0,) * len(shape))
     u, hot, stat = pl.pallas_call(
         own_kernel,
-        grid_spec=pltpu.PrefetchScalarGridSpec(
-            num_scalar_prefetch=2,
-            grid=(1,),
-            in_specs=[flat(rows, feat), own_mod],
-            out_specs=[flat(rows, feat), flat(rows, 128), flat(8, rows)],
-        ),
+        in_specs=[SMEM, WHOLE, WHOLE],
+        out_specs=[WHOLE] * 3,
         out_shape=[like(rows, feat), like(rows, 128), like(8, rows, kind=F32)],
         compiler_params=params(),
-        cost_estimate=cost(20 * rows * feat, 6 * rows * feat),
+        cost_estimate=cost(2 * rows * feat, rows * feat),
         name="own_features",
-    )(ints, tokens_per_request[0], tokens, mod)
-
-    send_down, send_up = pl.pallas_call(
-        functools.partial(send_kernel, count),
+    )(tokens_per_request, tokens, mod)
+
+    send_down, mine_down, send_up = pl.pallas_call(
+        send_kernel,
         in_specs=[SMEM, ANY, ANY],
-        out_specs=[WHOLE, WHOLE],
-        out_shape=[like(reqs, rank, feat), like(reqs, rank, hidden)],
-        scratch_shapes=[pltpu.SemaphoreType.DMA((2 * reqs,))],
-        compiler_params=params(),
-        cost_estimate=cost(0, 4 * reqs * rank * (feat + hidden)),
+        out_specs=[WHOLE] * 3,
+        out_shape=[like(reqs, rank, feat)] * 2 + [like(reqs, rank, hidden)],
+        scratch_shapes=[pltpu.SemaphoreType.DMA((3, reqs))],
+        compiler_params=params(SEND_MIB),
+        cost_estimate=cost(0, reqs * rank * (feat + hidden)),
         name="adapters_to_send",
-    )(ints, down, adapter_up_matrices)
+    )(adapter_per_request, down, adapter_up_matrices)
     swap = [(s, s ^ 1) for s in range(lax.axis_size("store"))]
     recv_down = lax.ppermute(send_down, "store", swap)
+
+    low, pack = pl.pallas_call(
+        functools.partial(low_kernel, count, stored),
+        in_specs=[SMEM] + [WHOLE] * 6,
+        out_specs=[WHOLE] * 2,
+        out_shape=[like(rank, rows), like(count + 2 * reqs + 8, rows, kind=F32)],
+        scratch_shapes=[pltpu.VMEM((reqs * rank, feat), BF)],
+        compiler_params=params(),
+        cost_estimate=cost(rows * feat * reqs, rows * feat),
+        name="low_rank_parts",
+    )(adapter_per_request, u, hot, stat, mod, mine_down, recv_down)
     recv_up = lax.ppermute(send_up, "store", swap)
-
     tail = pl.pallas_call(
         functools.partial(means_kernel, count),
         grid=(count,),
@@ -394,32 +420,27 @@
         out_shape=like(128, hidden),
         scratch_shapes=[pltpu.VMEM((2, count * reqs, hidden), F32)],
         compiler_params=params(),
-        cost_estimate=cost(64 * count * feat * hidden, 2 * count * feat * hidden),
+        cost_estimate=cost(64 * count * feat * hidden, 2 * count * feat * hidden, scale=0.1),
         name="means_part",
-    )(mod, first_weight, first_bias.reshape(1, hidden), send_down)
-
-    low, pack = pl.pallas_call(
-        functools.partial(low_kernel, count),
-        grid_spec=pltpu.PrefetchScalarGridSpec(
-            num_scalar_prefetch=1,
-            grid=(1,),
-            in_specs=[flat(rows, feat), flat(rows, 128), flat(8, rows), own_mod, ANY, ANY, ANY],
-            out_specs=[flat(rank, rows), flat(count + 2 * reqs + 8, rows)],
-            scratch_shapes=[
-                pltpu.VMEM((reqs * rank, feat), BF),
-                pltpu.SemaphoreType.DMA((reqs,)),
-            ],
-        ),
-        out_shape=[like(rank, rows), like(count + 2 * reqs + 8, rows, kind=F32)],
-        compiler_params=params(),
-        cost_estimate=cost(2 * rows * feat * reqs * rank, 4 * rows * feat),
-        name="low_rank_parts",
-    )(ints, u, hot, stat, mod, down, recv_down, tail)
-    gates = [low]
+    )(mod, first_weight, first_bias.reshape(1, hidden), low)
+
+    cut = rows // 2
+    a = b = u
+    seen = [u]
+    for k in range(1, half):
+        a, b = go(a, forth), go(b, back)
+        seen += [a, b]
+    far_c, far_d = go(a[:cut], forth), go(b[cut:], back)
+
+    turn = 0
     span = 1
     while span < count:
         route = [(t, t ^ span) for t in range(count)]
-        args = (low, pack, go(low, route), go(pack, route), hot)
+        low_b, pack_b = go(low, route), go(pack, route)
+        turn += 1
+        if turn in (1, 2):
+            low_b, pack_b, *_ = lax.optimization_barrier((low_b, pack_b, seen[2 * turn - 1], seen[2 * turn]))
+        args = (low, pack, low_b, pack_b, hot)
         if 2 * span == count:
             kernel = functools.partial(last_merge_kernel, count, span, reqs, feat)
             shapes = [like(rows, reqs * rank + 128), like(rows, 128, kind=F32)]
@@ -432,21 +453,12 @@
             out_specs=[WHOLE] * 2,
             out_shape=shapes,
             compiler_params=params(),
-            cost_estimate=cost(4e10, 8 * rank * rows),
+            cost_estimate=cost(1e+09, 8 * rank * rows),
             name="merge_sums",
         )(*args)
-        gates.append(low)
         span *= 2
     wide, cols = low, pack
 
-    cut = rows // 2
-    a = b = u
-    seen = [u]
-    for k in range(1, half):
-        a, b = go(a, forth), go(b, back)
-        seen += [a, b]
-        a, b, _ = lax.optimization_barrier((a, b, gates[k - 1]))
-    far_c, far_d = go(a[:cut], forth), go(b[cut:], back)
 
     tiles = hidden // N_TILE
     early, late = seen[:-2], seen[-2:]
@@ -459,8 +471,8 @@
         out_specs=WHOLE,
         out_shape=like(rows, hidden, kind=F32),
         scratch_shapes=w_scratch(len(early)) + [pltpu.SemaphoreType.DMA((len(early), tiles))],
-        compiler_params=params(),
-        cost_estimate=cost(2 * rows * feat * hidden * len(early), 2 * feat * hidden * len(early)),
+        compiler_params=params(24),
+        cost_estimate=cost(2 * rows * feat * hidden * len(early), 2 * feat * hidden * len(early), scale=1),
         name="first_blocks",
     )(ints, *early, first_weight)
     acc = pl.pallas_call(
@@ -474,10 +486,9 @@
             pltpu.SemaphoreType.DMA((len(late), tiles)),
             pltpu.SemaphoreType.DMA((reqs,)),
         ],
-        compiler_params=params(),
+        compiler_params=params(24),
         cost_estimate=cost(
-            2 * rows * hidden * (feat * len(late) + reqs * rank), 2 * feat * hidden * len(late)
-        ),
+            2 * rows * hidden * (feat * len(late) + reqs * rank), 2 * feat * hidden * len(late), scale=1),
         name="low_rank_added",
     )(ints, *late, first_weight, acc, wide, cols, tail, adapter_up_matrices, recv_up)
     steps = 4
@@ -500,8 +511,8 @@
             out_specs=[tiled(hidden), tiled(feat)],
         ),
         out_shape=[like(rows, hidden), like(rows, feat)],
-        compiler_params=params(),
-        cost_estimate=cost(4 * rows * hidden * feat, 14 * rows * hidden, rows * hidden),
+        compiler_params=params(16),
+        cost_estimate=cost(4 * rows * hidden * feat, 14 * rows * hidden, rows * hidden, scale=1),
         name="finish_first",
     )(ints, far_c, far_d, cols, first_weight, acc, second_weight)
 
@@ -515,7 +526,7 @@
                 pltpu.VMEM((hidden, blocks * feat), BF),
                 pltpu.SemaphoreType.DMA((blocks,)),
             ],
-            compiler_params=params(),
+            compiler_params=params(16),
             cost_estimate=cost(2 * rows * hidden * feat * blocks, blocks * rows * feat * 8),
             name=name,
         )(ints, act, second_weight)
@@ -533,7 +544,7 @@
         preferred_element_type=F32,
     )
     rights, lefts = [], []
-    chains = 2
+    chains = 1
     size = rows // chains
     for c in range(chains):
         lo = c * size

time: 139 us -> 118 us (0.85)
  starting transfers between devices: 39.4 us -> 26.1 us
  waiting for transfers between devices: 49.2 us -> 43 us
  Pallas kernels: 39.5 us -> 35.3 us
  local copies, waits for them, and re-layouts: 6.15 us -> 8.18 us
  other arithmetic: 2.73 us -> 4.61 us
    ppermute x30 -> x22, starting transfers between devices: 38.9 us -> 25.5 us  [go(): return lax.ppermute(x, 'tensor', route)]
    ppermute x30 -> x22, waiting for transfers between devices: 49.2 us -> 43 us  [go(): return lax.ppermute(x, 'tensor', route)]
    unnamed x40 -> x28, local copies, waits for them, and re-layouts: 3.99 us -> 7.3 us
    pallas_call x3, Pallas kernels: 3.89 us -> 2.26 us  [ring_device(): pl.pallas_call(kernel, in_specs=[WHOLE] * 5, out_specs=[WHOLE] * 2, out_s...]
  transfers between devices with their start and end apart: 32 -> 24, of which waited for: 19 -> 12; matrix products, arithmetic and copies ran while one was open for 2% -> 3% of each run, Pallas kernels for 19% -> 26%
where the time goes in v4:
time: 118 us
  waiting for transfers between devices  43 us (36%)
  Pallas kernels  35.3 us (30%)
  starting transfers between devices  26.1 us (22%)
  local copies, waits for them, and re-layouts  8.18 us (7%)
  other arithmetic  4.61 us (4%)
    ppermute x22, waiting for transfers between devices, go(): return lax.ppermute(x, 'tensor', route)  43 us
    ppermute x22, starting transfers between devices, go(): return lax.ppermute(x, 'tensor', route)  25.5 us
    pallas_call x3, Pallas kernels, second(): pl.pallas_call(functools.partial(second_kernel, blocks, base), in_specs=[...  9 us
    unnamed x28, local copies, waits for them, and re-layouts  7.3 us
    pallas_call x1, Pallas kernels, ring_device(): pl.pallas_call(functools.partial(first_kernel, count, len(early), 0), in_...  5.88 us
    pallas_call x1, Pallas kernels, ring_device(): pl.pallas_call(functools.partial(lora_kernel, count, len(late), len(early...  4.74 us
    pallas_call x1, Pallas kernels, ring_device(): pl.pallas_call(send_kernel, in_specs=[SMEM, ANY, ANY], out_specs=[WHOLE]...  4.18 us
    pallas_call x1, Pallas kernels, ring_device(): pl.pallas_call(finish_kernel, grid_spec=pltpu.PrefetchScalarGridSpec(num_...  4.13 us
  transfers between devices with their start and end apart: 24, of which 12 were waited for; matrix products, arithmetic and copies ran while one was open for 3% of the time, Pallas kernels for 26%

profile of v4, /device:TPU:0, one launch (start us, length us, event | category | flops | bytes accessed | tf_op | source)
XLA Modules:
  0.0 117.9 jit_solution(1121398366204832216)
XLA Ops:
  3.6 3.1 %collective-permute-start = (bf16[640,384]{1,0:T(8,128)(2,1)S(1)}, bf16[640,384]{1,0:T(8,128)(2,1)S(1)}, u32[]{:S(2)}, u32[]{:S(2)}) collective-permute-start(bf16[640,384]{1,0:T(8,128)(2,1)S(1)} %get-tuple-element.33.u_ref.refs_0_), channel_id=1, source_target_pairs={{0,4},{4,8},{8,12},{12,14},{14,10},{10,6},{6,2},{2,0},{1,5},{5,9},... | collective-permute-start | bytes 1474568 | tf_op jit(solution)/shard_map/ppermute | solution.py:357
  6.7 4.2 %adapters_to_send.1 = (bf16[8,64,384]{2,1,0:T(8,128)(2,1)}, bf16[8,64,384]{2,1,0:T(8,128)(2,1)}, bf16[8,64,1536]{2,1,0:T(8,128)(2,1)}) custom-call(s32[2,8]{1,0:T(2,128)} %ids.3, bf16[128,64,384]{2,1,0:T(8,128)(2,1)} %bitcast.20, bf16[128,64,1536]{2,1,0:T(8,128)(2,1)} %refs_7_.1), custom_call_target="tpu_custom_call" | custom-call | bytes 983040 | tf_op jit(solution)/shard_map/adapters_to_send/pallas_call | solution.py:386
  11.4 6.4 %collective-permute-done.refs_1_ = bf16[640,384]{1,0:T(8,128)(2,1)S(1)} collective-permute-done((bf16[640,384]{1,0:T(8,128)(2,1)S(1)}, bf16[640,384]{1,0:T(8,128)(2,1)S(1)}, u32[]{:S(2)}, u32[]{:S(2)}) %collective-permute-start) | collective-permute-done | bytes 491552 | tf_op jit(solution)/shard_map/ppermute | solution.py:357
  25.1 7.7 %collective-permute-done.9.refs_2_ = bf16[64,640]{1,0:T(8,128)(2,1)S(1)} collective-permute-done((bf16[64,640]{1,0:T(8,128)(2,1)S(1)}, bf16[64,640]{1,0:T(8,128)(2,1)S(1)}, u32[]{:S(2)}, u32[]{:S(2)}) %collective-permute-start.9) | collective-permute-done | bytes 81952 | tf_op jit(solution)/shard_map/ppermute | solution.py:357
  34.4 2.0 %collective-permute-start.12 = (f32[32,640]{1,0:T(8,128)S(1)}, f32[32,640]{1,0:T(8,128)S(1)}, u32[]{:S(2)}, u32[]{:S(2)}) collective-permute-start(f32[32,640]{1,0:T(8,128)S(1)} %get-tuple-element.42.refs_1_), channel_id=1, source_target_pairs={{0,4},{2,6},{4,0},{6,2},{8,12},{10,14},{12,8},{14,10},{1,5},{3,7},... | collective-permute-start | bytes 245768 | tf_op jit(solution)/shard_map/ppermute | solution.py:357
  36.5 1.9 %collective-permute-start.6 = (bf16[640,384]{1,0:T(8,128)(2,1)S(1)}, bf16[640,384]{1,0:T(8,128)(2,1)S(1)}, u32[]{:S(2)}, u32[]{:S(2)}) collective-permute-start(bf16[640,384]{1,0:T(8,128)(2,1)S(1)} %collective-permute-done.5.refs_4_), channel_id=1, source_target_pairs={{4,0},{8,4},{12,8},{14,12},{10,14},{6,10},{2,6},{0,2},{5,1},{9,5},... | collective-permute-start | bytes 1474568 | tf_op jit(solution)/shard_map/ppermute | solution.py:357
  38.5 3.7 %copy-done = bf16[3072,1536]{1,0:T(8,128)(2,1)S(1)} copy-done((bf16[3072,1536]{1,0:T(8,128)(2,1)S(1)}, bf16[3072,1536]{1,0:T(8,128)(2,1)}, u32[]{:S(2)}) %copy-start) | copy-done | bytes 9437208
  42.2 2.7 %means_part.1.refs_6_ = bf16[128,1536]{1,0:T(8,128)(2,1)S(1)} custom-call(bf16[3,8,3072]{2,1,0:T(8,128)(2,1)S(1)} %bitcast.18, bf16[3072,1536]{1,0:T(8,128)(2,1)S(1)} %copy-done, bf16[1,1536]{1,0:T(2,128)(2,1)S(1)} %reshape.5.bias_ref, bf16[64,640]{1,0:T(8,128)(2,1)S(1)} %get-tuple-element.37.refs_0_.after_ref), custom_call_target="tpu_custom_call" | custom-call | flops 30198988 | bytes 943718 | tf_op jit(solution)/shard_map/means_part/pallas_call | solution.py:410
  45.5 3.4 %collective-permute-start.13 = (bf16[64,640]{1,0:T(8,128)(2,1)S(1)}, bf16[64,640]{1,0:T(8,128)(2,1)S(1)}, u32[]{:S(2)}, u32[]{:S(2)}) collective-permute-start(bf16[64,640]{1,0:T(8,128)(2,1)S(1)} %get-tuple-element.45.refs_0_), channel_id=1, source_target_pairs={{0,8},{2,10},{4,12},{6,14},{8,0},{10,2},{12,4},{14,6},{1,9},{3,11}... | collective-permute-start | bytes 245768 | tf_op jit(solution)/shard_map/ppermute | solution.py:357
  49.0 5.9 %first_blocks.1.refs_3_ = f32[640,1536]{1,0:T(8,128)S(1)} custom-call(s32[32]{0:T(128)S(1)} %pad_add_fusion.ints, bf16[640,384]{1,0:T(8,128)(2,1)S(1)} %get-tuple-element.33.u_ref.refs_0_, bf16[640,384]{1,0:T(8,128)(2,1)S(1)} %collective-permute-done.refs_1_, bf16[640,384]{1,0:T(8,128)(2,1)S(1)} %collective-permute-done.4.refs_2_, ...), custom_call_target="tpu_custom_call" | custom-call | flops 3774873600 | bytes 5898240 | tf_op jit(solution)/shard_map/first_blocks/pallas_call | solution.py:468
  54.9 2.0 %collective-permute-start.3 = (bf16[320,384]{1,0:T(8,128)(2,1)S(1)}, bf16[320,384]{1,0:T(8,128)(2,1)S(1)}, u32[]{:S(2)}, u32[]{:S(2)}) collective-permute-start(bf16[320,384]{1,0:T(8,128)(2,1)S(1)} %slice.43), channel_id=1, source_target_pairs={{0,4},{4,8},{8,12},{12,14},{14,10},{10,6},{6,2},{2,0},{1,5},{5,9},... | collective-permute-start | bytes 737288 | tf_op jit(solution)/shard_map/ppermute | solution.py:357
  58.7 4.7 %low_rank_added.1.acc_ref = f32[640,1536]{1,0:T(8,128)S(1)} custom-call(s32[32]{0:T(128)S(1)} %pad_add_fusion.ints, bf16[640,384]{1,0:T(8,128)(2,1)S(1)} %collective-permute-done.2.refs_0_, bf16[640,384]{1,0:T(8,128)(2,1)S(1)} %collective-permute-done.6.refs_1_, bf16[3072,1536]{1,0:T(8,128)(2,1)S(1)} %copy-done.1, f32[640,1536]{1,0:T(8,128)S(1)} %first_blocks.1.refs_3_, ...), custom_call_target="tpu_custom_call" | custom-call | flops 2516582400 | bytes 2359296 | tf_op jit(solution)/shard_map/low_rank_added/pallas_call | solution.py:478
  63.5 4.1 %finish_first.1 = (bf16[640,1536]{1,0:T(8,128)(2,1)S(1)}, bf16[640,384]{1,0:T(8,128)(2,1)S(1)}) custom-call(s32[32]{0:T(128)S(1)} %pad_add_fusion.ints, bf16[320,384]{1,0:T(8,128)(2,1)S(1)} %collective-permute-done.3.c_ref, bf16[320,384]{1,0:T(8,128)(2,1)S(1)} %collective-permute-done.7.d_ref, f32[640,128]{1,0:T(8,128)S(1)} %get-tuple-element.47.refs_5_.col_ref, ...), custom_call_target="tpu_custom_call" | custom-call | flops 1509949440 | bytes 13762560 | tf_op jit(solution)/shard_map/finish_first/pallas_call | solution.py:498
  69.5 2.6 %second_blocks.5 = (f32[640,384]{1,0:T(8,128)S(1)}, f32[640,384]{1,0:T(8,128)S(1)}) custom-call(s32[32]{0:T(128)S(1)} %pad_add_fusion.ints, bf16[640,1536]{1,0:T(8,128)(2,1)S(1)} %get-tuple-element.50.act_ref, bf16[1536,3072]{1,0:T(8,128)(2,1)S(1)} %bitcast.15), custom_call_target="tpu_custom_call" | custom-call | flops 1509949440 | bytes 3932160 | tf_op jit(solution)/shard_map/second_blocks/pallas_call | solution.py:520
  72.7 4.1 %collective-permute-done.16 = bf16[320,384]{1,0:T(8,128)(2,1)S(1)} collective-permute-done((bf16[320,384]{1,0:T(8,128)(2,1)S(1)}, bf16[320,384]{1,0:T(8,128)(2,1)S(1)}, u32[]{:S(2)}, u32[]{:S(2)}) %collective-permute-start.16) | collective-permute-done | bytes 245792 | tf_op jit(solution)/shard_map/ppermute | solution.py:357
  78.5 2.5 %collective-permute-done.20 = bf16[320,384]{1,0:T(8,128)(2,1)S(1)} collective-permute-done((bf16[320,384]{1,0:T(8,128)(2,1)S(1)}, bf16[320,384]{1,0:T(8,128)(2,1)S(1)}, u32[]{:S(2)}, u32[]{:S(2)}) %collective-permute-start.20) | collective-permute-done | bytes 245792 | tf_op jit(solution)/shard_map/ppermute | solution.py:357
  81.7 2.6 %second_blocks.4 = (f32[640,384]{1,0:T(8,128)S(1)}, f32[640,384]{1,0:T(8,128)S(1)}) custom-call(s32[32]{0:T(128)S(1)} %pad_add_fusion.ints, bf16[640,1536]{1,0:T(8,128)(2,1)S(1)} %get-tuple-element.50.act_ref, bf16[1536,3072]{1,0:T(8,128)(2,1)S(1)} %bitcast.15), custom_call_target="tpu_custom_call" | custom-call | flops 1509949440 | bytes 3932160 | tf_op jit(solution)/shard_map/second_blocks/pallas_call | solution.py:520
  84.3 5.0 %collective-permute-done.17 = bf16[640,384]{1,0:T(8,128)(2,1)S(1)} collective-permute-done((bf16[640,384]{1,0:T(8,128)(2,1)S(1)}, bf16[640,384]{1,0:T(8,128)(2,1)S(1)}, u32[]{:S(2)}, u32[]{:S(2)}) %collective-permute-start.17) | collective-permute-done | bytes 491552 | tf_op jit(solution)/shard_map/ppermute | solution.py:357
  90.8 2.5 %collective-permute-done.21 = bf16[640,384]{1,0:T(8,128)(2,1)S(1)} collective-permute-done((bf16[640,384]{1,0:T(8,128)(2,1)S(1)}, bf16[640,384]{1,0:T(8,128)(2,1)S(1)}, u32[]{:S(2)}, u32[]{:S(2)}) %collective-permute-start.21) | collective-permute-done | bytes 491552 | tf_op jit(solution)/shard_map/ppermute | solution.py:357
  94.1 3.8 %second_blocks.3 = (f32[640,384]{1,0:T(8,128)S(1)}, f32[640,384]{1,0:T(8,128)S(1)}, f32[640,384]{1,0:T(8,128)S(1)}) custom-call(s32[32]{0:T(128)S(1)} %pad_add_fusion.ints, bf16[640,1536]{1,0:T(8,128)(2,1)S(1)} %get-tuple-element.50.act_ref, bf16[1536,3072]{1,0:T(8,128)(2,1)S(1)} %bitcast.15), custom_call_target="tpu_custom_call" | custom-call | flops 2264924160 | bytes 5898240 | tf_op jit(solution)/shard_map/second_blocks/pallas_call | solution.py:520
  98.0 3.6 %collective-permute-done.18 = bf16[640,384]{1,0:T(8,128)(2,1)S(1)} collective-permute-done((bf16[640,384]{1,0:T(8,128)(2,1)S(1)}, bf16[640,384]{1,0:T(8,128)(2,1)S(1)}, u32[]{:S(2)}, u32[]{:S(2)}) %collective-permute-start.18) | collective-permute-done | bytes 491552 | tf_op jit(solution)/shard_map/ppermute | solution.py:357
  107.4 4.2 %collective-permute-done.19 = bf16[640,384]{1,0:T(8,128)(2,1)} collective-permute-done((bf16[640,384]{1,0:T(8,128)(2,1)}, bf16[640,384]{1,0:T(8,128)(2,1)}, u32[]{:S(2)}, u32[]{:S(2)}) %collective-permute-start.19) | collective-permute-done | bytes 491552 | tf_op jit(solution)/shard_map/ppermute | solution.py:357
  111.6 4.0 %collective-permute-done.23 = bf16[640,384]{1,0:T(8,128)(2,1)} collective-permute-done((bf16[640,384]{1,0:T(8,128)(2,1)}, bf16[640,384]{1,0:T(8,128)(2,1)}, u32[]{:S(2)}, u32[]{:S(2)}) %collective-permute-start.23) | collective-permute-done | bytes 491552 | tf_op jit(solution)/shard_map/ppermute | solution.py:357
  115.6 2.3 %add_convert_fusion = bf16[640,384]{1,0:T(8,128)(2,1)} fusion(f32[640,384]{1,0:T(8,128)S(1)} %fusion, bf16[640,384]{1,0:T(8,128)(2,1)} %collective-permute-done.23, f32[640,384]{1,0:T(8,128)S(1)} %get-tuple-element.51, bf16[640,384]{1,0:T(8,128)(2,1)} %collective-permute-done.19, bf16[640,384]{1,0:T(8,128)(2,1)S(1)} %copy-done.3, f32[384]{0:T(512)S(1)} %convert_element_type.64), kind=kLoop, calls=%fused_computation | loop fusion | flops 2211840 | bytes 3933696 | tf_op jit(solution)/shard_map/convert_element_type | solution.py:568
  (89 shorter events, 28.5 us)
Async XLA Ops:
  3.6 14.2 %collective-permute-start = (bf16[640,384]{1,0:T(8,128)(2,1)S(1)}, bf16[640,384]{1,0:T(8,128)(2,1)S(1)}, u32[]{:S(2)}, u32[]{:S(2)}) collective-permute-start(bf16[640,384]{1,0:T(8,128)(2,1)S(1)} %get-tuple-element.33.u_ref.refs_0_), channel_id=1, source_target_pairs={{0,4},{4,8},{8,12},{12,14},{14,10},{10,6},{6,2},{2,0},{1,5},{5,9},... | collective-permute-start | bytes 1474568 | tf_op jit(solution)/shard_map/ppermute | solution.py:357
  6.7 13.0 %collective-permute-start.4 = (bf16[640,384]{1,0:T(8,128)(2,1)S(1)}, bf16[640,384]{1,0:T(8,128)(2,1)S(1)}, u32[]{:S(2)}, u32[]{:S(2)}) collective-permute-start(bf16[640,384]{1,0:T(8,128)(2,1)S(1)} %get-tuple-element.33.u_ref.refs_0_), channel_id=1, source_target_pairs={{4,0},{8,4},{12,8},{14,12},{10,14},{6,10},{2,6},{0,2},{5,1},{9,5},... | collective-permute-start | bytes 1474568 | tf_op jit(solution)/shard_map/ppermute | solution.py:357
  10.9 47.8 %collective-permute-start.15 = (bf16[8,64,1536]{2,1,0:T(8,128)(2,1)}, bf16[8,64,1536]{2,1,0:T(8,128)(2,1)}, u32[]{:S(2)}, u32[]{:S(2)}) collective-permute-start(bf16[8,64,1536]{2,1,0:T(8,128)(2,1)} %get-tuple-element.49), channel_id=1, source_target_pairs={{0,1},{1,0},{2,3},{3,2},{4,5},{5,4},{6,7},{7,6},{8,9},{9,8},{10,11... | collective-permute-start | bytes 4718600 | tf_op jit(solution)/shard_map/ppermute | solution.py:409
  11.0 9.5 %collective-permute-start.8 = (bf16[8,64,384]{2,1,0:T(8,128)(2,1)}, bf16[8,64,384]{2,1,0:T(8,128)(2,1)S(1)}, u32[]{:S(2)}, u32[]{:S(2)}) collective-permute-start(bf16[8,64,384]{2,1,0:T(8,128)(2,1)} %get-tuple-element.36), channel_id=1, source_target_pairs={{0,1},{1,0},{2,3},{3,2},{4,5},{5,4},{6,7},{7,6},{8,9},{9,8},{10,11... | collective-permute-start | bytes 1179656 | tf_op jit(solution)/shard_map/ppermute | solution.py:397
  17.8 18.6 %collective-permute-start.1 = (bf16[640,384]{1,0:T(8,128)(2,1)S(1)}, bf16[640,384]{1,0:T(8,128)(2,1)S(1)}, u32[]{:S(2)}, u32[]{:S(2)}) collective-permute-start(bf16[640,384]{1,0:T(8,128)(2,1)S(1)} %collective-permute-done.refs_1_), channel_id=1, source_target_pairs={{0,4},{4,8},{8,12},{12,14},{14,10},{10,6},{6,2},{2,0},{1,5},{5,9},... | collective-permute-start | bytes 1474568 | tf_op jit(solution)/shard_map/ppermute | solution.py:357
  19.6 16.8 %collective-permute-start.5 = (bf16[640,384]{1,0:T(8,128)(2,1)S(1)}, bf16[640,384]{1,0:T(8,128)(2,1)S(1)}, u32[]{:S(2)}, u32[]{:S(2)}) collective-permute-start(bf16[640,384]{1,0:T(8,128)(2,1)S(1)} %collective-permute-done.4.refs_2_), channel_id=1, source_target_pairs={{4,0},{8,4},{12,8},{14,12},{10,14},{6,10},{2,6},{0,2},{5,1},{9,5},... | collective-permute-start | bytes 1474568 | tf_op jit(solution)/shard_map/ppermute | solution.py:357
  23.0 9.9 %collective-permute-start.9 = (bf16[64,640]{1,0:T(8,128)(2,1)S(1)}, bf16[64,640]{1,0:T(8,128)(2,1)S(1)}, u32[]{:S(2)}, u32[]{:S(2)}) collective-permute-start(bf16[64,640]{1,0:T(8,128)(2,1)S(1)} %get-tuple-element.37.refs_0_.after_ref), channel_id=1, source_target_pairs={{0,2},{2,0},{4,6},{6,4},{8,10},{10,8},{12,14},{14,12},{1,3},{3,1},... | collective-permute-start | bytes 245768 | tf_op jit(solution)/shard_map/ppermute | solution.py:357
  24.8 9.0 %collective-permute-start.10 = (f32[32,640]{1,0:T(8,128)S(1)}, f32[32,640]{1,0:T(8,128)S(1)}, u32[]{:S(2)}, u32[]{:S(2)}) collective-permute-start(f32[32,640]{1,0:T(8,128)S(1)} %get-tuple-element.38.refs_1_), channel_id=1, source_target_pairs={{0,2},{2,0},{4,6},{6,4},{8,10},{10,8},{12,14},{14,12},{1,3},{3,1},... | collective-permute-start | bytes 245768 | tf_op jit(solution)/shard_map/ppermute | solution.py:357
  34.3 10.7 %collective-permute-start.11 = (bf16[64,640]{1,0:T(8,128)(2,1)S(1)}, bf16[64,640]{1,0:T(8,128)(2,1)S(1)}, u32[]{:S(2)}, u32[]{:S(2)}) collective-permute-start(bf16[64,640]{1,0:T(8,128)(2,1)S(1)} %get-tuple-element.41.refs_0_), channel_id=1, source_target_pairs={{0,4},{2,6},{4,0},{6,2},{8,12},{10,14},{12,8},{14,10},{1,5},{3,7},... | collective-permute-start | bytes 245768 | tf_op jit(solution)/shard_map/ppermute | solution.py:357
  34.4 10.6 %collective-permute-start.12 = (f32[32,640]{1,0:T(8,128)S(1)}, f32[32,640]{1,0:T(8,128)S(1)}, u32[]{:S(2)}, u32[]{:S(2)}) collective-permute-start(f32[32,640]{1,0:T(8,128)S(1)} %get-tuple-element.42.refs_1_), channel_id=1, source_target_pairs={{0,4},{2,6},{4,0},{6,2},{8,12},{10,14},{12,8},{14,10},{1,5},{3,7},... | collective-permute-start | bytes 245768 | tf_op jit(solution)/shard_map/ppermute | solution.py:357
  36.4 18.5 %collective-permute-start.2 = (bf16[640,384]{1,0:T(8,128)(2,1)S(1)}, bf16[640,384]{1,0:T(8,128)(2,1)S(1)}, u32[]{:S(2)}, u32[]{:S(2)}) collective-permute-start(bf16[640,384]{1,0:T(8,128)(2,1)S(1)} %collective-permute-done.1.refs_3_), channel_id=1, source_target_pairs={{0,4},{4,8},{8,12},{12,14},{14,10},{10,6},{6,2},{2,0},{1,5},{5,9},... | collective-permute-start | bytes 1474568 | tf_op jit(solution)/shard_map/ppermute | solution.py:357
  36.5 20.5 %collective-permute-start.6 = (bf16[640,384]{1,0:T(8,128)(2,1)S(1)}, bf16[640,384]{1,0:T(8,128)(2,1)S(1)}, u32[]{:S(2)}, u32[]{:S(2)}) collective-permute-start(bf16[640,384]{1,0:T(8,128)(2,1)S(1)} %collective-permute-done.5.refs_4_), channel_id=1, source_target_pairs={{4,0},{8,4},{12,8},{14,12},{10,14},{6,10},{2,6},{0,2},{5,1},{9,5},... | collective-permute-start | bytes 1474568 | tf_op jit(solution)/shard_map/ppermute | solution.py:357
  45.5 11.6 %collective-permute-start.13 = (bf16[64,640]{1,0:T(8,128)(2,1)S(1)}, bf16[64,640]{1,0:T(8,128)(2,1)S(1)}, u32[]{:S(2)}, u32[]{:S(2)}) collective-permute-start(bf16[64,640]{1,0:T(8,128)(2,1)S(1)} %get-tuple-element.45.refs_0_), channel_id=1, source_target_pairs={{0,8},{2,10},{4,12},{6,14},{8,0},{10,2},{12,4},{14,6},{1,9},{3,11}... | collective-permute-start | bytes 245768 | tf_op jit(solution)/shard_map/ppermute | solution.py:357
  48.9 8.6 %collective-permute-start.14 = (f32[32,640]{1,0:T(8,128)S(1)}, f32[32,640]{1,0:T(8,128)S(1)}, u32[]{:S(2)}, u32[]{:S(2)}) collective-permute-start(f32[32,640]{1,0:T(8,128)S(1)} %get-tuple-element.46.refs_1_), channel_id=1, source_target_pairs={{0,8},{2,10},{4,12},{6,14},{8,0},{10,2},{12,4},{14,6},{1,9},{3,11}... | collective-permute-start | bytes 245768 | tf_op jit(solution)/shard_map/ppermute | solution.py:357
  54.9 8.5 %collective-permute-start.3 = (bf16[320,384]{1,0:T(8,128)(2,1)S(1)}, bf16[320,384]{1,0:T(8,128)(2,1)S(1)}, u32[]{:S(2)}, u32[]{:S(2)}) collective-permute-start(bf16[320,384]{1,0:T(8,128)(2,1)S(1)} %slice.43), channel_id=1, source_target_pairs={{0,4},{4,8},{8,12},{12,14},{14,10},{10,6},{6,2},{2,0},{1,5},{5,9},... | collective-permute-start | bytes 737288 | tf_op jit(solution)/shard_map/ppermute | solution.py:357
  57.0 6.5 %collective-permute-start.7 = (bf16[320,384]{1,0:T(8,128)(2,1)S(1)}, bf16[320,384]{1,0:T(8,128)(2,1)S(1)}, u32[]{:S(2)}, u32[]{:S(2)}) collective-permute-start(bf16[320,384]{1,0:T(8,128)(2,1)S(1)} %slice.44), channel_id=1, source_target_pairs={{4,0},{8,4},{12,8},{14,12},{10,14},{6,10},{2,6},{0,2},{5,1},{9,5},... | collective-permute-start | bytes 737288 | tf_op jit(solution)/shard_map/ppermute | solution.py:357
  67.7 9.1 %collective-permute-start.16 = (bf16[320,384]{1,0:T(8,128)(2,1)S(1)}, bf16[320,384]{1,0:T(8,128)(2,1)S(1)}, u32[]{:S(2)}, u32[]{:S(2)}) collective-permute-start(bf16[320,384]{1,0:T(8,128)(2,1)S(1)} %get-tuple-element.61), channel_id=1, source_target_pairs={{0,4},{4,8},{8,12},{12,14},{14,10},{10,6},{6,2},{2,0},{1,5},{5,9},... | collective-permute-start | bytes 737288 | tf_op jit(solution)/shard_map/ppermute | solution.py:357
  72.2 8.8 %collective-permute-start.20 = (bf16[320,384]{1,0:T(8,128)(2,1)S(1)}, bf16[320,384]{1,0:T(8,128)(2,1)S(1)}, u32[]{:S(2)}, u32[]{:S(2)}) collective-permute-start(bf16[320,384]{1,0:T(8,128)(2,1)S(1)} %get-tuple-element.62), channel_id=1, source_target_pairs={{4,0},{8,4},{12,8},{14,12},{10,14},{6,10},{2,6},{0,2},{5,1},{9,5},... | collective-permute-start | bytes 737288 | tf_op jit(solution)/shard_map/ppermute | solution.py:357
  76.9 12.4 %collective-permute-start.17 = (bf16[640,384]{1,0:T(8,128)(2,1)S(1)}, bf16[640,384]{1,0:T(8,128)(2,1)S(1)}, u32[]{:S(2)}, u32[]{:S(2)}) collective-permute-start(bf16[640,384]{1,0:T(8,128)(2,1)S(1)} %pad_maximum_fusion), channel_id=1, source_target_pairs={{0,4},{4,8},{8,12},{12,14},{14,10},{10,6},{6,2},{2,0},{1,5},{5,9},... | collective-permute-start | bytes 1474568 | tf_op jit(solution)/shard_map/ppermute | solution.py:357
  81.1 12.3 %collective-permute-start.21 = (bf16[640,384]{1,0:T(8,128)(2,1)S(1)}, bf16[640,384]{1,0:T(8,128)(2,1)S(1)}, u32[]{:S(2)}, u32[]{:S(2)}) collective-permute-start(bf16[640,384]{1,0:T(8,128)(2,1)S(1)} %pad_maximum_fusion.1), channel_id=1, source_target_pairs={{4,0},{8,4},{12,8},{14,12},{10,14},{6,10},{2,6},{0,2},{5,1},{9,5},... | collective-permute-start | bytes 1474568 | tf_op jit(solution)/shard_map/ppermute | solution.py:357
  89.4 12.2 %collective-permute-start.18 = (bf16[640,384]{1,0:T(8,128)(2,1)S(1)}, bf16[640,384]{1,0:T(8,128)(2,1)S(1)}, u32[]{:S(2)}, u32[]{:S(2)}) collective-permute-start(bf16[640,384]{1,0:T(8,128)(2,1)S(1)} %add_convert_fusion.4), channel_id=1, source_target_pairs={{0,4},{4,8},{8,12},{12,14},{14,10},{10,6},{6,2},{2,0},{1,5},{5,9},... | collective-permute-start | bytes 1474568 | tf_op jit(solution)/shard_map/ppermute | solution.py:357
  93.4 12.1 %collective-permute-start.22 = (bf16[640,384]{1,0:T(8,128)(2,1)S(1)}, bf16[640,384]{1,0:T(8,128)(2,1)S(1)}, u32[]{:S(2)}, u32[]{:S(2)}) collective-permute-start(bf16[640,384]{1,0:T(8,128)(2,1)S(1)} %add_convert_fusion.2), channel_id=1, source_target_pairs={{4,0},{8,4},{12,8},{14,12},{10,14},{6,10},{2,6},{0,2},{5,1},{9,5},... | collective-permute-start | bytes 1474568 | tf_op jit(solution)/shard_map/ppermute | solution.py:357
  102.5 9.1 %collective-permute-start.19 = (bf16[640,384]{1,0:T(8,128)(2,1)}, bf16[640,384]{1,0:T(8,128)(2,1)}, u32[]{:S(2)}, u32[]{:S(2)}) collective-permute-start(bf16[640,384]{1,0:T(8,128)(2,1)} %add_convert_fusion.3), channel_id=1, source_target_pairs={{0,4},{4,8},{8,12},{12,14},{14,10},{10,6},{6,2},{2,0},{1,5},{5,9},... | collective-permute-start | bytes 1474568 | tf_op jit(solution)/shard_map/ppermute | solution.py:357
  106.4 9.1 %collective-permute-start.23 = (bf16[640,384]{1,0:T(8,128)(2,1)}, bf16[640,384]{1,0:T(8,128)(2,1)}, u32[]{:S(2)}, u32[]{:S(2)}) collective-permute-start(bf16[640,384]{1,0:T(8,128)(2,1)} %add_convert_fusion.1), channel_id=1, source_target_pairs={{4,0},{8,4},{12,8},{14,12},{10,14},{6,10},{2,6},{0,2},{5,1},{9,5},... | collective-permute-start | bytes 1474568 | tf_op jit(solution)/shard_map/ppermute | solution.py:357
  (14 other events, 110.0 us)

commit v5 on v4

--- a/solution.py
+++ b/solution.py
@@ -396,17 +396,6 @@
     swap = [(s, s ^ 1) for s in range(lax.axis_size("store"))]
     recv_down = lax.ppermute(send_down, "store", swap)
 
-    low, pack = pl.pallas_call(
-        functools.partial(low_kernel, count, stored),
-        in_specs=[SMEM] + [WHOLE] * 6,
-        out_specs=[WHOLE] * 2,
-        out_shape=[like(rank, rows), like(count + 2 * reqs + 8, rows, kind=F32)],
-        scratch_shapes=[pltpu.VMEM((reqs * rank, feat), BF)],
-        compiler_params=params(),
-        cost_estimate=cost(rows * feat * reqs, rows * feat),
-        name="low_rank_parts",
-    )(adapter_per_request, u, hot, stat, mod, mine_down, recv_down)
-    recv_up = lax.ppermute(send_up, "store", swap)
     tail = pl.pallas_call(
         functools.partial(means_kernel, count),
         grid=(count,),
@@ -422,7 +411,19 @@
         compiler_params=params(),
         cost_estimate=cost(64 * count * feat * hidden, 2 * count * feat * hidden, scale=0.1),
         name="means_part",
-    )(mod, first_weight, first_bias.reshape(1, hidden), low)
+    )(mod, first_weight, first_bias.reshape(1, hidden), send_up)
+
+    low, pack = pl.pallas_call(
+        functools.partial(low_kernel, count, stored),
+        in_specs=[SMEM] + [WHOLE] * 6,
+        out_specs=[WHOLE] * 2,
+        out_shape=[like(rank, rows), like(count + 2 * reqs + 8, rows, kind=F32)],
+        scratch_shapes=[pltpu.VMEM((reqs * rank, feat), BF)],
+        compiler_params=params(),
+        cost_estimate=cost(rows * feat * reqs, rows * feat),
+        name="low_rank_parts",
+    )(adapter_per_request, u, hot, stat, mod, mine_down, recv_down)
+    recv_up = lax.ppermute(send_up, "store", swap)
 
     cut = rows // 2
     a = b = u
@@ -430,6 +431,8 @@
     for k in range(1, half):
         a, b = go(a, forth), go(b, back)
         seen += [a, b]
+        if k == 1:
+            a, b, _ = lax.optimization_barrier((a, b, low))
     far_c, far_d = go(a[:cut], forth), go(b[cut:], back)
 
     turn = 0

time: 118 us -> 117 us (level)
  other arithmetic: 4.61 us -> 2.62 us
    ppermute x1, waiting for transfers between devices: 0.01 us -> 1.55 us  [ring_device(): recv_down = lax.ppermute(send_down, 'store', swap)]
    unnamed x28 -> x30, local copies, waits for them, and re-layouts: 7.3 us -> 7.31 us
  transfers between devices with their start and end apart: 24 -> 24, of which waited for: 12 -> 13; matrix products, arithmetic and copies ran while one was open for 3% -> 2% of each run, Pallas kernels for 26% -> 26%
where the time goes in v5:
time: 117 us
  waiting for transfers between devices  43.8 us (37%)
  Pallas kernels  35.7 us (31%)
  starting transfers between devices  25.9 us (22%)
  local copies, waits for them, and re-layouts  8.18 us (7%)
  other arithmetic  2.62 us (2%)
    ppermute x22, waiting for transfers between devices, go(): return lax.ppermute(x, 'tensor', route)  42.3 us
    ppermute x22, starting transfers between devices, go(): return lax.ppermute(x, 'tensor', route)  25.3 us
    pallas_call x3, Pallas kernels, second(): pl.pallas_call(functools.partial(second_kernel, blocks, base), in_specs=[...  9 us
    unnamed x30, local copies, waits for them, and re-layouts  7.31 us
    pallas_call x1, Pallas kernels, ring_device(): pl.pallas_call(functools.partial(first_kernel, count, len(early), 0), in_...  5.89 us
    pallas_call x1, Pallas kernels, ring_device(): pl.pallas_call(functools.partial(lora_kernel, count, len(late), len(early...  4.69 us
    pallas_call x1, Pallas kernels, ring_device(): pl.pallas_call(send_kernel, in_specs=[SMEM, ANY, ANY], out_specs=[WHOLE]...  4.18 us
    pallas_call x1, Pallas kernels, ring_device(): pl.pallas_call(finish_kernel, grid_spec=pltpu.PrefetchScalarGridSpec(num_...  4.06 us
  transfers between devices with their start and end apart: 24, of which 13 were waited for; matrix products, arithmetic and copies ran while one was open for 2% of the time, Pallas kernels for 26%

profile of v5, /device:TPU:0, one launch (start us, length us, event | category | flops | bytes accessed | tf_op | source)
XLA Modules:
  0.0 116.8 jit_solution(89105096441372963)
XLA Ops:
  3.6 3.1 %collective-permute-start = (bf16[640,384]{1,0:T(8,128)(2,1)S(1)}, bf16[640,384]{1,0:T(8,128)(2,1)S(1)}, u32[]{:S(2)}, u32[]{:S(2)}) collective-permute-start(bf16[640,384]{1,0:T(8,128)(2,1)S(1)} %get-tuple-element.35.u_ref.refs_0_), channel_id=1, source_target_pairs={{0,4},{4,8},{8,12},{12,14},{14,10},{10,6},{6,2},{2,0},{1,5},{5,9},... | collective-permute-start | bytes 1474568 | tf_op jit(solution)/shard_map/ppermute | solution.py:357
  6.7 4.2 %adapters_to_send.1 = (bf16[8,64,384]{2,1,0:T(8,128)(2,1)}, bf16[8,64,384]{2,1,0:T(8,128)(2,1)}, bf16[8,64,1536]{2,1,0:T(8,128)(2,1)}) custom-call(s32[2,8]{1,0:T(2,128)} %ids.3, bf16[128,64,384]{2,1,0:T(8,128)(2,1)} %bitcast.20, bf16[128,64,1536]{2,1,0:T(8,128)(2,1)} %refs_7_.1), custom_call_target="tpu_custom_call" | custom-call | bytes 983040 | tf_op jit(solution)/shard_map/adapters_to_send/pallas_call | solution.py:386
  14.0 1.8 %low_rank_parts.1 = (bf16[64,640]{1,0:T(8,128)(2,1)S(1)}, f32[32,640]{1,0:T(8,128)S(1)}) custom-call(s32[2,8]{1,0:T(2,128)S(1)} %copy-done.8, bf16[640,384]{1,0:T(8,128)(2,1)S(1)} %get-tuple-element.35.u_ref.refs_0_, bf16[640,128]{1,0:T(8,128)(2,1)S(1)} %get-tuple-element.34.hot_ref.refs_4_, f32[8,640]{1,0:T(8,128)S(1)} %get-tuple-element.36.stat_ref, ...), custom_call_target="tpu_custom_call" | custom-call | flops 1966080 | bytes 245760 | tf_op jit(solution)/shard_map/low_rank_parts/pallas_call | solution.py:416
  15.9 2.0 %collective-permute-done.refs_1_ = bf16[640,384]{1,0:T(8,128)(2,1)S(1)} collective-permute-done((bf16[640,384]{1,0:T(8,128)(2,1)S(1)}, bf16[640,384]{1,0:T(8,128)(2,1)S(1)}, u32[]{:S(2)}, u32[]{:S(2)}) %collective-permute-start) | collective-permute-done | bytes 491552 | tf_op jit(solution)/shard_map/ppermute | solution.py:357
  24.3 9.5 %collective-permute-done.9.refs_2_ = bf16[64,640]{1,0:T(8,128)(2,1)S(1)} collective-permute-done((bf16[64,640]{1,0:T(8,128)(2,1)S(1)}, bf16[64,640]{1,0:T(8,128)(2,1)S(1)}, u32[]{:S(2)}, u32[]{:S(2)}) %collective-permute-start.9) | collective-permute-done | bytes 81952 | tf_op jit(solution)/shard_map/ppermute | solution.py:357
  35.3 2.0 %collective-permute-start.12 = (f32[32,640]{1,0:T(8,128)S(1)}, f32[32,640]{1,0:T(8,128)S(1)}, u32[]{:S(2)}, u32[]{:S(2)}) collective-permute-start(f32[32,640]{1,0:T(8,128)S(1)} %get-tuple-element.46.refs_1_), channel_id=1, source_target_pairs={{0,4},{2,6},{4,0},{6,2},{8,12},{10,14},{12,8},{14,10},{1,5},{3,7},... | collective-permute-start | bytes 245768 | tf_op jit(solution)/shard_map/ppermute | solution.py:357
  37.4 1.9 %collective-permute-start.7 = (bf16[640,384]{1,0:T(8,128)(2,1)S(1)}, bf16[640,384]{1,0:T(8,128)(2,1)S(1)}, u32[]{:S(2)}, u32[]{:S(2)}) collective-permute-start(bf16[640,384]{1,0:T(8,128)(2,1)S(1)} %collective-permute-done.6.refs_4_), channel_id=1, source_target_pairs={{4,0},{8,4},{12,8},{14,12},{10,14},{6,10},{2,6},{0,2},{5,1},{9,5},... | collective-permute-start | bytes 1474568 | tf_op jit(solution)/shard_map/ppermute | solution.py:357
  39.4 3.7 %copy-done = bf16[3072,1536]{1,0:T(8,128)(2,1)S(1)} copy-done((bf16[3072,1536]{1,0:T(8,128)(2,1)S(1)}, bf16[3072,1536]{1,0:T(8,128)(2,1)}, u32[]{:S(2)}) %copy-start) | copy-done | bytes 9437208
  43.1 2.7 %means_part.1.refs_6_ = bf16[128,1536]{1,0:T(8,128)(2,1)S(1)} custom-call(bf16[3,8,3072]{2,1,0:T(8,128)(2,1)S(1)} %bitcast.18, bf16[3072,1536]{1,0:T(8,128)(2,1)S(1)} %copy-done, bf16[1,1536]{1,0:T(2,128)(2,1)S(1)} %reshape.5.bias_ref, bf16[8,64,1536]{2,1,0:T(8,128)(2,1)S(1)} %copy-done.6), custom_call_target="tpu_custom_call" | custom-call | flops 30198988 | bytes 943718 | tf_op jit(solution)/shard_map/means_part/pallas_call | solution.py:399
  46.4 2.5 %collective-permute-start.13 = (bf16[64,640]{1,0:T(8,128)(2,1)S(1)}, bf16[64,640]{1,0:T(8,128)(2,1)S(1)}, u32[]{:S(2)}, u32[]{:S(2)}) collective-permute-start(bf16[64,640]{1,0:T(8,128)(2,1)S(1)} %get-tuple-element.49.refs_0_), channel_id=1, source_target_pairs={{0,8},{2,10},{4,12},{6,14},{8,0},{10,2},{12,4},{14,6},{1,9},{3,11}... | collective-permute-start | bytes 245768 | tf_op jit(solution)/shard_map/ppermute | solution.py:357
  49.4 5.9 %first_blocks.1.refs_3_ = f32[640,1536]{1,0:T(8,128)S(1)} custom-call(s32[32]{0:T(128)S(1)} %pad_add_fusion.ints, bf16[640,384]{1,0:T(8,128)(2,1)S(1)} %get-tuple-element.35.u_ref.refs_0_, bf16[640,384]{1,0:T(8,128)(2,1)S(1)} %collective-permute-done.refs_1_, bf16[640,384]{1,0:T(8,128)(2,1)S(1)} %collective-permute-done.1.refs_2_, ...), custom_call_target="tpu_custom_call" | custom-call | flops 3774873600 | bytes 5898240 | tf_op jit(solution)/shard_map/first_blocks/pallas_call | solution.py:471
  58.7 4.7 %low_rank_added.1.acc_ref = f32[640,1536]{1,0:T(8,128)S(1)} custom-call(s32[32]{0:T(128)S(1)} %pad_add_fusion.ints, bf16[640,384]{1,0:T(8,128)(2,1)S(1)} %collective-permute-done.4.refs_0_, bf16[640,384]{1,0:T(8,128)(2,1)S(1)} %collective-permute-done.7.refs_1_, bf16[3072,1536]{1,0:T(8,128)(2,1)S(1)} %copy-done.1, f32[640,1536]{1,0:T(8,128)S(1)} %first_blocks.1.refs_3_, ...), custom_call_target="tpu_custom_call" | custom-call | flops 2516582400 | bytes 2359296 | tf_op jit(solution)/shard_map/low_rank_added/pallas_call | solution.py:481
  63.5 4.1 %finish_first.1 = (bf16[640,1536]{1,0:T(8,128)(2,1)S(1)}, bf16[640,384]{1,0:T(8,128)(2,1)S(1)}) custom-call(s32[32]{0:T(128)S(1)} %pad_add_fusion.ints, bf16[320,384]{1,0:T(8,128)(2,1)S(1)} %collective-permute-done.5.c_ref, bf16[320,384]{1,0:T(8,128)(2,1)S(1)} %collective-permute-done.8.d_ref, f32[640,128]{1,0:T(8,128)S(1)} %get-tuple-element.51.refs_5_.col_ref, ...), custom_call_target="tpu_custom_call" | custom-call | flops 1509949440 | bytes 13762560 | tf_op jit(solution)/shard_map/finish_first/pallas_call | solution.py:501
  67.6 1.8 %collective-permute-start.16 = (bf16[320,384]{1,0:T(8,128)(2,1)S(1)}, bf16[320,384]{1,0:T(8,128)(2,1)S(1)}, u32[]{:S(2)}, u32[]{:S(2)}) collective-permute-start(bf16[320,384]{1,0:T(8,128)(2,1)S(1)} %get-tuple-element.65), channel_id=1, source_target_pairs={{0,4},{4,8},{8,12},{12,14},{14,10},{10,6},{6,2},{2,0},{1,5},{5,9},... | collective-permute-start | bytes 737288 | tf_op jit(solution)/shard_map/ppermute | solution.py:357
  69.4 2.6 %second_blocks.5 = (f32[640,384]{1,0:T(8,128)S(1)}, f32[640,384]{1,0:T(8,128)S(1)}) custom-call(s32[32]{0:T(128)S(1)} %pad_add_fusion.ints, bf16[640,1536]{1,0:T(8,128)(2,1)S(1)} %get-tuple-element.54.act_ref, bf16[1536,3072]{1,0:T(8,128)(2,1)S(1)} %bitcast.15), custom_call_target="tpu_custom_call" | custom-call | flops 1509949440 | bytes 3932160 | tf_op jit(solution)/shard_map/second_blocks/pallas_call | solution.py:523
  72.6 4.1 %collective-permute-done.16 = bf16[320,384]{1,0:T(8,128)(2,1)S(1)} collective-permute-done((bf16[320,384]{1,0:T(8,128)(2,1)S(1)}, bf16[320,384]{1,0:T(8,128)(2,1)S(1)}, u32[]{:S(2)}, u32[]{:S(2)}) %collective-permute-start.16) | collective-permute-done | bytes 245792 | tf_op jit(solution)/shard_map/ppermute | solution.py:357
  78.4 2.5 %collective-permute-done.20 = bf16[320,384]{1,0:T(8,128)(2,1)S(1)} collective-permute-done((bf16[320,384]{1,0:T(8,128)(2,1)S(1)}, bf16[320,384]{1,0:T(8,128)(2,1)S(1)}, u32[]{:S(2)}, u32[]{:S(2)}) %collective-permute-start.20) | collective-permute-done | bytes 245792 | tf_op jit(solution)/shard_map/ppermute | solution.py:357
  81.6 2.6 %second_blocks.4 = (f32[640,384]{1,0:T(8,128)S(1)}, f32[640,384]{1,0:T(8,128)S(1)}) custom-call(s32[32]{0:T(128)S(1)} %pad_add_fusion.ints, bf16[640,1536]{1,0:T(8,128)(2,1)S(1)} %get-tuple-element.54.act_ref, bf16[1536,3072]{1,0:T(8,128)(2,1)S(1)} %bitcast.15), custom_call_target="tpu_custom_call" | custom-call | flops 1509949440 | bytes 3932160 | tf_op jit(solution)/shard_map/second_blocks/pallas_call | solution.py:523
  84.2 5.2 %collective-permute-done.17 = bf16[640,384]{1,0:T(8,128)(2,1)S(1)} collective-permute-done((bf16[640,384]{1,0:T(8,128)(2,1)S(1)}, bf16[640,384]{1,0:T(8,128)(2,1)S(1)}, u32[]{:S(2)}, u32[]{:S(2)}) %collective-permute-start.17) | collective-permute-done | bytes 491552 | tf_op jit(solution)/shard_map/ppermute | solution.py:357
  90.9 2.5 %collective-permute-done.21 = bf16[640,384]{1,0:T(8,128)(2,1)S(1)} collective-permute-done((bf16[640,384]{1,0:T(8,128)(2,1)S(1)}, bf16[640,384]{1,0:T(8,128)(2,1)S(1)}, u32[]{:S(2)}, u32[]{:S(2)}) %collective-permute-start.21) | collective-permute-done | bytes 491552 | tf_op jit(solution)/shard_map/ppermute | solution.py:357
  94.3 3.8 %second_blocks.3 = (f32[640,384]{1,0:T(8,128)S(1)}, f32[640,384]{1,0:T(8,128)S(1)}, f32[640,384]{1,0:T(8,128)S(1)}) custom-call(s32[32]{0:T(128)S(1)} %pad_add_fusion.ints, bf16[640,1536]{1,0:T(8,128)(2,1)S(1)} %get-tuple-element.54.act_ref, bf16[1536,3072]{1,0:T(8,128)(2,1)S(1)} %bitcast.15), custom_call_target="tpu_custom_call" | custom-call | flops 2264924160 | bytes 5898240 | tf_op jit(solution)/shard_map/second_blocks/pallas_call | solution.py:523
  98.1 4.7 %collective-permute-done.18 = bf16[640,384]{1,0:T(8,128)(2,1)S(1)} collective-permute-done((bf16[640,384]{1,0:T(8,128)(2,1)S(1)}, bf16[640,384]{1,0:T(8,128)(2,1)S(1)}, u32[]{:S(2)}, u32[]{:S(2)}) %collective-permute-start.18) | collective-permute-done | bytes 491552 | tf_op jit(solution)/shard_map/ppermute | solution.py:357
  107.9 4.2 %collective-permute-done.19 = bf16[640,384]{1,0:T(8,128)(2,1)S(1)} collective-permute-done((bf16[640,384]{1,0:T(8,128)(2,1)S(1)}, bf16[640,384]{1,0:T(8,128)(2,1)S(1)}, u32[]{:S(2)}, u32[]{:S(2)}) %collective-permute-start.19) | collective-permute-done | bytes 491552 | tf_op jit(solution)/shard_map/ppermute | solution.py:357
  112.1 3.7 %collective-permute-done.23 = bf16[640,384]{1,0:T(8,128)(2,1)S(1)} collective-permute-done((bf16[640,384]{1,0:T(8,128)(2,1)}, bf16[640,384]{1,0:T(8,128)(2,1)S(1)}, u32[]{:S(2)}, u32[]{:S(2)}) %collective-permute-start.23) | collective-permute-done | bytes 491552 | tf_op jit(solution)/shard_map/ppermute | solution.py:357
  (91 shorter events, 30.8 us)
Async XLA Ops:
  3.6 14.2 %collective-permute-start = (bf16[640,384]{1,0:T(8,128)(2,1)S(1)}, bf16[640,384]{1,0:T(8,128)(2,1)S(1)}, u32[]{:S(2)}, u32[]{:S(2)}) collective-permute-start(bf16[640,384]{1,0:T(8,128)(2,1)S(1)} %get-tuple-element.35.u_ref.refs_0_), channel_id=1, source_target_pairs={{0,4},{4,8},{8,12},{12,14},{14,10},{10,6},{6,2},{2,0},{1,5},{5,9},... | collective-permute-start | bytes 1474568 | tf_op jit(solution)/shard_map/ppermute | solution.py:357
  6.7 12.7 %collective-permute-start.1 = (bf16[640,384]{1,0:T(8,128)(2,1)S(1)}, bf16[640,384]{1,0:T(8,128)(2,1)S(1)}, u32[]{:S(2)}, u32[]{:S(2)}) collective-permute-start(bf16[640,384]{1,0:T(8,128)(2,1)S(1)} %get-tuple-element.35.u_ref.refs_0_), channel_id=1, source_target_pairs={{4,0},{8,4},{12,8},{14,12},{10,14},{6,10},{2,6},{0,2},{5,1},{9,5},... | collective-permute-start | bytes 1474568 | tf_op jit(solution)/shard_map/ppermute | solution.py:357
  10.9 2.1 %collective-permute-start.2 = (bf16[8,64,384]{2,1,0:T(8,128)(2,1)}, bf16[8,64,384]{2,1,0:T(8,128)(2,1)}, u32[]{:S(2)}, u32[]{:S(2)}) collective-permute-start(bf16[8,64,384]{2,1,0:T(8,128)(2,1)} %get-tuple-element.38), channel_id=1, source_target_pairs={{0,1},{1,0},{2,3},{3,2},{4,5},{5,4},{6,7},{7,6},{8,9},{9,8},{10,11... | collective-permute-start | bytes 1179656 | tf_op jit(solution)/shard_map/ppermute | solution.py:397
  11.0 47.7 %collective-permute-start.15 = (bf16[8,64,1536]{2,1,0:T(8,128)(2,1)}, bf16[8,64,1536]{2,1,0:T(8,128)(2,1)}, u32[]{:S(2)}, u32[]{:S(2)}) collective-permute-start(bf16[8,64,1536]{2,1,0:T(8,128)(2,1)} %get-tuple-element.53.after_ref), channel_id=1, source_target_pairs={{0,1},{1,0},{2,3},{3,2},{4,5},{5,4},{6,7},{7,6},{8,9},{9,8},{10,11... | collective-permute-start | bytes 4718600 | tf_op jit(solution)/shard_map/ppermute | solution.py:426
  19.3 17.9 %collective-permute-start.3 = (bf16[640,384]{1,0:T(8,128)(2,1)S(1)}, bf16[640,384]{1,0:T(8,128)(2,1)S(1)}, u32[]{:S(2)}, u32[]{:S(2)}) collective-permute-start(bf16[640,384]{1,0:T(8,128)(2,1)S(1)} %collective-permute-done.refs_1_), channel_id=1, source_target_pairs={{0,4},{4,8},{8,12},{12,14},{14,10},{10,6},{6,2},{2,0},{1,5},{5,9},... | collective-permute-start | bytes 1474568 | tf_op jit(solution)/shard_map/ppermute | solution.py:357
  20.9 16.4 %collective-permute-start.6 = (bf16[640,384]{1,0:T(8,128)(2,1)S(1)}, bf16[640,384]{1,0:T(8,128)(2,1)S(1)}, u32[]{:S(2)}, u32[]{:S(2)}) collective-permute-start(bf16[640,384]{1,0:T(8,128)(2,1)S(1)} %collective-permute-done.1.refs_2_), channel_id=1, source_target_pairs={{4,0},{8,4},{12,8},{14,12},{10,14},{6,10},{2,6},{0,2},{5,1},{9,5},... | collective-permute-start | bytes 1474568 | tf_op jit(solution)/shard_map/ppermute | solution.py:357
  22.1 11.7 %collective-permute-start.9 = (bf16[64,640]{1,0:T(8,128)(2,1)S(1)}, bf16[64,640]{1,0:T(8,128)(2,1)S(1)}, u32[]{:S(2)}, u32[]{:S(2)}) collective-permute-start(bf16[64,640]{1,0:T(8,128)(2,1)S(1)} %get-tuple-element.39.refs_0_), channel_id=1, source_target_pairs={{0,2},{2,0},{4,6},{6,4},{8,10},{10,8},{12,14},{14,12},{1,3},{3,1},... | collective-permute-start | bytes 245768 | tf_op jit(solution)/shard_map/ppermute | solution.py:357
  22.4 12.2 %collective-permute-start.10 = (f32[32,640]{1,0:T(8,128)S(1)}, f32[32,640]{1,0:T(8,128)S(1)}, u32[]{:S(2)}, u32[]{:S(2)}) collective-permute-start(f32[32,640]{1,0:T(8,128)S(1)} %get-tuple-element.42.refs_1_), channel_id=1, source_target_pairs={{0,2},{2,0},{4,6},{6,4},{8,10},{10,8},{12,14},{14,12},{1,3},{3,1},... | collective-permute-start | bytes 245768 | tf_op jit(solution)/shard_map/ppermute | solution.py:357
  35.2 10.7 %collective-permute-start.11 = (bf16[64,640]{1,0:T(8,128)(2,1)S(1)}, bf16[64,640]{1,0:T(8,128)(2,1)S(1)}, u32[]{:S(2)}, u32[]{:S(2)}) collective-permute-start(bf16[64,640]{1,0:T(8,128)(2,1)S(1)} %get-tuple-element.45.refs_0_), channel_id=1, source_target_pairs={{0,4},{2,6},{4,0},{6,2},{8,12},{10,14},{12,8},{14,10},{1,5},{3,7},... | collective-permute-start | bytes 245768 | tf_op jit(solution)/shard_map/ppermute | solution.py:357
  35.3 10.6 %collective-permute-start.12 = (f32[32,640]{1,0:T(8,128)S(1)}, f32[32,640]{1,0:T(8,128)S(1)}, u32[]{:S(2)}, u32[]{:S(2)}) collective-permute-start(f32[32,640]{1,0:T(8,128)S(1)} %get-tuple-element.46.refs_1_), channel_id=1, source_target_pairs={{0,4},{2,6},{4,0},{6,2},{8,12},{10,14},{12,8},{14,10},{1,5},{3,7},... | collective-permute-start | bytes 245768 | tf_op jit(solution)/shard_map/ppermute | solution.py:357
  37.3 18.0 %collective-permute-start.4 = (bf16[640,384]{1,0:T(8,128)(2,1)S(1)}, bf16[640,384]{1,0:T(8,128)(2,1)S(1)}, u32[]{:S(2)}, u32[]{:S(2)}) collective-permute-start(bf16[640,384]{1,0:T(8,128)(2,1)S(1)} %collective-permute-done.3.refs_3_), channel_id=1, source_target_pairs={{0,4},{4,8},{8,12},{12,14},{14,10},{10,6},{6,2},{2,0},{1,5},{5,9},... | collective-permute-start | bytes 1474568 | tf_op jit(solution)/shard_map/ppermute | solution.py:357
  37.4 19.6 %collective-permute-start.7 = (bf16[640,384]{1,0:T(8,128)(2,1)S(1)}, bf16[640,384]{1,0:T(8,128)(2,1)S(1)}, u32[]{:S(2)}, u32[]{:S(2)}) collective-permute-start(bf16[640,384]{1,0:T(8,128)(2,1)S(1)} %collective-permute-done.6.refs_4_), channel_id=1, source_target_pairs={{4,0},{8,4},{12,8},{14,12},{10,14},{6,10},{2,6},{0,2},{5,1},{9,5},... | collective-permute-start | bytes 1474568 | tf_op jit(solution)/shard_map/ppermute | solution.py:357
  46.4 11.1 %collective-permute-start.13 = (bf16[64,640]{1,0:T(8,128)(2,1)S(1)}, bf16[64,640]{1,0:T(8,128)(2,1)S(1)}, u32[]{:S(2)}, u32[]{:S(2)}) collective-permute-start(bf16[64,640]{1,0:T(8,128)(2,1)S(1)} %get-tuple-element.49.refs_0_), channel_id=1, source_target_pairs={{0,8},{2,10},{4,12},{6,14},{8,0},{10,2},{12,4},{14,6},{1,9},{3,11}... | collective-permute-start | bytes 245768 | tf_op jit(solution)/shard_map/ppermute | solution.py:357
  48.9 8.6 %collective-permute-start.14 = (f32[32,640]{1,0:T(8,128)S(1)}, f32[32,640]{1,0:T(8,128)S(1)}, u32[]{:S(2)}, u32[]{:S(2)}) collective-permute-start(f32[32,640]{1,0:T(8,128)S(1)} %get-tuple-element.50.refs_1_), channel_id=1, source_target_pairs={{0,8},{2,10},{4,12},{6,14},{8,0},{10,2},{12,4},{14,6},{1,9},{3,11}... | collective-permute-start | bytes 245768 | tf_op jit(solution)/shard_map/ppermute | solution.py:357
  55.3 8.1 %collective-permute-start.5 = (bf16[320,384]{1,0:T(8,128)(2,1)S(1)}, bf16[320,384]{1,0:T(8,128)(2,1)S(1)}, u32[]{:S(2)}, u32[]{:S(2)}) collective-permute-start(bf16[320,384]{1,0:T(8,128)(2,1)S(1)} %slice.43), channel_id=1, source_target_pairs={{0,4},{4,8},{8,12},{12,14},{14,10},{10,6},{6,2},{2,0},{1,5},{5,9},... | collective-permute-start | bytes 737288 | tf_op jit(solution)/shard_map/ppermute | solution.py:357
  57.0 6.5 %collective-permute-start.8 = (bf16[320,384]{1,0:T(8,128)(2,1)S(1)}, bf16[320,384]{1,0:T(8,128)(2,1)S(1)}, u32[]{:S(2)}, u32[]{:S(2)}) collective-permute-start(bf16[320,384]{1,0:T(8,128)(2,1)S(1)} %slice.44), channel_id=1, source_target_pairs={{4,0},{8,4},{12,8},{14,12},{10,14},{6,10},{2,6},{0,2},{5,1},{9,5},... | collective-permute-start | bytes 737288 | tf_op jit(solution)/shard_map/ppermute | solution.py:357
  67.6 9.1 %collective-permute-start.16 = (bf16[320,384]{1,0:T(8,128)(2,1)S(1)}, bf16[320,384]{1,0:T(8,128)(2,1)S(1)}, u32[]{:S(2)}, u32[]{:S(2)}) collective-permute-start(bf16[320,384]{1,0:T(8,128)(2,1)S(1)} %get-tuple-element.65), channel_id=1, source_target_pairs={{0,4},{4,8},{8,12},{12,14},{14,10},{10,6},{6,2},{2,0},{1,5},{5,9},... | collective-permute-start | bytes 737288 | tf_op jit(solution)/shard_map/ppermute | solution.py:357
  72.0 8.9 %collective-permute-start.20 = (bf16[320,384]{1,0:T(8,128)(2,1)S(1)}, bf16[320,384]{1,0:T(8,128)(2,1)S(1)}, u32[]{:S(2)}, u32[]{:S(2)}) collective-permute-start(bf16[320,384]{1,0:T(8,128)(2,1)S(1)} %get-tuple-element.66), channel_id=1, source_target_pairs={{4,0},{8,4},{12,8},{14,12},{10,14},{6,10},{2,6},{0,2},{5,1},{9,5},... | collective-permute-start | bytes 737288 | tf_op jit(solution)/shard_map/ppermute | solution.py:357
  76.8 12.6 %collective-permute-start.17 = (bf16[640,384]{1,0:T(8,128)(2,1)S(1)}, bf16[640,384]{1,0:T(8,128)(2,1)S(1)}, u32[]{:S(2)}, u32[]{:S(2)}) collective-permute-start(bf16[640,384]{1,0:T(8,128)(2,1)S(1)} %pad_maximum_fusion), channel_id=1, source_target_pairs={{0,4},{4,8},{8,12},{12,14},{14,10},{10,6},{6,2},{2,0},{1,5},{5,9},... | collective-permute-start | bytes 1474568 | tf_op jit(solution)/shard_map/ppermute | solution.py:357
  81.0 12.4 %collective-permute-start.21 = (bf16[640,384]{1,0:T(8,128)(2,1)S(1)}, bf16[640,384]{1,0:T(8,128)(2,1)S(1)}, u32[]{:S(2)}, u32[]{:S(2)}) collective-permute-start(bf16[640,384]{1,0:T(8,128)(2,1)S(1)} %pad_maximum_fusion.1), channel_id=1, source_target_pairs={{4,0},{8,4},{12,8},{14,12},{10,14},{6,10},{2,6},{0,2},{5,1},{9,5},... | collective-permute-start | bytes 1474568 | tf_op jit(solution)/shard_map/ppermute | solution.py:357
  89.4 13.4 %collective-permute-start.18 = (bf16[640,384]{1,0:T(8,128)(2,1)S(1)}, bf16[640,384]{1,0:T(8,128)(2,1)S(1)}, u32[]{:S(2)}, u32[]{:S(2)}) collective-permute-start(bf16[640,384]{1,0:T(8,128)(2,1)S(1)} %add_convert_fusion.4), channel_id=1, source_target_pairs={{0,4},{4,8},{8,12},{12,14},{14,10},{10,6},{6,2},{2,0},{1,5},{5,9},... | collective-permute-start | bytes 1474568 | tf_op jit(solution)/shard_map/ppermute | solution.py:357
  93.5 12.3 %collective-permute-start.22 = (bf16[640,384]{1,0:T(8,128)(2,1)S(1)}, bf16[640,384]{1,0:T(8,128)(2,1)S(1)}, u32[]{:S(2)}, u32[]{:S(2)}) collective-permute-start(bf16[640,384]{1,0:T(8,128)(2,1)S(1)} %add_convert_fusion.2), channel_id=1, source_target_pairs={{4,0},{8,4},{12,8},{14,12},{10,14},{6,10},{2,6},{0,2},{5,1},{9,5},... | collective-permute-start | bytes 1474568 | tf_op jit(solution)/shard_map/ppermute | solution.py:357
  103.0 9.1 %collective-permute-start.19 = (bf16[640,384]{1,0:T(8,128)(2,1)S(1)}, bf16[640,384]{1,0:T(8,128)(2,1)S(1)}, u32[]{:S(2)}, u32[]{:S(2)}) collective-permute-start(bf16[640,384]{1,0:T(8,128)(2,1)S(1)} %add_convert_fusion.3), channel_id=1, source_target_pairs={{0,4},{4,8},{8,12},{12,14},{14,10},{10,6},{6,2},{2,0},{1,5},{5,9},... | collective-permute-start | bytes 1474568 | tf_op jit(solution)/shard_map/ppermute | solution.py:357
  106.7 9.0 %collective-permute-start.23 = (bf16[640,384]{1,0:T(8,128)(2,1)}, bf16[640,384]{1,0:T(8,128)(2,1)S(1)}, u32[]{:S(2)}, u32[]{:S(2)}) collective-permute-start(bf16[640,384]{1,0:T(8,128)(2,1)} %add_convert_fusion.1), channel_id=1, source_target_pairs={{4,0},{8,4},{12,8},{14,12},{10,14},{6,10},{2,6},{0,2},{5,1},{9,5},... | collective-permute-start | bytes 1474568 | tf_op jit(solution)/shard_map/ppermute | solution.py:357
  (15 other events, 128.9 us)

commit v6 on v5

--- a/solution.py
+++ b/solution.py
@@ -494,7 +494,7 @@
             2 * rows * hidden * (feat * len(late) + reqs * rank), 2 * feat * hidden * len(late), scale=1),
         name="low_rank_added",
     )(ints, *late, first_weight, acc, wide, cols, tail, adapter_up_matrices, recv_up)
-    steps = 4
+    steps = 2
     tile = rows // steps
     last = count - 1
     tiled = lambda width: pl.BlockSpec((tile, width), lambda i, *s: (i, 0))

time: 117 us -> 117 us (level)
  no operation moved by 1% of the time
where the time goes in v6:
time: 117 us; the launch traced here: 116 us
  waiting for transfers between devices  43.9 us (38%)
  Pallas kernels  35.2 us (30%)
  starting transfers between devices  25.9 us (22%)
  local copies, waits for them, and re-layouts  8.18 us (7%)
  other arithmetic  2.62 us (2%)
    ppermute x22, waiting for transfers between devices, go(): return lax.ppermute(x, 'tensor', route)  42.3 us
    ppermute x22, starting transfers between devices, go(): return lax.ppermute(x, 'tensor', route)  25.3 us
    pallas_call x3, Pallas kernels, second(): pl.pallas_call(functools.partial(second_kernel, blocks, base), in_specs=[...  9.01 us
    unnamed x30, local copies, waits for them, and re-layouts  7.31 us
    pallas_call x1, Pallas kernels, ring_device(): pl.pallas_call(functools.partial(first_kernel, count, len(early), 0), in_...  5.89 us
    pallas_call x1, Pallas kernels, ring_device(): pl.pallas_call(functools.partial(lora_kernel, count, len(late), len(early...  4.69 us
    pallas_call x1, Pallas kernels, ring_device(): pl.pallas_call(send_kernel, in_specs=[SMEM, ANY, ANY], out_specs=[WHOLE]...  4.18 us
    pallas_call x1, Pallas kernels, ring_device(): pl.pallas_call(finish_kernel, grid_spec=pltpu.PrefetchScalarGridSpec(num_...  3.6 us
  transfers between devices with their start and end apart: 24, of which 13 were waited for; matrix products, arithmetic and copies ran while one was open for 2% of the time, Pallas kernels for 26%

profile of v6, /device:TPU:0, one launch (start us, length us, event | category | flops | bytes accessed | tf_op | source)
XLA Modules:
  0.0 116.4 jit_solution(15155455859672412264)
XLA Ops:
  3.6 3.1 %collective-permute-start = (bf16[640,384]{1,0:T(8,128)(2,1)S(1)}, bf16[640,384]{1,0:T(8,128)(2,1)S(1)}, u32[]{:S(2)}, u32[]{:S(2)}) collective-permute-start(bf16[640,384]{1,0:T(8,128)(2,1)S(1)} %get-tuple-element.35.u_ref.refs_0_), channel_id=1, source_target_pairs={{0,4},{4,8},{8,12},{12,14},{14,10},{10,6},{6,2},{2,0},{1,5},{5,9},... | collective-permute-start | bytes 1474568 | tf_op jit(solution)/shard_map/ppermute | solution.py:357
  6.7 4.2 %adapters_to_send.1 = (bf16[8,64,384]{2,1,0:T(8,128)(2,1)}, bf16[8,64,384]{2,1,0:T(8,128)(2,1)}, bf16[8,64,1536]{2,1,0:T(8,128)(2,1)}) custom-call(s32[2,8]{1,0:T(2,128)} %ids.3, bf16[128,64,384]{2,1,0:T(8,128)(2,1)} %bitcast.20, bf16[128,64,1536]{2,1,0:T(8,128)(2,1)} %refs_7_.1), custom_call_target="tpu_custom_call" | custom-call | bytes 983040 | tf_op jit(solution)/shard_map/adapters_to_send/pallas_call | solution.py:386
  14.0 1.8 %low_rank_parts.1 = (bf16[64,640]{1,0:T(8,128)(2,1)S(1)}, f32[32,640]{1,0:T(8,128)S(1)}) custom-call(s32[2,8]{1,0:T(2,128)S(1)} %copy-done.8, bf16[640,384]{1,0:T(8,128)(2,1)S(1)} %get-tuple-element.35.u_ref.refs_0_, bf16[640,128]{1,0:T(8,128)(2,1)S(1)} %get-tuple-element.34.hot_ref.refs_4_, f32[8,640]{1,0:T(8,128)S(1)} %get-tuple-element.36.stat_ref, ...), custom_call_target="tpu_custom_call" | custom-call | flops 1966080 | bytes 245760 | tf_op jit(solution)/shard_map/low_rank_parts/pallas_call | solution.py:416
  15.9 2.0 %collective-permute-done.refs_1_ = bf16[640,384]{1,0:T(8,128)(2,1)S(1)} collective-permute-done((bf16[640,384]{1,0:T(8,128)(2,1)S(1)}, bf16[640,384]{1,0:T(8,128)(2,1)S(1)}, u32[]{:S(2)}, u32[]{:S(2)}) %collective-permute-start) | collective-permute-done | bytes 491552 | tf_op jit(solution)/shard_map/ppermute | solution.py:357
  24.3 9.5 %collective-permute-done.9.refs_2_ = bf16[64,640]{1,0:T(8,128)(2,1)S(1)} collective-permute-done((bf16[64,640]{1,0:T(8,128)(2,1)S(1)}, bf16[64,640]{1,0:T(8,128)(2,1)S(1)}, u32[]{:S(2)}, u32[]{:S(2)}) %collective-permute-start.9) | collective-permute-done | bytes 81952 | tf_op jit(solution)/shard_map/ppermute | solution.py:357
  35.3 2.0 %collective-permute-start.12 = (f32[32,640]{1,0:T(8,128)S(1)}, f32[32,640]{1,0:T(8,128)S(1)}, u32[]{:S(2)}, u32[]{:S(2)}) collective-permute-start(f32[32,640]{1,0:T(8,128)S(1)} %get-tuple-element.46.refs_1_), channel_id=1, source_target_pairs={{0,4},{2,6},{4,0},{6,2},{8,12},{10,14},{12,8},{14,10},{1,5},{3,7},... | collective-permute-start | bytes 245768 | tf_op jit(solution)/shard_map/ppermute | solution.py:357
  37.4 1.9 %collective-permute-start.7 = (bf16[640,384]{1,0:T(8,128)(2,1)S(1)}, bf16[640,384]{1,0:T(8,128)(2,1)S(1)}, u32[]{:S(2)}, u32[]{:S(2)}) collective-permute-start(bf16[640,384]{1,0:T(8,128)(2,1)S(1)} %collective-permute-done.6.refs_4_), channel_id=1, source_target_pairs={{4,0},{8,4},{12,8},{14,12},{10,14},{6,10},{2,6},{0,2},{5,1},{9,5},... | collective-permute-start | bytes 1474568 | tf_op jit(solution)/shard_map/ppermute | solution.py:357
  39.4 3.7 %copy-done = bf16[3072,1536]{1,0:T(8,128)(2,1)S(1)} copy-done((bf16[3072,1536]{1,0:T(8,128)(2,1)S(1)}, bf16[3072,1536]{1,0:T(8,128)(2,1)}, u32[]{:S(2)}) %copy-start) | copy-done | bytes 9437208
  43.1 2.7 %means_part.1.refs_6_ = bf16[128,1536]{1,0:T(8,128)(2,1)S(1)} custom-call(bf16[3,8,3072]{2,1,0:T(8,128)(2,1)S(1)} %bitcast.18, bf16[3072,1536]{1,0:T(8,128)(2,1)S(1)} %copy-done, bf16[1,1536]{1,0:T(2,128)(2,1)S(1)} %reshape.5.bias_ref, bf16[8,64,1536]{2,1,0:T(8,128)(2,1)S(1)} %copy-done.6), custom_call_target="tpu_custom_call" | custom-call | flops 30198988 | bytes 943718 | tf_op jit(solution)/shard_map/means_part/pallas_call | solution.py:399
  46.4 2.5 %collective-permute-start.13 = (bf16[64,640]{1,0:T(8,128)(2,1)S(1)}, bf16[64,640]{1,0:T(8,128)(2,1)S(1)}, u32[]{:S(2)}, u32[]{:S(2)}) collective-permute-start(bf16[64,640]{1,0:T(8,128)(2,1)S(1)} %get-tuple-element.49.refs_0_), channel_id=1, source_target_pairs={{0,8},{2,10},{4,12},{6,14},{8,0},{10,2},{12,4},{14,6},{1,9},{3,11}... | collective-permute-start | bytes 245768 | tf_op jit(solution)/shard_map/ppermute | solution.py:357
  49.4 5.9 %first_blocks.1.refs_3_ = f32[640,1536]{1,0:T(8,128)S(1)} custom-call(s32[32]{0:T(128)S(1)} %pad_add_fusion.ints, bf16[640,384]{1,0:T(8,128)(2,1)S(1)} %get-tuple-element.35.u_ref.refs_0_, bf16[640,384]{1,0:T(8,128)(2,1)S(1)} %collective-permute-done.refs_1_, bf16[640,384]{1,0:T(8,128)(2,1)S(1)} %collective-permute-done.1.refs_2_, ...), custom_call_target="tpu_custom_call" | custom-call | flops 3774873600 | bytes 5898240 | tf_op jit(solution)/shard_map/first_blocks/pallas_call | solution.py:471
  58.7 4.7 %low_rank_added.1.acc_ref = f32[640,1536]{1,0:T(8,128)S(1)} custom-call(s32[32]{0:T(128)S(1)} %pad_add_fusion.ints, bf16[640,384]{1,0:T(8,128)(2,1)S(1)} %collective-permute-done.4.refs_0_, bf16[640,384]{1,0:T(8,128)(2,1)S(1)} %collective-permute-done.7.refs_1_, bf16[3072,1536]{1,0:T(8,128)(2,1)S(1)} %copy-done.1, f32[640,1536]{1,0:T(8,128)S(1)} %first_blocks.1.refs_3_, ...), custom_call_target="tpu_custom_call" | custom-call | flops 2516582400 | bytes 2359296 | tf_op jit(solution)/shard_map/low_rank_added/pallas_call | solution.py:481
  63.5 3.6 %finish_first.1 = (bf16[640,1536]{1,0:T(8,128)(2,1)S(1)}, bf16[640,384]{1,0:T(8,128)(2,1)S(1)}) custom-call(s32[32]{0:T(128)S(1)} %pad_add_fusion.ints, bf16[320,384]{1,0:T(8,128)(2,1)S(1)} %collective-permute-done.5.c_ref, bf16[320,384]{1,0:T(8,128)(2,1)S(1)} %collective-permute-done.8.d_ref, f32[640,128]{1,0:T(8,128)S(1)} %get-tuple-element.51.refs_5_.col_ref, ...), custom_call_target="tpu_custom_call" | custom-call | flops 1509949440 | bytes 13762560 | tf_op jit(solution)/shard_map/finish_first/pallas_call | solution.py:501
  67.2 1.8 %collective-permute-start.16 = (bf16[320,384]{1,0:T(8,128)(2,1)S(1)}, bf16[320,384]{1,0:T(8,128)(2,1)S(1)}, u32[]{:S(2)}, u32[]{:S(2)}) collective-permute-start(bf16[320,384]{1,0:T(8,128)(2,1)S(1)} %get-tuple-element.65), channel_id=1, source_target_pairs={{0,4},{4,8},{8,12},{12,14},{14,10},{10,6},{6,2},{2,0},{1,5},{5,9},... | collective-permute-start | bytes 737288 | tf_op jit(solution)/shard_map/ppermute | solution.py:357
  68.9 2.6 %second_blocks.5 = (f32[640,384]{1,0:T(8,128)S(1)}, f32[640,384]{1,0:T(8,128)S(1)}) custom-call(s32[32]{0:T(128)S(1)} %pad_add_fusion.ints, bf16[640,1536]{1,0:T(8,128)(2,1)S(1)} %get-tuple-element.54.act_ref, bf16[1536,3072]{1,0:T(8,128)(2,1)S(1)} %bitcast.15), custom_call_target="tpu_custom_call" | custom-call | flops 1509949440 | bytes 3932160 | tf_op jit(solution)/shard_map/second_blocks/pallas_call | solution.py:523
  72.2 4.1 %collective-permute-done.16 = bf16[320,384]{1,0:T(8,128)(2,1)S(1)} collective-permute-done((bf16[320,384]{1,0:T(8,128)(2,1)S(1)}, bf16[320,384]{1,0:T(8,128)(2,1)S(1)}, u32[]{:S(2)}, u32[]{:S(2)}) %collective-permute-start.16) | collective-permute-done | bytes 245792 | tf_op jit(solution)/shard_map/ppermute | solution.py:357
  77.9 2.5 %collective-permute-done.20 = bf16[320,384]{1,0:T(8,128)(2,1)S(1)} collective-permute-done((bf16[320,384]{1,0:T(8,128)(2,1)S(1)}, bf16[320,384]{1,0:T(8,128)(2,1)S(1)}, u32[]{:S(2)}, u32[]{:S(2)}) %collective-permute-start.20) | collective-permute-done | bytes 245792 | tf_op jit(solution)/shard_map/ppermute | solution.py:357
  81.1 2.6 %second_blocks.4 = (f32[640,384]{1,0:T(8,128)S(1)}, f32[640,384]{1,0:T(8,128)S(1)}) custom-call(s32[32]{0:T(128)S(1)} %pad_add_fusion.ints, bf16[640,1536]{1,0:T(8,128)(2,1)S(1)} %get-tuple-element.54.act_ref, bf16[1536,3072]{1,0:T(8,128)(2,1)S(1)} %bitcast.15), custom_call_target="tpu_custom_call" | custom-call | flops 1509949440 | bytes 3932160 | tf_op jit(solution)/shard_map/second_blocks/pallas_call | solution.py:523
  83.7 5.2 %collective-permute-done.17 = bf16[640,384]{1,0:T(8,128)(2,1)S(1)} collective-permute-done((bf16[640,384]{1,0:T(8,128)(2,1)S(1)}, bf16[640,384]{1,0:T(8,128)(2,1)S(1)}, u32[]{:S(2)}, u32[]{:S(2)}) %collective-permute-start.17) | collective-permute-done | bytes 491552 | tf_op jit(solution)/shard_map/ppermute | solution.py:357
  90.5 2.5 %collective-permute-done.21 = bf16[640,384]{1,0:T(8,128)(2,1)S(1)} collective-permute-done((bf16[640,384]{1,0:T(8,128)(2,1)S(1)}, bf16[640,384]{1,0:T(8,128)(2,1)S(1)}, u32[]{:S(2)}, u32[]{:S(2)}) %collective-permute-start.21) | collective-permute-done | bytes 491552 | tf_op jit(solution)/shard_map/ppermute | solution.py:357
  93.8 3.8 %second_blocks.3 = (f32[640,384]{1,0:T(8,128)S(1)}, f32[640,384]{1,0:T(8,128)S(1)}, f32[640,384]{1,0:T(8,128)S(1)}) custom-call(s32[32]{0:T(128)S(1)} %pad_add_fusion.ints, bf16[640,1536]{1,0:T(8,128)(2,1)S(1)} %get-tuple-element.54.act_ref, bf16[1536,3072]{1,0:T(8,128)(2,1)S(1)} %bitcast.15), custom_call_target="tpu_custom_call" | custom-call | flops 2264924160 | bytes 5898240 | tf_op jit(solution)/shard_map/second_blocks/pallas_call | solution.py:523
  97.7 4.8 %collective-permute-done.18 = bf16[640,384]{1,0:T(8,128)(2,1)S(1)} collective-permute-done((bf16[640,384]{1,0:T(8,128)(2,1)S(1)}, bf16[640,384]{1,0:T(8,128)(2,1)S(1)}, u32[]{:S(2)}, u32[]{:S(2)}) %collective-permute-start.18) | collective-permute-done | bytes 491552 | tf_op jit(solution)/shard_map/ppermute | solution.py:357
  107.4 4.2 %collective-permute-done.19 = bf16[640,384]{1,0:T(8,128)(2,1)S(1)} collective-permute-done((bf16[640,384]{1,0:T(8,128)(2,1)S(1)}, bf16[640,384]{1,0:T(8,128)(2,1)S(1)}, u32[]{:S(2)}, u32[]{:S(2)}) %collective-permute-start.19) | collective-permute-done | bytes 491552 | tf_op jit(solution)/shard_map/ppermute | solution.py:357
  111.6 3.7 %collective-permute-done.23 = bf16[640,384]{1,0:T(8,128)(2,1)S(1)} collective-permute-done((bf16[640,384]{1,0:T(8,128)(2,1)}, bf16[640,384]{1,0:T(8,128)(2,1)S(1)}, u32[]{:S(2)}, u32[]{:S(2)}) %collective-permute-start.23) | collective-permute-done | bytes 491552 | tf_op jit(solution)/shard_map/ppermute | solution.py:357
  (91 shorter events, 30.7 us)
Async XLA Ops:
  3.6 14.2 %collective-permute-start = (bf16[640,384]{1,0:T(8,128)(2,1)S(1)}, bf16[640,384]{1,0:T(8,128)(2,1)S(1)}, u32[]{:S(2)}, u32[]{:S(2)}) collective-permute-start(bf16[640,384]{1,0:T(8,128)(2,1)S(1)} %get-tuple-element.35.u_ref.refs_0_), channel_id=1, source_target_pairs={{0,4},{4,8},{8,12},{12,14},{14,10},{10,6},{6,2},{2,0},{1,5},{5,9},... | collective-permute-start | bytes 1474568 | tf_op jit(solution)/shard_map/ppermute | solution.py:357
  6.7 12.7 %collective-permute-start.1 = (bf16[640,384]{1,0:T(8,128)(2,1)S(1)}, bf16[640,384]{1,0:T(8,128)(2,1)S(1)}, u32[]{:S(2)}, u32[]{:S(2)}) collective-permute-start(bf16[640,384]{1,0:T(8,128)(2,1)S(1)} %get-tuple-element.35.u_ref.refs_0_), channel_id=1, source_target_pairs={{4,0},{8,4},{12,8},{14,12},{10,14},{6,10},{2,6},{0,2},{5,1},{9,5},... | collective-permute-start | bytes 1474568 | tf_op jit(solution)/shard_map/ppermute | solution.py:357
  10.9 2.1 %collective-permute-start.2 = (bf16[8,64,384]{2,1,0:T(8,128)(2,1)}, bf16[8,64,384]{2,1,0:T(8,128)(2,1)}, u32[]{:S(2)}, u32[]{:S(2)}) collective-permute-start(bf16[8,64,384]{2,1,0:T(8,128)(2,1)} %get-tuple-element.38), channel_id=1, source_target_pairs={{0,1},{1,0},{2,3},{3,2},{4,5},{5,4},{6,7},{7,6},{8,9},{9,8},{10,11... | collective-permute-start | bytes 1179656 | tf_op jit(solution)/shard_map/ppermute | solution.py:397
  11.0 47.7 %collective-permute-start.15 = (bf16[8,64,1536]{2,1,0:T(8,128)(2,1)}, bf16[8,64,1536]{2,1,0:T(8,128)(2,1)}, u32[]{:S(2)}, u32[]{:S(2)}) collective-permute-start(bf16[8,64,1536]{2,1,0:T(8,128)(2,1)} %get-tuple-element.53.after_ref), channel_id=1, source_target_pairs={{0,1},{1,0},{2,3},{3,2},{4,5},{5,4},{6,7},{7,6},{8,9},{9,8},{10,11... | collective-permute-start | bytes 4718600 | tf_op jit(solution)/shard_map/ppermute | solution.py:426
  19.3 17.9 %collective-permute-start.3 = (bf16[640,384]{1,0:T(8,128)(2,1)S(1)}, bf16[640,384]{1,0:T(8,128)(2,1)S(1)}, u32[]{:S(2)}, u32[]{:S(2)}) collective-permute-start(bf16[640,384]{1,0:T(8,128)(2,1)S(1)} %collective-permute-done.refs_1_), channel_id=1, source_target_pairs={{0,4},{4,8},{8,12},{12,14},{14,10},{10,6},{6,2},{2,0},{1,5},{5,9},... | collective-permute-start | bytes 1474568 | tf_op jit(solution)/shard_map/ppermute | solution.py:357
  20.9 16.4 %collective-permute-start.6 = (bf16[640,384]{1,0:T(8,128)(2,1)S(1)}, bf16[640,384]{1,0:T(8,128)(2,1)S(1)}, u32[]{:S(2)}, u32[]{:S(2)}) collective-permute-start(bf16[640,384]{1,0:T(8,128)(2,1)S(1)} %collective-permute-done.1.refs_2_), channel_id=1, source_target_pairs={{4,0},{8,4},{12,8},{14,12},{10,14},{6,10},{2,6},{0,2},{5,1},{9,5},... | collective-permute-start | bytes 1474568 | tf_op jit(solution)/shard_map/ppermute | solution.py:357
  22.1 11.7 %collective-permute-start.9 = (bf16[64,640]{1,0:T(8,128)(2,1)S(1)}, bf16[64,640]{1,0:T(8,128)(2,1)S(1)}, u32[]{:S(2)}, u32[]{:S(2)}) collective-permute-start(bf16[64,640]{1,0:T(8,128)(2,1)S(1)} %get-tuple-element.39.refs_0_), channel_id=1, source_target_pairs={{0,2},{2,0},{4,6},{6,4},{8,10},{10,8},{12,14},{14,12},{1,3},{3,1},... | collective-permute-start | bytes 245768 | tf_op jit(solution)/shard_map/ppermute | solution.py:357
  22.4 12.2 %collective-permute-start.10 = (f32[32,640]{1,0:T(8,128)S(1)}, f32[32,640]{1,0:T(8,128)S(1)}, u32[]{:S(2)}, u32[]{:S(2)}) collective-permute-start(f32[32,640]{1,0:T(8,128)S(1)} %get-tuple-element.42.refs_1_), channel_id=1, source_target_pairs={{0,2},{2,0},{4,6},{6,4},{8,10},{10,8},{12,14},{14,12},{1,3},{3,1},... | collective-permute-start | bytes 245768 | tf_op jit(solution)/shard_map/ppermute | solution.py:357
  35.2 10.7 %collective-permute-start.11 = (bf16[64,640]{1,0:T(8,128)(2,1)S(1)}, bf16[64,640]{1,0:T(8,128)(2,1)S(1)}, u32[]{:S(2)}, u32[]{:S(2)}) collective-permute-start(bf16[64,640]{1,0:T(8,128)(2,1)S(1)} %get-tuple-element.45.refs_0_), channel_id=1, source_target_pairs={{0,4},{2,6},{4,0},{6,2},{8,12},{10,14},{12,8},{14,10},{1,5},{3,7},... | collective-permute-start | bytes 245768 | tf_op jit(solution)/shard_map/ppermute | solution.py:357
  35.3 10.6 %collective-permute-start.12 = (f32[32,640]{1,0:T(8,128)S(1)}, f32[32,640]{1,0:T(8,128)S(1)}, u32[]{:S(2)}, u32[]{:S(2)}) collective-permute-start(f32[32,640]{1,0:T(8,128)S(1)} %get-tuple-element.46.refs_1_), channel_id=1, source_target_pairs={{0,4},{2,6},{4,0},{6,2},{8,12},{10,14},{12,8},{14,10},{1,5},{3,7},... | collective-permute-start | bytes 245768 | tf_op jit(solution)/shard_map/ppermute | solution.py:357
  37.3 18.0 %collective-permute-start.4 = (bf16[640,384]{1,0:T(8,128)(2,1)S(1)}, bf16[640,384]{1,0:T(8,128)(2,1)S(1)}, u32[]{:S(2)}, u32[]{:S(2)}) collective-permute-start(bf16[640,384]{1,0:T(8,128)(2,1)S(1)} %collective-permute-done.3.refs_3_), channel_id=1, source_target_pairs={{0,4},{4,8},{8,12},{12,14},{14,10},{10,6},{6,2},{2,0},{1,5},{5,9},... | collective-permute-start | bytes 1474568 | tf_op jit(solution)/shard_map/ppermute | solution.py:357
  37.4 19.6 %collective-permute-start.7 = (bf16[640,384]{1,0:T(8,128)(2,1)S(1)}, bf16[640,384]{1,0:T(8,128)(2,1)S(1)}, u32[]{:S(2)}, u32[]{:S(2)}) collective-permute-start(bf16[640,384]{1,0:T(8,128)(2,1)S(1)} %collective-permute-done.6.refs_4_), channel_id=1, source_target_pairs={{4,0},{8,4},{12,8},{14,12},{10,14},{6,10},{2,6},{0,2},{5,1},{9,5},... | collective-permute-start | bytes 1474568 | tf_op jit(solution)/shard_map/ppermute | solution.py:357
  46.4 11.1 %collective-permute-start.13 = (bf16[64,640]{1,0:T(8,128)(2,1)S(1)}, bf16[64,640]{1,0:T(8,128)(2,1)S(1)}, u32[]{:S(2)}, u32[]{:S(2)}) collective-permute-start(bf16[64,640]{1,0:T(8,128)(2,1)S(1)} %get-tuple-element.49.refs_0_), channel_id=1, source_target_pairs={{0,8},{2,10},{4,12},{6,14},{8,0},{10,2},{12,4},{14,6},{1,9},{3,11}... | collective-permute-start | bytes 245768 | tf_op jit(solution)/shard_map/ppermute | solution.py:357
  48.9 8.6 %collective-permute-start.14 = (f32[32,640]{1,0:T(8,128)S(1)}, f32[32,640]{1,0:T(8,128)S(1)}, u32[]{:S(2)}, u32[]{:S(2)}) collective-permute-start(f32[32,640]{1,0:T(8,128)S(1)} %get-tuple-element.50.refs_1_), channel_id=1, source_target_pairs={{0,8},{2,10},{4,12},{6,14},{8,0},{10,2},{12,4},{14,6},{1,9},{3,11}... | collective-permute-start | bytes 245768 | tf_op jit(solution)/shard_map/ppermute | solution.py:357
  55.3 8.1 %collective-permute-start.5 = (bf16[320,384]{1,0:T(8,128)(2,1)S(1)}, bf16[320,384]{1,0:T(8,128)(2,1)S(1)}, u32[]{:S(2)}, u32[]{:S(2)}) collective-permute-start(bf16[320,384]{1,0:T(8,128)(2,1)S(1)} %slice.43), channel_id=1, source_target_pairs={{0,4},{4,8},{8,12},{12,14},{14,10},{10,6},{6,2},{2,0},{1,5},{5,9},... | collective-permute-start | bytes 737288 | tf_op jit(solution)/shard_map/ppermute | solution.py:357
  57.0 6.5 %collective-permute-start.8 = (bf16[320,384]{1,0:T(8,128)(2,1)S(1)}, bf16[320,384]{1,0:T(8,128)(2,1)S(1)}, u32[]{:S(2)}, u32[]{:S(2)}) collective-permute-start(bf16[320,384]{1,0:T(8,128)(2,1)S(1)} %slice.44), channel_id=1, source_target_pairs={{4,0},{8,4},{12,8},{14,12},{10,14},{6,10},{2,6},{0,2},{5,1},{9,5},... | collective-permute-start | bytes 737288 | tf_op jit(solution)/shard_map/ppermute | solution.py:357
  67.2 9.1 %collective-permute-start.16 = (bf16[320,384]{1,0:T(8,128)(2,1)S(1)}, bf16[320,384]{1,0:T(8,128)(2,1)S(1)}, u32[]{:S(2)}, u32[]{:S(2)}) collective-permute-start(bf16[320,384]{1,0:T(8,128)(2,1)S(1)} %get-tuple-element.65), channel_id=1, source_target_pairs={{0,4},{4,8},{8,12},{12,14},{14,10},{10,6},{6,2},{2,0},{1,5},{5,9},... | collective-permute-start | bytes 737288 | tf_op jit(solution)/shard_map/ppermute | solution.py:357
  71.6 8.9 %collective-permute-start.20 = (bf16[320,384]{1,0:T(8,128)(2,1)S(1)}, bf16[320,384]{1,0:T(8,128)(2,1)S(1)}, u32[]{:S(2)}, u32[]{:S(2)}) collective-permute-start(bf16[320,384]{1,0:T(8,128)(2,1)S(1)} %get-tuple-element.66), channel_id=1, source_target_pairs={{4,0},{8,4},{12,8},{14,12},{10,14},{6,10},{2,6},{0,2},{5,1},{9,5},... | collective-permute-start | bytes 737288 | tf_op jit(solution)/shard_map/ppermute | solution.py:357
  76.3 12.6 %collective-permute-start.17 = (bf16[640,384]{1,0:T(8,128)(2,1)S(1)}, bf16[640,384]{1,0:T(8,128)(2,1)S(1)}, u32[]{:S(2)}, u32[]{:S(2)}) collective-permute-start(bf16[640,384]{1,0:T(8,128)(2,1)S(1)} %pad_maximum_fusion), channel_id=1, source_target_pairs={{0,4},{4,8},{8,12},{12,14},{14,10},{10,6},{6,2},{2,0},{1,5},{5,9},... | collective-permute-start | bytes 1474568 | tf_op jit(solution)/shard_map/ppermute | solution.py:357
  80.6 12.4 %collective-permute-start.21 = (bf16[640,384]{1,0:T(8,128)(2,1)S(1)}, bf16[640,384]{1,0:T(8,128)(2,1)S(1)}, u32[]{:S(2)}, u32[]{:S(2)}) collective-permute-start(bf16[640,384]{1,0:T(8,128)(2,1)S(1)} %pad_maximum_fusion.1), channel_id=1, source_target_pairs={{4,0},{8,4},{12,8},{14,12},{10,14},{6,10},{2,6},{0,2},{5,1},{9,5},... | collective-permute-start | bytes 1474568 | tf_op jit(solution)/shard_map/ppermute | solution.py:357
  89.0 13.4 %collective-permute-start.18 = (bf16[640,384]{1,0:T(8,128)(2,1)S(1)}, bf16[640,384]{1,0:T(8,128)(2,1)S(1)}, u32[]{:S(2)}, u32[]{:S(2)}) collective-permute-start(bf16[640,384]{1,0:T(8,128)(2,1)S(1)} %add_convert_fusion.4), channel_id=1, source_target_pairs={{0,4},{4,8},{8,12},{12,14},{14,10},{10,6},{6,2},{2,0},{1,5},{5,9},... | collective-permute-start | bytes 1474568 | tf_op jit(solution)/shard_map/ppermute | solution.py:357
  93.1 12.3 %collective-permute-start.22 = (bf16[640,384]{1,0:T(8,128)(2,1)S(1)}, bf16[640,384]{1,0:T(8,128)(2,1)S(1)}, u32[]{:S(2)}, u32[]{:S(2)}) collective-permute-start(bf16[640,384]{1,0:T(8,128)(2,1)S(1)} %add_convert_fusion.2), channel_id=1, source_target_pairs={{4,0},{8,4},{12,8},{14,12},{10,14},{6,10},{2,6},{0,2},{5,1},{9,5},... | collective-permute-start | bytes 1474568 | tf_op jit(solution)/shard_map/ppermute | solution.py:357
  102.5 9.1 %collective-permute-start.19 = (bf16[640,384]{1,0:T(8,128)(2,1)S(1)}, bf16[640,384]{1,0:T(8,128)(2,1)S(1)}, u32[]{:S(2)}, u32[]{:S(2)}) collective-permute-start(bf16[640,384]{1,0:T(8,128)(2,1)S(1)} %add_convert_fusion.3), channel_id=1, source_target_pairs={{0,4},{4,8},{8,12},{12,14},{14,10},{10,6},{6,2},{2,0},{1,5},{5,9},... | collective-permute-start | bytes 1474568 | tf_op jit(solution)/shard_map/ppermute | solution.py:357
  106.2 9.0 %collective-permute-start.23 = (bf16[640,384]{1,0:T(8,128)(2,1)}, bf16[640,384]{1,0:T(8,128)(2,1)S(1)}, u32[]{:S(2)}, u32[]{:S(2)}) collective-permute-start(bf16[640,384]{1,0:T(8,128)(2,1)} %add_convert_fusion.1), channel_id=1, source_target_pairs={{4,0},{8,4},{12,8},{14,12},{10,14},{6,10},{2,6},{0,2},{5,1},{9,5},... | collective-permute-start | bytes 1474568 | tf_op jit(solution)/shard_map/ppermute | solution.py:357
  (15 other events, 128.9 us)

commit v7 on v6

--- a/solution.py
+++ b/solution.py
@@ -378,7 +378,7 @@
         in_specs=[SMEM, WHOLE, WHOLE],
         out_specs=[WHOLE] * 3,
         out_shape=[like(rows, feat), like(rows, 128), like(8, rows, kind=F32)],
-        compiler_params=params(),
+        compiler_params=params(60),
         cost_estimate=cost(2 * rows * feat, rows * feat),
         name="own_features",
     )(tokens_per_request, tokens, mod)
@@ -530,7 +530,7 @@
                 pltpu.SemaphoreType.DMA((blocks,)),
             ],
             compiler_params=params(16),
-            cost_estimate=cost(2 * rows * hidden * feat * blocks, blocks * rows * feat * 8),
+            cost_estimate=cost(rows * hidden * feat * blocks // 2, blocks * rows * feat),
             name=name,
         )(ints, act, second_weight)
 

time: 117 us -> 117 us (level)
  local copies, waits for them, and re-layouts: 8.18 us -> 5.6 us
  other arithmetic: 2.62 us -> 4.42 us
  Pallas kernels: 35.2 us -> 36.5 us
    unnamed x30, local copies, waits for them, and re-layouts: 7.31 us -> 4.73 us
    pallas_call x1, Pallas kernels: 1.01 us -> 2.26 us  [ring_device(): pl.pallas_call(own_kernel, in_specs=[SMEM, WHOLE, WHOLE], out_specs=[WHOL...]
  transfers between devices with their start and end apart: 24 -> 24, of which waited for: 13 -> 13; matrix products, arithmetic and copies ran while one was open for 2% -> 3% of each run, Pallas kernels for 26% -> 26%
where the time goes in v7:
time: 117 us; the launch traced here: 116 us
  waiting for transfers between devices  43.4 us (37%)
  Pallas kernels  36.5 us (31%)
  starting transfers between devices  25.8 us (22%)
  local copies, waits for them, and re-layouts  5.6 us (5%)
  other arithmetic  4.42 us (4%)
    ppermute x22, waiting for transfers between devices, go(): return lax.ppermute(x, 'tensor', route)  41.8 us
    ppermute x22, starting transfers between devices, go(): return lax.ppermute(x, 'tensor', route)  25.2 us
    pallas_call x3, Pallas kernels, second(): pl.pallas_call(functools.partial(second_kernel, blocks, base), in_specs=[...  9 us
    pallas_call x1, Pallas kernels, ring_device(): pl.pallas_call(functools.partial(first_kernel, count, len(early), 0), in_...  5.89 us
    unnamed x30, local copies, waits for them, and re-layouts  4.73 us
    pallas_call x1, Pallas kernels, ring_device(): pl.pallas_call(functools.partial(lora_kernel, count, len(late), len(early...  4.7 us
    pallas_call x1, Pallas kernels, ring_device(): pl.pallas_call(send_kernel, in_specs=[SMEM, ANY, ANY], out_specs=[WHOLE]...  4.23 us
    pallas_call x1, Pallas kernels, ring_device(): pl.pallas_call(finish_kernel, grid_spec=pltpu.PrefetchScalarGridSpec(num_...  3.6 us
  transfers between devices with their start and end apart: 24, of which 13 were waited for; matrix products, arithmetic and copies ran while one was open for 3% of the time, Pallas kernels for 26%

profile of v7, /device:TPU:0, one launch (start us, length us, event | category | flops | bytes accessed | tf_op | source)
XLA Modules:
  0.0 116.3 jit_solution(8976063904501854416)
XLA Ops:
  0.0 2.3 %own_features.1 = (bf16[640,384]{1,0:T(8,128)(2,1)}, bf16[640,128]{1,0:T(8,128)(2,1)}, f32[8,640]{1,0:T(8,128)}) custom-call(s32[1,8]{1,0:T(1,128)} %lengths.1, bf16[640,384]{1,0:T(8,128)(2,1)} %x_ref.1, bf16[3,8,3072]{2,1,0:T(8,128)(2,1)} %bitcast.16), custom_call_target="tpu_custom_call" | custom-call | flops 491520 | bytes 245760 | tf_op jit(solution)/shard_map/own_features/pallas_call | solution.py:376
  2.3 3.0 %collective-permute-start = (bf16[640,384]{1,0:T(8,128)(2,1)}, bf16[640,384]{1,0:T(8,128)(2,1)S(1)}, u32[]{:S(2)}, u32[]{:S(2)}) collective-permute-start(bf16[640,384]{1,0:T(8,128)(2,1)} %get-tuple-element.35.u_ref.refs_0_), channel_id=1, source_target_pairs={{0,4},{4,8},{8,12},{12,14},{14,10},{10,6},{6,2},{2,0},{1,5},{5,9},... | collective-permute-start | bytes 1474568 | tf_op jit(solution)/shard_map/ppermute | solution.py:357
  5.3 4.2 %adapters_to_send.1 = (bf16[8,64,384]{2,1,0:T(8,128)(2,1)}, bf16[8,64,384]{2,1,0:T(8,128)(2,1)}, bf16[8,64,1536]{2,1,0:T(8,128)(2,1)}) custom-call(s32[2,8]{1,0:T(2,128)} %ids.3, bf16[128,64,384]{2,1,0:T(8,128)(2,1)} %bitcast.20, bf16[128,64,1536]{2,1,0:T(8,128)(2,1)} %refs_7_.1), custom_call_target="tpu_custom_call" | custom-call | bytes 983040 | tf_op jit(solution)/shard_map/adapters_to_send/pallas_call | solution.py:386
  14.6 2.0 %collective-permute-done.refs_1_ = bf16[640,384]{1,0:T(8,128)(2,1)S(1)} collective-permute-done((bf16[640,384]{1,0:T(8,128)(2,1)}, bf16[640,384]{1,0:T(8,128)(2,1)S(1)}, u32[]{:S(2)}, u32[]{:S(2)}) %collective-permute-start) | collective-permute-done | bytes 491552 | tf_op jit(solution)/shard_map/ppermute | solution.py:357
  23.1 9.5 %collective-permute-done.9.refs_2_ = bf16[64,640]{1,0:T(8,128)(2,1)S(1)} collective-permute-done((bf16[64,640]{1,0:T(8,128)(2,1)S(1)}, bf16[64,640]{1,0:T(8,128)(2,1)S(1)}, u32[]{:S(2)}, u32[]{:S(2)}) %collective-permute-start.9) | collective-permute-done | bytes 81952 | tf_op jit(solution)/shard_map/ppermute | solution.py:357
  34.1 2.0 %collective-permute-start.12 = (f32[32,640]{1,0:T(8,128)S(1)}, f32[32,640]{1,0:T(8,128)S(1)}, u32[]{:S(2)}, u32[]{:S(2)}) collective-permute-start(f32[32,640]{1,0:T(8,128)S(1)} %get-tuple-element.46.refs_1_), channel_id=1, source_target_pairs={{0,4},{2,6},{4,0},{6,2},{8,12},{10,14},{12,8},{14,10},{1,5},{3,7},... | collective-permute-start | bytes 245768 | tf_op jit(solution)/shard_map/ppermute | solution.py:357
  36.2 1.9 %collective-permute-start.7 = (bf16[640,384]{1,0:T(8,128)(2,1)S(1)}, bf16[640,384]{1,0:T(8,128)(2,1)S(1)}, u32[]{:S(2)}, u32[]{:S(2)}) collective-permute-start(bf16[640,384]{1,0:T(8,128)(2,1)S(1)} %collective-permute-done.6.refs_4_), channel_id=1, source_target_pairs={{4,0},{8,4},{12,8},{14,12},{10,14},{6,10},{2,6},{0,2},{5,1},{9,5},... | collective-permute-start | bytes 1474568 | tf_op jit(solution)/shard_map/ppermute | solution.py:357
  38.2 3.7 %copy-done = bf16[3072,1536]{1,0:T(8,128)(2,1)S(1)} copy-done((bf16[3072,1536]{1,0:T(8,128)(2,1)S(1)}, bf16[3072,1536]{1,0:T(8,128)(2,1)}, u32[]{:S(2)}) %copy-start) | copy-done | bytes 9437208
  41.9 2.7 %means_part.1.refs_6_ = bf16[128,1536]{1,0:T(8,128)(2,1)S(1)} custom-call(bf16[3,8,3072]{2,1,0:T(8,128)(2,1)S(1)} %bitcast.18, bf16[3072,1536]{1,0:T(8,128)(2,1)S(1)} %copy-done, bf16[1,1536]{1,0:T(2,128)(2,1)S(1)} %reshape.5.bias_ref, bf16[8,64,1536]{2,1,0:T(8,128)(2,1)S(1)} %copy-done.4), custom_call_target="tpu_custom_call" | custom-call | flops 30198988 | bytes 943718 | tf_op jit(solution)/shard_map/means_part/pallas_call | solution.py:399
  45.2 2.5 %collective-permute-start.13 = (bf16[64,640]{1,0:T(8,128)(2,1)S(1)}, bf16[64,640]{1,0:T(8,128)(2,1)S(1)}, u32[]{:S(2)}, u32[]{:S(2)}) collective-permute-start(bf16[64,640]{1,0:T(8,128)(2,1)S(1)} %get-tuple-element.49.refs_0_), channel_id=1, source_target_pairs={{0,8},{2,10},{4,12},{6,14},{8,0},{10,2},{12,4},{14,6},{1,9},{3,11}... | collective-permute-start | bytes 245768 | tf_op jit(solution)/shard_map/ppermute | solution.py:357
  48.2 5.9 %first_blocks.1.refs_3_ = f32[640,1536]{1,0:T(8,128)S(1)} custom-call(s32[32]{0:T(128)S(1)} %pad_add_fusion.ints, bf16[640,384]{1,0:T(8,128)(2,1)S(1)} %copy-done.2, bf16[640,384]{1,0:T(8,128)(2,1)S(1)} %collective-permute-done.refs_1_, bf16[640,384]{1,0:T(8,128)(2,1)S(1)} %collective-permute-done.1.refs_2_, ...), custom_call_target="tpu_custom_call" | custom-call | flops 3774873600 | bytes 5898240 | tf_op jit(solution)/shard_map/first_blocks/pallas_call | solution.py:471
  57.6 4.7 %low_rank_added.1.acc_ref = f32[640,1536]{1,0:T(8,128)S(1)} custom-call(s32[32]{0:T(128)S(1)} %pad_add_fusion.ints, bf16[640,384]{1,0:T(8,128)(2,1)S(1)} %collective-permute-done.4.refs_0_, bf16[640,384]{1,0:T(8,128)(2,1)S(1)} %collective-permute-done.7.refs_1_, bf16[3072,1536]{1,0:T(8,128)(2,1)S(1)} %copy-done.1, f32[640,1536]{1,0:T(8,128)S(1)} %first_blocks.1.refs_3_, ...), custom_call_target="tpu_custom_call" | custom-call | flops 2516582400 | bytes 2359296 | tf_op jit(solution)/shard_map/low_rank_added/pallas_call | solution.py:481
  62.3 3.6 %finish_first.1 = (bf16[640,1536]{1,0:T(8,128)(2,1)S(1)}, bf16[640,384]{1,0:T(8,128)(2,1)S(1)}) custom-call(s32[32]{0:T(128)S(1)} %pad_add_fusion.ints, bf16[320,384]{1,0:T(8,128)(2,1)S(1)} %collective-permute-done.5.c_ref, bf16[320,384]{1,0:T(8,128)(2,1)S(1)} %collective-permute-done.8.d_ref, f32[640,128]{1,0:T(8,128)S(1)} %get-tuple-element.51.refs_5_.col_ref, ...), custom_call_target="tpu_custom_call" | custom-call | flops 1509949440 | bytes 13762560 | tf_op jit(solution)/shard_map/finish_first/pallas_call | solution.py:501
  67.8 2.6 %second_blocks.5 = (f32[640,384]{1,0:T(8,128)S(1)}, f32[640,384]{1,0:T(8,128)S(1)}) custom-call(s32[32]{0:T(128)S(1)} %pad_add_fusion.ints, bf16[640,1536]{1,0:T(8,128)(2,1)S(1)} %get-tuple-element.54.act_ref, bf16[1536,3072]{1,0:T(8,128)(2,1)S(1)} %bitcast.15), custom_call_target="tpu_custom_call" | custom-call | flops 377487360 | bytes 491520 | tf_op jit(solution)/shard_map/second_blocks/pallas_call | solution.py:523
  71.0 4.1 %collective-permute-done.16 = bf16[320,384]{1,0:T(8,128)(2,1)S(1)} collective-permute-done((bf16[320,384]{1,0:T(8,128)(2,1)S(1)}, bf16[320,384]{1,0:T(8,128)(2,1)S(1)}, u32[]{:S(2)}, u32[]{:S(2)}) %collective-permute-start.16) | collective-permute-done | bytes 245792 | tf_op jit(solution)/shard_map/ppermute | solution.py:357
  76.8 2.5 %collective-permute-done.20 = bf16[320,384]{1,0:T(8,128)(2,1)S(1)} collective-permute-done((bf16[320,384]{1,0:T(8,128)(2,1)S(1)}, bf16[320,384]{1,0:T(8,128)(2,1)S(1)}, u32[]{:S(2)}, u32[]{:S(2)}) %collective-permute-start.20) | collective-permute-done | bytes 245792 | tf_op jit(solution)/shard_map/ppermute | solution.py:357
  79.9 2.6 %second_blocks.4 = (f32[640,384]{1,0:T(8,128)S(1)}, f32[640,384]{1,0:T(8,128)S(1)}) custom-call(s32[32]{0:T(128)S(1)} %pad_add_fusion.ints, bf16[640,1536]{1,0:T(8,128)(2,1)S(1)} %get-tuple-element.54.act_ref, bf16[1536,3072]{1,0:T(8,128)(2,1)S(1)} %bitcast.15), custom_call_target="tpu_custom_call" | custom-call | flops 377487360 | bytes 491520 | tf_op jit(solution)/shard_map/second_blocks/pallas_call | solution.py:523
  82.5 5.2 %collective-permute-done.17 = bf16[640,384]{1,0:T(8,128)(2,1)S(1)} collective-permute-done((bf16[640,384]{1,0:T(8,128)(2,1)S(1)}, bf16[640,384]{1,0:T(8,128)(2,1)S(1)}, u32[]{:S(2)}, u32[]{:S(2)}) %collective-permute-start.17) | collective-permute-done | bytes 491552 | tf_op jit(solution)/shard_map/ppermute | solution.py:357
  89.3 2.5 %collective-permute-done.21 = bf16[640,384]{1,0:T(8,128)(2,1)S(1)} collective-permute-done((bf16[640,384]{1,0:T(8,128)(2,1)S(1)}, bf16[640,384]{1,0:T(8,128)(2,1)S(1)}, u32[]{:S(2)}, u32[]{:S(2)}) %collective-permute-start.21) | collective-permute-done | bytes 491552 | tf_op jit(solution)/shard_map/ppermute | solution.py:357
  92.7 3.8 %second_blocks.3 = (f32[640,384]{1,0:T(8,128)S(1)}, f32[640,384]{1,0:T(8,128)S(1)}, f32[640,384]{1,0:T(8,128)S(1)}) custom-call(s32[32]{0:T(128)S(1)} %pad_add_fusion.ints, bf16[640,1536]{1,0:T(8,128)(2,1)S(1)} %get-tuple-element.54.act_ref, bf16[1536,3072]{1,0:T(8,128)(2,1)S(1)} %bitcast.15), custom_call_target="tpu_custom_call" | custom-call | flops 566231040 | bytes 737280 | tf_op jit(solution)/shard_map/second_blocks/pallas_call | solution.py:523
  96.5 3.7 %collective-permute-done.18 = bf16[640,384]{1,0:T(8,128)(2,1)S(1)} collective-permute-done((bf16[640,384]{1,0:T(8,128)(2,1)S(1)}, bf16[640,384]{1,0:T(8,128)(2,1)S(1)}, u32[]{:S(2)}, u32[]{:S(2)}) %collective-permute-start.18) | collective-permute-done | bytes 491552 | tf_op jit(solution)/shard_map/ppermute | solution.py:357
  106.3 4.1 %collective-permute-done.19 = bf16[640,384]{1,0:T(8,128)(2,1)S(1)} collective-permute-done((bf16[640,384]{1,0:T(8,128)(2,1)}, bf16[640,384]{1,0:T(8,128)(2,1)S(1)}, u32[]{:S(2)}, u32[]{:S(2)}) %collective-permute-start.19) | collective-permute-done | bytes 491552 | tf_op jit(solution)/shard_map/ppermute | solution.py:357
  110.3 3.9 %collective-permute-done.23 = bf16[640,384]{1,0:T(8,128)(2,1)} collective-permute-done((bf16[640,384]{1,0:T(8,128)(2,1)}, bf16[640,384]{1,0:T(8,128)(2,1)}, u32[]{:S(2)}, u32[]{:S(2)}) %collective-permute-start.23) | collective-permute-done | bytes 491552 | tf_op jit(solution)/shard_map/ppermute | solution.py:357
  114.2 2.1 %add_convert_fusion = bf16[640,384]{1,0:T(8,128)(2,1)} fusion(f32[640,384]{1,0:T(8,128)S(1)} %fusion, bf16[640,384]{1,0:T(8,128)(2,1)} %collective-permute-done.23, f32[640,384]{1,0:T(8,128)S(1)} %get-tuple-element.55, bf16[640,384]{1,0:T(8,128)(2,1)S(1)} %collective-permute-done.19, bf16[640,384]{1,0:T(8,128)(2,1)S(1)} %copy-done.9, ...), kind=kLoop, calls=%fused_computation | loop fusion | flops 2211840 | bytes 3933696 | tf_op jit(solution)/shard_map/convert_element_type | solution.py:571
  (91 shorter events, 30.7 us)
Async XLA Ops:
  2.3 14.4 %collective-permute-start = (bf16[640,384]{1,0:T(8,128)(2,1)}, bf16[640,384]{1,0:T(8,128)(2,1)S(1)}, u32[]{:S(2)}, u32[]{:S(2)}) collective-permute-start(bf16[640,384]{1,0:T(8,128)(2,1)} %get-tuple-element.35.u_ref.refs_0_), channel_id=1, source_target_pairs={{0,4},{4,8},{8,12},{12,14},{14,10},{10,6},{6,2},{2,0},{1,5},{5,9},... | collective-permute-start | bytes 1474568 | tf_op jit(solution)/shard_map/ppermute | solution.py:357
  5.3 12.9 %collective-permute-start.1 = (bf16[640,384]{1,0:T(8,128)(2,1)}, bf16[640,384]{1,0:T(8,128)(2,1)S(1)}, u32[]{:S(2)}, u32[]{:S(2)}) collective-permute-start(bf16[640,384]{1,0:T(8,128)(2,1)} %get-tuple-element.35.u_ref.refs_0_), channel_id=1, source_target_pairs={{4,0},{8,4},{12,8},{14,12},{10,14},{6,10},{2,6},{0,2},{5,1},{9,5},... | collective-permute-start | bytes 1474568 | tf_op jit(solution)/shard_map/ppermute | solution.py:357
  9.6 2.1 %collective-permute-start.2 = (bf16[8,64,384]{2,1,0:T(8,128)(2,1)}, bf16[8,64,384]{2,1,0:T(8,128)(2,1)}, u32[]{:S(2)}, u32[]{:S(2)}) collective-permute-start(bf16[8,64,384]{2,1,0:T(8,128)(2,1)} %get-tuple-element.38), channel_id=1, source_target_pairs={{0,1},{1,0},{2,3},{3,2},{4,5},{5,4},{6,7},{7,6},{8,9},{9,8},{10,11... | collective-permute-start | bytes 1179656 | tf_op jit(solution)/shard_map/ppermute | solution.py:397
  9.7 47.8 %collective-permute-start.15 = (bf16[8,64,1536]{2,1,0:T(8,128)(2,1)}, bf16[8,64,1536]{2,1,0:T(8,128)(2,1)}, u32[]{:S(2)}, u32[]{:S(2)}) collective-permute-start(bf16[8,64,1536]{2,1,0:T(8,128)(2,1)} %get-tuple-element.53.after_ref), channel_id=1, source_target_pairs={{0,1},{1,0},{2,3},{3,2},{4,5},{5,4},{6,7},{7,6},{8,9},{9,8},{10,11... | collective-permute-start | bytes 4718600 | tf_op jit(solution)/shard_map/ppermute | solution.py:426
  18.2 17.9 %collective-permute-start.3 = (bf16[640,384]{1,0:T(8,128)(2,1)S(1)}, bf16[640,384]{1,0:T(8,128)(2,1)S(1)}, u32[]{:S(2)}, u32[]{:S(2)}) collective-permute-start(bf16[640,384]{1,0:T(8,128)(2,1)S(1)} %collective-permute-done.refs_1_), channel_id=1, source_target_pairs={{0,4},{4,8},{8,12},{12,14},{14,10},{10,6},{6,2},{2,0},{1,5},{5,9},... | collective-permute-start | bytes 1474568 | tf_op jit(solution)/shard_map/ppermute | solution.py:357
  19.8 16.4 %collective-permute-start.6 = (bf16[640,384]{1,0:T(8,128)(2,1)S(1)}, bf16[640,384]{1,0:T(8,128)(2,1)S(1)}, u32[]{:S(2)}, u32[]{:S(2)}) collective-permute-start(bf16[640,384]{1,0:T(8,128)(2,1)S(1)} %collective-permute-done.1.refs_2_), channel_id=1, source_target_pairs={{4,0},{8,4},{12,8},{14,12},{10,14},{6,10},{2,6},{0,2},{5,1},{9,5},... | collective-permute-start | bytes 1474568 | tf_op jit(solution)/shard_map/ppermute | solution.py:357
  20.9 11.7 %collective-permute-start.9 = (bf16[64,640]{1,0:T(8,128)(2,1)S(1)}, bf16[64,640]{1,0:T(8,128)(2,1)S(1)}, u32[]{:S(2)}, u32[]{:S(2)}) collective-permute-start(bf16[64,640]{1,0:T(8,128)(2,1)S(1)} %get-tuple-element.39.refs_0_), channel_id=1, source_target_pairs={{0,2},{2,0},{4,6},{6,4},{8,10},{10,8},{12,14},{14,12},{1,3},{3,1},... | collective-permute-start | bytes 245768 | tf_op jit(solution)/shard_map/ppermute | solution.py:357
  21.3 12.2 %collective-permute-start.10 = (f32[32,640]{1,0:T(8,128)S(1)}, f32[32,640]{1,0:T(8,128)S(1)}, u32[]{:S(2)}, u32[]{:S(2)}) collective-permute-start(f32[32,640]{1,0:T(8,128)S(1)} %get-tuple-element.42.refs_1_), channel_id=1, source_target_pairs={{0,2},{2,0},{4,6},{6,4},{8,10},{10,8},{12,14},{14,12},{1,3},{3,1},... | collective-permute-start | bytes 245768 | tf_op jit(solution)/shard_map/ppermute | solution.py:357
  34.0 10.7 %collective-permute-start.11 = (bf16[64,640]{1,0:T(8,128)(2,1)S(1)}, bf16[64,640]{1,0:T(8,128)(2,1)S(1)}, u32[]{:S(2)}, u32[]{:S(2)}) collective-permute-start(bf16[64,640]{1,0:T(8,128)(2,1)S(1)} %get-tuple-element.45.refs_0_), channel_id=1, source_target_pairs={{0,4},{2,6},{4,0},{6,2},{8,12},{10,14},{12,8},{14,10},{1,5},{3,7},... | collective-permute-start | bytes 245768 | tf_op jit(solution)/shard_map/ppermute | solution.py:357
  34.1 10.6 %collective-permute-start.12 = (f32[32,640]{1,0:T(8,128)S(1)}, f32[32,640]{1,0:T(8,128)S(1)}, u32[]{:S(2)}, u32[]{:S(2)}) collective-permute-start(f32[32,640]{1,0:T(8,128)S(1)} %get-tuple-element.46.refs_1_), channel_id=1, source_target_pairs={{0,4},{2,6},{4,0},{6,2},{8,12},{10,14},{12,8},{14,10},{1,5},{3,7},... | collective-permute-start | bytes 245768 | tf_op jit(solution)/shard_map/ppermute | solution.py:357
  36.1 18.0 %collective-permute-start.4 = (bf16[640,384]{1,0:T(8,128)(2,1)S(1)}, bf16[640,384]{1,0:T(8,128)(2,1)S(1)}, u32[]{:S(2)}, u32[]{:S(2)}) collective-permute-start(bf16[640,384]{1,0:T(8,128)(2,1)S(1)} %collective-permute-done.3.refs_3_), channel_id=1, source_target_pairs={{0,4},{4,8},{8,12},{12,14},{14,10},{10,6},{6,2},{2,0},{1,5},{5,9},... | collective-permute-start | bytes 1474568 | tf_op jit(solution)/shard_map/ppermute | solution.py:357
  36.2 19.6 %collective-permute-start.7 = (bf16[640,384]{1,0:T(8,128)(2,1)S(1)}, bf16[640,384]{1,0:T(8,128)(2,1)S(1)}, u32[]{:S(2)}, u32[]{:S(2)}) collective-permute-start(bf16[640,384]{1,0:T(8,128)(2,1)S(1)} %collective-permute-done.6.refs_4_), channel_id=1, source_target_pairs={{4,0},{8,4},{12,8},{14,12},{10,14},{6,10},{2,6},{0,2},{5,1},{9,5},... | collective-permute-start | bytes 1474568 | tf_op jit(solution)/shard_map/ppermute | solution.py:357
  45.2 11.1 %collective-permute-start.13 = (bf16[64,640]{1,0:T(8,128)(2,1)S(1)}, bf16[64,640]{1,0:T(8,128)(2,1)S(1)}, u32[]{:S(2)}, u32[]{:S(2)}) collective-permute-start(bf16[64,640]{1,0:T(8,128)(2,1)S(1)} %get-tuple-element.49.refs_0_), channel_id=1, source_target_pairs={{0,8},{2,10},{4,12},{6,14},{8,0},{10,2},{12,4},{14,6},{1,9},{3,11}... | collective-permute-start | bytes 245768 | tf_op jit(solution)/shard_map/ppermute | solution.py:357
  47.8 8.6 %collective-permute-start.14 = (f32[32,640]{1,0:T(8,128)S(1)}, f32[32,640]{1,0:T(8,128)S(1)}, u32[]{:S(2)}, u32[]{:S(2)}) collective-permute-start(f32[32,640]{1,0:T(8,128)S(1)} %get-tuple-element.50.refs_1_), channel_id=1, source_target_pairs={{0,8},{2,10},{4,12},{6,14},{8,0},{10,2},{12,4},{14,6},{1,9},{3,11}... | collective-permute-start | bytes 245768 | tf_op jit(solution)/shard_map/ppermute | solution.py:357
  54.2 8.1 %collective-permute-start.5 = (bf16[320,384]{1,0:T(8,128)(2,1)S(1)}, bf16[320,384]{1,0:T(8,128)(2,1)S(1)}, u32[]{:S(2)}, u32[]{:S(2)}) collective-permute-start(bf16[320,384]{1,0:T(8,128)(2,1)S(1)} %slice.43), channel_id=1, source_target_pairs={{0,4},{4,8},{8,12},{12,14},{14,10},{10,6},{6,2},{2,0},{1,5},{5,9},... | collective-permute-start | bytes 737288 | tf_op jit(solution)/shard_map/ppermute | solution.py:357
  55.8 6.5 %collective-permute-start.8 = (bf16[320,384]{1,0:T(8,128)(2,1)S(1)}, bf16[320,384]{1,0:T(8,128)(2,1)S(1)}, u32[]{:S(2)}, u32[]{:S(2)}) collective-permute-start(bf16[320,384]{1,0:T(8,128)(2,1)S(1)} %slice.44), channel_id=1, source_target_pairs={{4,0},{8,4},{12,8},{14,12},{10,14},{6,10},{2,6},{0,2},{5,1},{9,5},... | collective-permute-start | bytes 737288 | tf_op jit(solution)/shard_map/ppermute | solution.py:357
  66.0 9.1 %collective-permute-start.16 = (bf16[320,384]{1,0:T(8,128)(2,1)S(1)}, bf16[320,384]{1,0:T(8,128)(2,1)S(1)}, u32[]{:S(2)}, u32[]{:S(2)}) collective-permute-start(bf16[320,384]{1,0:T(8,128)(2,1)S(1)} %get-tuple-element.65), channel_id=1, source_target_pairs={{0,4},{4,8},{8,12},{12,14},{14,10},{10,6},{6,2},{2,0},{1,5},{5,9},... | collective-permute-start | bytes 737288 | tf_op jit(solution)/shard_map/ppermute | solution.py:357
  70.4 8.9 %collective-permute-start.20 = (bf16[320,384]{1,0:T(8,128)(2,1)S(1)}, bf16[320,384]{1,0:T(8,128)(2,1)S(1)}, u32[]{:S(2)}, u32[]{:S(2)}) collective-permute-start(bf16[320,384]{1,0:T(8,128)(2,1)S(1)} %get-tuple-element.66), channel_id=1, source_target_pairs={{4,0},{8,4},{12,8},{14,12},{10,14},{6,10},{2,6},{0,2},{5,1},{9,5},... | collective-permute-start | bytes 737288 | tf_op jit(solution)/shard_map/ppermute | solution.py:357
  75.2 12.6 %collective-permute-start.17 = (bf16[640,384]{1,0:T(8,128)(2,1)S(1)}, bf16[640,384]{1,0:T(8,128)(2,1)S(1)}, u32[]{:S(2)}, u32[]{:S(2)}) collective-permute-start(bf16[640,384]{1,0:T(8,128)(2,1)S(1)} %pad_maximum_fusion), channel_id=1, source_target_pairs={{0,4},{4,8},{8,12},{12,14},{14,10},{10,6},{6,2},{2,0},{1,5},{5,9},... | collective-permute-start | bytes 1474568 | tf_op jit(solution)/shard_map/ppermute | solution.py:357
  79.4 12.4 %collective-permute-start.21 = (bf16[640,384]{1,0:T(8,128)(2,1)S(1)}, bf16[640,384]{1,0:T(8,128)(2,1)S(1)}, u32[]{:S(2)}, u32[]{:S(2)}) collective-permute-start(bf16[640,384]{1,0:T(8,128)(2,1)S(1)} %pad_maximum_fusion.1), channel_id=1, source_target_pairs={{4,0},{8,4},{12,8},{14,12},{10,14},{6,10},{2,6},{0,2},{5,1},{9,5},... | collective-permute-start | bytes 1474568 | tf_op jit(solution)/shard_map/ppermute | solution.py:357
  87.8 12.4 %collective-permute-start.18 = (bf16[640,384]{1,0:T(8,128)(2,1)S(1)}, bf16[640,384]{1,0:T(8,128)(2,1)S(1)}, u32[]{:S(2)}, u32[]{:S(2)}) collective-permute-start(bf16[640,384]{1,0:T(8,128)(2,1)S(1)} %add_convert_fusion.4), channel_id=1, source_target_pairs={{0,4},{4,8},{8,12},{12,14},{14,10},{10,6},{6,2},{2,0},{1,5},{5,9},... | collective-permute-start | bytes 1474568 | tf_op jit(solution)/shard_map/ppermute | solution.py:357
  91.9 12.3 %collective-permute-start.22 = (bf16[640,384]{1,0:T(8,128)(2,1)S(1)}, bf16[640,384]{1,0:T(8,128)(2,1)S(1)}, u32[]{:S(2)}, u32[]{:S(2)}) collective-permute-start(bf16[640,384]{1,0:T(8,128)(2,1)S(1)} %add_convert_fusion.2), channel_id=1, source_target_pairs={{4,0},{8,4},{12,8},{14,12},{10,14},{6,10},{2,6},{0,2},{5,1},{9,5},... | collective-permute-start | bytes 1474568 | tf_op jit(solution)/shard_map/ppermute | solution.py:357
  101.1 9.2 %collective-permute-start.19 = (bf16[640,384]{1,0:T(8,128)(2,1)}, bf16[640,384]{1,0:T(8,128)(2,1)S(1)}, u32[]{:S(2)}, u32[]{:S(2)}) collective-permute-start(bf16[640,384]{1,0:T(8,128)(2,1)} %add_convert_fusion.3), channel_id=1, source_target_pairs={{0,4},{4,8},{8,12},{12,14},{14,10},{10,6},{6,2},{2,0},{1,5},{5,9},... | collective-permute-start | bytes 1474568 | tf_op jit(solution)/shard_map/ppermute | solution.py:357
  105.1 9.1 %collective-permute-start.23 = (bf16[640,384]{1,0:T(8,128)(2,1)}, bf16[640,384]{1,0:T(8,128)(2,1)}, u32[]{:S(2)}, u32[]{:S(2)}) collective-permute-start(bf16[640,384]{1,0:T(8,128)(2,1)} %add_convert_fusion.1), channel_id=1, source_target_pairs={{4,0},{8,4},{12,8},{14,12},{10,14},{6,10},{2,6},{0,2},{5,1},{9,5},... | collective-permute-start | bytes 1474568 | tf_op jit(solution)/shard_map/ppermute | solution.py:357
  (15 other events, 146.2 us)
